TPU v7x, 512 devices: a whole 4x4x16 slice. The times are simulated.
512 devices in a mesh: rep: 16 (over z_hi, x, core), fsdp: 32 (over z_lo, y).
Axes of the slice: x: 4, y: 4, z: 16 (z_hi: 2, z_lo: 8; z = z_hi * 8 + z_lo), core: 2. Of those that a mesh axis runs over, the one named last changes fastest.
Arguments:
- hidden_in: bfloat16 [65536, 8192], P(('rep', 'fsdp')), may hold values from -6 to 6
- gain: float32 [8192], replicated, may hold values from 0.5 to 1.5
- key_grad: bfloat16 [65536, 512], P(('rep', 'fsdp')), may hold values from -6 to 6
- weights: float32 [16, 8192, 512], P('rep', 'fsdp'), may hold values from -6 to 6
- first_moment: float32 [16, 8192, 512], P('rep', 'fsdp'), may hold values from -1 to 1
- second_moment: bfloat16 [16, 8192, 512], P('rep', 'fsdp'), may hold values from 0.0099487305 to 0.099609375
- anchor: float32 [8192, 256], P('fsdp'), may hold values from -6 to 6
- momentum: float32 [8192, 256], P('fsdp'), may hold values from -4 to 4
- fragment: int32 [1], replicated, may hold values from 0 to 1
Outputs:
- keys: bfloat16 [65536, 512], P(('rep', 'fsdp'))
- weights_out: float32 [16, 8192, 512], P('rep', 'fsdp')
- momentum_out: float32 [8192, 256], P('fsdp')
All inputs are finite; a program needn't handle non-finite values.
Results may differ from a plain program's by a relative error of at most 0.012.
Values may be sent and summed in bfloat16 or wider, within the bound.
No kernel may reach another device: no remote copies, remote signals or barrier semaphores. Data moves between devices by JAX's collectives and lax.ppermute only.
A program may use at most 64 MiB of HBM per device.

v0:
```python
import jax
import jax.numpy as jnp
from jax import lax
from jax.sharding import PartitionSpec as P

NORM_EPS = 1e-05
ADAM_EPS = 1e-08
INNER_RATE = 0.6


def outer_step(mean_cols, anchor_part, momentum_part):
    delta = anchor_part - mean_cols
    momentum_next = 0.9 * momentum_part + delta
    return (anchor_part - 0.7 * (delta + 0.9 * momentum_next), momentum_next)


def on_device(
    hidden_in, gain, key_grad, weights, first_moment, second_moment, anchor, momentum, fragment
):
    token_rows = hidden_in.shape[0]
    features = hidden_in.shape[1]
    multiplier = float(features) ** (-0.5)
    tokens_f = hidden_in.astype(jnp.float32)
    factor = lax.rsqrt(jnp.mean(tokens_f * tokens_f, axis=1, keepdims=True) + NORM_EPS)
    normed = (tokens_f * factor * gain).astype(jnp.bfloat16)
    weight_now = weights[0]
    weight_low = weight_now.astype(jnp.bfloat16)
    local_rows = weight_now.shape[0]
    key_width = weight_now.shape[1]
    columns = lax.all_to_all(normed, "fsdp", split_axis=1, concat_axis=0, tiled=True)
    gathered = lax.all_gather(weight_low, "fsdp", axis=0, tiled=True)
    groups = lax.axis_size("fsdp")
    blocks = gathered.reshape(groups, local_rows, key_width)
    split_tokens = normed.reshape(token_rows, groups, local_rows)
    partial_keys = (
        jnp.einsum("tgd,gdk->gtk", split_tokens, blocks, preferred_element_type=jnp.float32)
        * multiplier
    )
    rounded = lax.optimization_barrier(partial_keys.astype(jnp.bfloat16))
    keys = jnp.sum(rounded.astype(jnp.float32), axis=0).astype(jnp.bfloat16)
    grad_sum = lax.dot_general(
        columns,
        lax.all_gather(key_grad, "fsdp", axis=0, tiled=True),
        (((0,), (0,)), ((), ())),
        preferred_element_type=jnp.float32,
    )
    gradient = grad_sum * multiplier
    moment_next = 0.9 * first_moment[0] + 0.1 * gradient
    second_next = 0.95 * second_moment[0].astype(jnp.float32) + 0.05 * gradient * gradient
    inner = weight_now - INNER_RATE * (
        moment_next / (jnp.sqrt(second_next) + ADAM_EPS) + 0.1 * weight_now
    )
    frag_width = anchor.shape[1]
    col_offset = fragment[0] * frag_width
    start_cols = lax.dynamic_slice_in_dim(weight_now, col_offset, frag_width, 1)
    replicas = lax.axis_size("rep")
    summed_cols = lax.psum(start_cols.astype(jnp.bfloat16), "rep").astype(jnp.float32)
    fresh, momentum_out = outer_step(summed_cols / replicas, anchor, momentum)
    current = lax.dynamic_slice_in_dim(inner, col_offset, frag_width, 1)
    merged = 0.5 * current + 0.5 * fresh
    weights_out = lax.dynamic_update_slice_in_dim(inner, merged, col_offset, 1)
    return (keys, weights_out[None], momentum_out)


def solution(mesh):
    return jax.shard_map(
        on_device,
        mesh=mesh,
        in_specs=(
            P(("rep", "fsdp"), None),
            P(),
            P(("rep", "fsdp"), None),
            P("rep", "fsdp", None),
            P("rep", "fsdp", None),
            P("rep", "fsdp", None),
            P("fsdp", None),
            P("fsdp", None),
            P(),
        ),
        out_specs=(P(("rep", "fsdp"), None), P("rep", "fsdp", None), P("fsdp", None)),
        check_vma=False,
    )
```

profile of v0, /device:TPU:14, one launch (start us, length us, event | category | flops | bytes accessed | tf_op | source)
XLA Modules:
  0.0 503.3 jit_solution(1126153812130512168)
XLA Ops:
  8.0 0.0 copy-start.4
  8.0 0.0 all-gather.5.cloned.1.call-start
  8.1 0.7 all-gather.5.cloned.1.call-update
  8.7 0.0 all-reduce.2.cloned.1.call-start
  9.4 1.6 fusion.9
  11.1 0.0 all-reduce.2.cloned.1.call-update
  11.1 0.0 all-gather.3.cloned.1.call-start
  11.1 1.8 bitcast_convert_fusion
  12.9 0.0 all-gather.3.cloned.1.call-update
  12.9 3.2 copy.13
  16.2 0.0 copy-start
  16.2 1.1 fusion
  17.3 0.2 copy-done
  17.5 0.0 copy-done.4
  17.5 4.6 fusion.2
  22.1 0.0 copy-start.1
  22.1 128.5 %all_to_all.16 = bf16[128,32,256]{0,2,1:T(8,128)(2,1)} all-to-all(bf16[128,32,256]{0,2,1:T(8,128)(2,1)S(1)} %bitcast.38), channel_id=1, replica_groups=mesh['rep'=16,'fsdp'=32] {'fsdp'}, dimensions={1} | all-to-all | bytes 4194304 | tf_op jit(solution)/shard_map/all_to_all | solution.py:30
  150.6 4.1 copy.15
  154.7 92.3 %all-gather.5.cloned.1.call-done = bf16[4096,512]{1,0:T(8,128)(2,1)} async-done(((bf16[128,512]{1,0:T(8,128)(2,1)}), bf16[4096,512]{1,0:T(8,128)(2,1)}) %all-gather.5.cloned.1.call-update) | async-done | bytes 4194320 | tf_op jit(solution)/shard_map/all_gather | solution.py:43
  247.0 0.0 copy-done.1
  247.0 0.0 copy-start.3
  247.0 4.6 fusion.8
  251.7 61.2 %all-reduce.2.cloned.1.call-done = bf16[256,256]{1,0:T(8,128)(2,1)} async-done(((bf16[256,256]{1,0:T(8,128)(2,1)}), bf16[256,256]{1,0:T(8,128)(2,1)}) %all-reduce.2.cloned.1.call-update) | async-done | bytes 131088 | tf_op jit(solution)/shard_map/psum | solution.py:57
  312.9 0.0 copy-done.3
  312.9 1.8 bitcast_dynamic-update-slice_fusion
  314.7 0.0 copy-start.2
  314.7 170.7 %all-gather.3.cloned.1.call-done = bf16[8192,512]{1,0:T(8,128)(2,1)} async-done(((bf16[256,512]{1,0:T(8,128)(2,1)}), bf16[8192,512]{1,0:T(8,128)(2,1)}) %all-gather.3.cloned.1.call-update) | async-done | bytes 8388624 | tf_op jit(solution)/shard_map/all_gather | solution.py:31
  485.4 6.9 %multiply_convert_fusion = bf16[32,128,512]{2,1,0:T(8,128)(2,1)} fusion(bf16[128,32,256]{0,2,1:T(8,128)(2,1)S(1)} %bitcast.39, bf16[32,256,512]{2,1,0:T(8,128)(2,1)} %bitcast.40), kind=kOutput, calls=%fused_computation | convolution fusion | flops 1077936128 | bytes 14680064 | tf_op jit(solution)/shard_map/tgd,gdk->gtk/dot_general | solution.py:36
  492.4 0.0 copy-done.2
  492.4 3.5 reduce_sum.22
  (2 shorter events, 0.0 us)
Async XLA Ops:
  8.0 9.5 %copy-start.4 = (f32[8192]{0:T(1024)S(1)}, f32[8192]{0:T(1024)}, u32[]{:S(2)}) copy-start(f32[8192]{0:T(1024)} %param.10) | copy-start | bytes 98308
  8.0 239.0 %all-gather.5.cloned.1.call-start = ((), (), s32[]{:S(2)}) async-start(), calls=%async_computation.2 | async-start | bytes 4325376 | tf_op jit(solution)/shard_map/all_gather | solution.py:43
  8.7 304.2 %all-reduce.2.cloned.1.call-start = ((), (), s32[]{:S(2)}) async-start(), calls=%async_computation.3 | async-start | bytes 262144 | tf_op jit(solution)/shard_map/psum | solution.py:57
  11.1 474.3 %all-gather.3.cloned.1.call-start = ((), (), s32[]{:S(2)}) async-start(), calls=%async_computation.1 | async-start | bytes 8650752 | tf_op jit(solution)/shard_map/all_gather | solution.py:31
  16.2 1.3 copy-start
  22.1 224.9 %copy-start.1 = (f32[1,256,512]{2,1,0:T(8,128)S(1)}, f32[1,256,512]{2,1,0:T(8,128)}, u32[]{:S(2)}) copy-start(f32[1,256,512]{2,1,0:T(8,128)} %param.12) | copy-start | bytes 1572868
  247.0 65.9 %copy-start.3 = (f32[256,256]{1,0:T(8,128)S(1)}, f32[256,256]{1,0:T(8,128)}, u32[]{:S(2)}) copy-start(f32[256,256]{1,0:T(8,128)} %param.15) | copy-start | bytes 786436
  314.7 177.6 %copy-start.2 = (f32[1,256,512]{2,1,0:T(8,128)}, f32[1,256,512]{2,1,0:T(8,128)S(1)}, u32[]{:S(2)}) copy-start(f32[1,256,512]{2,1,0:T(8,128)S(1)} %get-tuple-element.3) | copy-start | bytes 1572868
Sparse Core Ops, SparseCore 0:
  10.9 236.0 all-gather.4
  249.1 236.2 all-gather.2
Sparse Core Ops, SparseCore 1:
  12.7 300.2 all-reduce.1
where the time goes:
time: 504 us; the launch traced here: 503 us
  waiting for transfers between devices  325 us (64%)
  blocking collectives  129 us (26%)
  between operations  16.2 us (3%)
  other arithmetic  12.8 us (3%)
  matrix products  11.5 us (2%)
  local copies, waits for them, and re-layouts  9.19 us (2%)
    all_gather x1, waiting for transfers between devices, on_device(): gathered = lax.all_gather(weight_low, 'fsdp', axis=0, tiled=True)  171 us
    all_to_all x1, blocking collectives, on_device(): lax.all_to_all(normed, 'fsdp', split_axis=1, concat_axis=0, tiled=True)  129 us
    all_gather x1, waiting for transfers between devices, on_device(): lax.all_gather(key_grad, 'fsdp', axis=0, tiled=True)  92.3 us
    psum x1, waiting for transfers between devices, on_device(): lax.psum(start_cols.astype(jnp.bfloat16), 'rep').astype(jnp.float32)  61.2 us
  transfers between devices with their start and end apart: 3, of which 3 were waited for; matrix products, arithmetic and copies ran while one was open for 5% of the time, Pallas kernels for 0%

commit v1 on v0

v1 whole, which is shorter than its diff:
```python
import jax
import jax.numpy as jnp
from jax import lax
from jax.experimental import pallas as pl
from jax.experimental.pallas import tpu as pltpu
from jax.sharding import Mesh, PartitionSpec as P

NORM_EPS = 1e-05
ADAM_EPS = 1e-08
INNER_RATE = 0.6

REP = ("zh", "x", "c")
FSDP = ("zq", "zp", "y")
NEAR = ("zp", "y")
VMEM = pl.BlockSpec(memory_space=pltpu.VMEM)
SMEM = pl.BlockSpec(memory_space=pltpu.SMEM)
PARAMS = pltpu.CompilerParams(vmem_limit_bytes=32 * 1024 * 1024)


def outer_step(mean_cols, anchor_part, momentum_part):
    delta = anchor_part - mean_cols
    momentum_next = 0.9 * momentum_part + delta
    return (anchor_part - 0.7 * (delta + 0.9 * momentum_next), momentum_next)


def swap(value, bit):
    return lax.ppermute(value, "zq", [(i, i ^ bit) for i in range(4)])


def flip(value, axis, bit=1):
    return lax.ppermute(value, axis, [(i, i ^ bit) for i in range(lax.axis_size(axis))])


def add(a, b):
    return (a.astype(jnp.float32) + b.astype(jnp.float32)).astype(jnp.bfloat16)


def after(value, *others):
    return lax.optimization_barrier((value, *others))[0]


def exchange(value, axes):
    return lax.all_to_all(value, axes, split_axis=0, concat_axis=0, tiled=True)


def kernel_call(body, outs, args, flops=0, scalars=0, scratch=()):
    moved = sum(a.size * a.dtype.itemsize for a in (*args, *outs))
    return pl.pallas_call(
        body,
        out_shape=outs,
        in_specs=[SMEM] * scalars + [VMEM] * (len(args) - scalars),
        out_specs=[VMEM] * len(outs),
        scratch_shapes=list(scratch),
        compiler_params=PARAMS,
        cost_estimate=pl.CostEstimate(flops=flops, bytes_accessed=moved, transcendentals=0),
    )(*args)


def pack_tiles(far, near, rows, hidden_ref, tiles_ref):
    for a in range(near):
        for q in range(far):
            tiles_ref[a, :, q * rows : (q + 1) * rows] = hidden_ref[:, (q * near + a) * rows : (q * near + a + 1) * rows]


def scale_tokens(hidden_ref, grad_ref, factor_ref, scaled_ref):
    tokens, features = hidden_ref.shape
    wide = 512
    total = jnp.zeros((tokens, wide), jnp.float32)
    for i in range(features // wide):
        part = hidden_ref[:, i * wide : (i + 1) * wide].astype(jnp.float32)
        total = total + part * part
    mean = jnp.sum(total, axis=1, keepdims=True) / features
    factor = lax.rsqrt(mean + NORM_EPS)
    factor_ref[...] = factor
    scaled_ref[...] = (grad_ref[...].astype(jnp.float32) * factor).astype(jnp.bfloat16)


def block_of(place_ref, dh, dl, rows):
    block = (place_ref[0] ^ dh) * 2 + (place_ref[1] ^ dl)
    return pl.ds(pl.multiple_of(block * rows, rows), rows)


def gradient_blocks(rows, tokens, place_ref, tiles_ref, g0, g1, g2, g3, keep_a, keep_b, send_a, send_b, grad_ref):
    half = grad_ref.shape[1] // 2
    for turn, piece in enumerate((g0, g1, g2, g3)):
        for j in range(2):
            source = (place_ref[2] ^ j) * 4 + ((place_ref[3] + 4 - turn) & 3)
            where = pl.ds(pl.multiple_of(source * tokens, tokens), tokens)
            grad_ref[where, :] = piece[j * tokens : (j + 1) * tokens, :]
    for dh in range(2):
        for dl in range(2):
            left = tiles_ref[:, block_of(place_ref, dh, dl, rows)]
            value = lax.dot_general(left, grad_ref[...], (((0,), (0,)), ((), ())), preferred_element_type=jnp.float32)
            if dl:
                send_a[dh] = value[:, :half].astype(jnp.bfloat16)
            else:
                keep_a[dh] = value[:, :half]
            if dh:
                send_b[dl] = value[:, half:].astype(jnp.bfloat16)
            else:
                keep_b[dl] = value[:, half:]


def key_partials(rows, multiplier, place_ref, tiles_ref, pair_ref, other_ref, out_ref):
    total = None
    for dh in range(2):
        for dl in range(2):
            left = tiles_ref[:, block_of(place_ref, dh, dl, rows)]
            right = (other_ref if dl else pair_ref)[dh]
            value = jnp.dot(left, right, preferred_element_type=jnp.float32)
            total = value if total is None else total + value
    out_ref[...] = (total * multiplier).astype(jnp.bfloat16)


def on_device(
    hidden_in, gain, key_grad, weights, first_moment, second_moment, anchor, momentum, fragment
):
    tokens, features = hidden_in.shape
    key_width = key_grad.shape[1]
    half = key_width // 2
    multiplier = float(features) ** (-0.5)
    weight_now = weights[0]
    rows = weight_now.shape[0]
    near = lax.axis_size(NEAR)
    far = lax.axis_size("zq")
    far_index = lax.axis_index("zq")
    place = jnp.stack([far_index >> 1, far_index & 1, lax.axis_index("zp"), lax.axis_index("y")]).astype(jnp.int32)
    shape = jax.ShapeDtypeStruct
    f32, b16 = jnp.float32, jnp.bfloat16

    (tiles,) = kernel_call(
        lambda *refs: pack_tiles(far, near, rows, *refs), [shape((near, tokens, far * rows), b16)], (hidden_in,)
    )
    tiles = exchange(tiles, NEAR).reshape(near * tokens, far * rows)

    own_gain = lax.dynamic_slice_in_dim(gain, lax.axis_index(FSDP) * rows, rows, 0)[:, None]
    weight_low = (weight_now * own_gain).astype(b16)
    pair = jnp.stack([weight_low, swap(weight_low, 2)])
    other_pair = swap(pair, 1)

    factor, scaled_grad = kernel_call(
        scale_tokens, [shape((tokens, 1), f32), shape((tokens, key_width), b16)], (hidden_in, key_grad)
    )
    both_grad = jnp.concatenate([scaled_grad, flip(scaled_grad, "zp")])
    turned = [lax.ppermute(both_grad, "y", [(i, (i + k) % 4) for i in range(4)]) for k in (1, 3, 2)]
    grads = (both_grad, turned[0], turned[2], turned[1])

    frag_width = anchor.shape[1]
    col_offset = fragment[0] * frag_width
    start_cols = lax.dynamic_slice_in_dim(weight_now, col_offset, frag_width, 1).astype(b16)
    core = lax.axis_index("c")
    mine = lax.dynamic_slice_in_dim(start_cols, core * (rows // 2), rows // 2, 0)
    theirs = lax.dynamic_slice_in_dim(start_cols, (1 - core) * (rows // 2), rows // 2, 0)
    part = add(mine, flip(theirs, "c"))

    flops = 2 * near * tokens * far * rows * key_width
    block = (2, rows, half)
    keep_a, keep_b, send_a, send_b = kernel_call(
        lambda *refs: gradient_blocks(rows, tokens, *refs),
        [shape(block, f32), shape(block, f32), shape(block, b16), shape(block, b16)],
        (place, after(tiles, pair, part, *grads), *grads),
        flops,
        1,
        [pltpu.VMEM((near * tokens, key_width), b16)],
    )
    sum_a = keep_a + swap(send_a, 1).astype(f32)
    sum_b = keep_b + swap(send_b, 2).astype(f32)
    part = add(part, flip(part, "x", 1))
    part = add(part, flip(part, "x", 2))

    (partial_keys,) = kernel_call(
        lambda *refs: key_partials(rows, multiplier, *refs),
        [shape((near * tokens, key_width), b16)],
        (place, tiles, pair, other_pair),
        flops,
        1,
    )
    rest_a, rest_b = sum_a[1].astype(b16), sum_b[1].astype(b16)
    rest_a, rest_b, partial_keys, part = lax.optimization_barrier((rest_a, rest_b, partial_keys, part))
    grad_a = sum_a[0] + swap(rest_a, 2).astype(f32)
    grad_b = sum_b[0] + swap(rest_b, 1).astype(f32)
    grad_sum = jnp.concatenate([grad_a, grad_b], axis=1)
    rounded = exchange(partial_keys.reshape(near, tokens, key_width), NEAR)
    keys = (jnp.sum(rounded.astype(f32), axis=0) * factor).astype(b16)

    gradient = grad_sum * (multiplier * own_gain)
    moment_next = 0.9 * first_moment[0] + 0.1 * gradient
    second_next = 0.95 * second_moment[0].astype(f32) + 0.05 * gradient * gradient
    inner = weight_now - INNER_RATE * (
        moment_next / (jnp.sqrt(second_next) + ADAM_EPS) + 0.1 * weight_now
    )
    part = add(part, flip(part, "zh"))
    other = flip(part, "c")
    summed_cols = jnp.where(core == 0, jnp.concatenate([part, other]), jnp.concatenate([other, part])).astype(f32)
    replicas = lax.axis_size(REP)
    fresh, momentum_out = outer_step(summed_cols / replicas, anchor, momentum)
    current = lax.dynamic_slice_in_dim(inner, col_offset, frag_width, 1)
    merged = 0.5 * current + 0.5 * fresh
    weights_out = lax.dynamic_update_slice_in_dim(inner, merged, col_offset, 1)
    return (keys, weights_out[None], momentum_out)


def solution(mesh):
    fine = Mesh(mesh.devices.reshape(2, 4, 2, 4, 2, 4), REP + FSDP)
    both = REP + FSDP
    return jax.shard_map(
        on_device,
        mesh=fine,
        in_specs=(
            P(both, None),
            P(),
            P(both, None),
            P(REP, FSDP, None),
            P(REP, FSDP, None),
            P(REP, FSDP, None),
            P(FSDP, None),
            P(FSDP, None),
            P(),
        ),
        out_specs=(P(both, None), P(REP, FSDP, None), P(FSDP, None)),
        check_vma=False,
    )
```

time: 504 us -> 166 us (0.33)
  the two profiles are of different devices: /device:TPU:14 before, /device:TPU:1 now
where the time goes in v1:
time: 166 us; the launch traced here: 163 us
  starting transfers between devices  107 us (64%)
  waiting for transfers between devices  35.7 us (22%)
  Pallas kernels  7.5 us (5%)
  other arithmetic  5.69 us (3%)
  local copies, waits for them, and re-layouts  4.59 us (3%)
  between operations  1.71 us (1%)
    ppermute x6, starting transfers between devices, swap(): return lax.ppermute(value, 'zq', [(i, i ^ bit) for i in range(4)])  44.9 us
    ppermute x6, starting transfers between devices, flip(): lax.ppermute(value, axis, [(i, i ^ bit) for i in range(lax.axis_size(axis...  41.5 us
    ppermute x6, waiting for transfers between devices, swap(): return lax.ppermute(value, 'zq', [(i, i ^ bit) for i in range(4)])  20 us
    ppermute x6, waiting for transfers between devices, flip(): lax.ppermute(value, axis, [(i, i ^ bit) for i in range(lax.axis_size(axis...  15.7 us
    all_to_all x2, starting transfers between devices, exchange(): return lax.all_to_all(value, axes, split_axis=0, concat_axis=0, tiled=True)  10.5 us
    ppermute x3, starting transfers between devices, on_device(): lax.ppermute(both_grad, 'y', [(i, (i + k) % 4) for i in range(4)])  10.5 us
    pallas_call x4, Pallas kernels, kernel_call(): pl.pallas_call(body, out_shape=outs, in_specs=[SMEM] * scalars + [VMEM] *...  7.5 us
  transfers between devices with their start and end apart: 17, of which 5 were waited for; matrix products, arithmetic and copies ran while one was open for 3% of the time, Pallas kernels for 4%

profile of v1, /device:TPU:1, one launch (start us, length us, event | category | flops | bytes accessed | tf_op | source)
XLA Modules:
  0.0 162.7 jit_solution(579111598205450627)
XLA Ops:
  0.6 0.0 copy-start
  0.6 1.6 copy-done
  2.2 0.3 shard_map.112
  2.5 0.0 copy-start.2
  2.5 1.3 copy-done.2
  3.8 6.6 %all-to-all-start = ((bf16[8,128,1024]{2,1,0:T(8,128)(2,1)}), bf16[8,128,1024]{2,1,0:T(8,128)(2,1)}, u32[]{:S(2)}, u32[]{:S(2)}) async-start(bf16[8,128,1024]{2,1,0:T(8,128)(2,1)} %copy-done.2), calls=%async_computation | async-start | bytes 4194304 | tf_op jit(solution)/shard_map/all_to_all | solution.py:43
  10.4 0.8 broadcast_multiply_fusion
  11.2 0.1 multiply_convert_fusion
  11.3 8.8 %collective-permute-start = (bf16[256,512]{1,0:T(8,128)(2,1)S(1)}, bf16[256,512]{1,0:T(8,128)(2,1)}, u32[]{:S(2)}, u32[]{:S(2)}) collective-permute-start(bf16[256,512]{1,0:T(8,128)(2,1)S(1)} %multiply_convert_fusion), channel_id=1, source_target_pairs={{0,16},{8,24},{16,0},{24,8},{1,17},{9,25},{17,1},{25,9},{2,18},{10... | collective-permute-start | bytes 786440 | tf_op jit(solution)/shard_map/ppermute | solution.py:27
  20.9 3.1 %collective-permute-start.1 = (bf16[128,256]{1,0:T(8,128)(2,1)S(1)}, bf16[128,256]{1,0:T(8,128)(2,1)S(1)}, u32[]{:S(2)}, u32[]{:S(2)}) collective-permute-start(bf16[128,256]{1,0:T(8,128)(2,1)S(1)} %dynamic-slice_bitcast_fusion), channel_id=1, source_target_pairs={{0,32},{32,0},{1,33},{33,1},{2,34},{34,2},{3,35},{35,3},{4,36},{36... | collective-permute-start | bytes 196616 | tf_op jit(solution)/shard_map/ppermute | solution.py:31
  24.0 0.5 shard_map.113
  24.5 3.7 %collective-permute-start.2 = (bf16[128,512]{1,0:T(8,128)(2,1)S(1)}, bf16[128,512]{1,0:T(8,128)(2,1)S(1)}, u32[]{:S(2)}, u32[]{:S(2)}) collective-permute-start(bf16[128,512]{1,0:T(8,128)(2,1)S(1)} %get-tuple-element.14), channel_id=1, source_target_pairs={{0,4},{4,0},{1,5},{5,1},{2,6},{6,2},{3,7},{7,3},{8,12},{12,8},{9,1... | collective-permute-start | bytes 393224 | tf_op jit(solution)/shard_map/ppermute | solution.py:31
  28.2 0.1 multiply_convert_fusion.1
  28.3 0.1 pad_add_fusion.refs_0_
  28.3 0.0 collective-permute-done.1
  28.4 3.1 %collective-permute-start.9 = (bf16[128,256]{1,0:T(8,128)(2,1)S(1)}, bf16[128,256]{1,0:T(8,128)(2,1)S(1)}, u32[]{:S(2)}, u32[]{:S(2)}) collective-permute-start(bf16[128,256]{1,0:T(8,128)(2,1)S(1)} %fusion.19), channel_id=1, source_target_pairs={{0,64},{64,0},{128,192},{192,128},{1,65},{65,1},{129,193},{193,129... | collective-permute-start | bytes 196616 | tf_op jit(solution)/shard_map/ppermute | solution.py:31
  31.5 7.7 %collective-permute-done.2 = bf16[128,512]{1,0:T(8,128)(2,1)S(1)} collective-permute-done((bf16[128,512]{1,0:T(8,128)(2,1)S(1)}, bf16[128,512]{1,0:T(8,128)(2,1)S(1)}, u32[]{:S(2)}, u32[]{:S(2)}) %collective-permute-start.2) | collective-permute-done | bytes 131104 | tf_op jit(solution)/shard_map/ppermute | solution.py:31
  39.3 3.0 %collective-permute-start.3 = (bf16[256,512]{1,0:T(8,128)(2,1)S(1)}, bf16[256,512]{1,0:T(8,128)(2,1)S(1)}, u32[]{:S(2)}, u32[]{:S(2)}) collective-permute-start(bf16[256,512]{1,0:T(8,128)(2,1)S(1)} %constant_dynamic-update-slice_fusion.refs_2_), channel_id=1, source_target_pairs={{0,1},{1,2},{2,3},{3,0},{4,5},{5,6},{6,7},{7,4},{8,9},{9,10},{10,1... | collective-permute-start | bytes 786440 | tf_op jit(solution)/shard_map/ppermute | solution.py:145
  42.3 4.4 %collective-permute-start.4 = (bf16[256,512]{1,0:T(8,128)(2,1)S(1)}, bf16[256,512]{1,0:T(8,128)(2,1)S(1)}, u32[]{:S(2)}, u32[]{:S(2)}) collective-permute-start(bf16[256,512]{1,0:T(8,128)(2,1)S(1)} %constant_dynamic-update-slice_fusion.refs_2_), channel_id=1, source_target_pairs={{0,2},{1,3},{2,0},{3,1},{4,6},{5,7},{6,4},{7,5},{8,10},{9,11},{10,... | collective-permute-start | bytes 786440 | tf_op jit(solution)/shard_map/ppermute | solution.py:145
  46.7 3.1 %collective-permute-start.5 = (bf16[256,512]{1,0:T(8,128)(2,1)S(1)}, bf16[256,512]{1,0:T(8,128)(2,1)S(1)}, u32[]{:S(2)}, u32[]{:S(2)}) collective-permute-start(bf16[256,512]{1,0:T(8,128)(2,1)S(1)} %constant_dynamic-update-slice_fusion.refs_2_), channel_id=1, source_target_pairs={{0,3},{1,0},{2,1},{3,2},{4,7},{5,4},{6,5},{7,6},{8,11},{9,8},{10,9... | collective-permute-start | bytes 786440 | tf_op jit(solution)/shard_map/ppermute | solution.py:145
  49.8 0.0 collective-permute-done
  49.8 1.0 pad_maximum_fusion.refs_2_
  50.8 17.8 %collective-permute-start.8 = (bf16[2,256,512]{2,1,0:T(8,128)(2,1)S(1)}, bf16[2,256,512]{2,1,0:T(8,128)(2,1)S(1)}, u32[]{:S(2)}, u32[]{:S(2)}) collective-permute-start(bf16[2,256,512]{2,1,0:T(8,128)(2,1)S(1)} %pad_maximum_fusion.refs_2_), channel_id=1, source_target_pairs={{0,8},{8,0},{16,24},{24,16},{1,9},{9,1},{17,25},{25,17},{2,10},{10... | collective-permute-start | bytes 1572872 | tf_op jit(solution)/shard_map/ppermute | solution.py:27
  68.6 0.0 collective-permute-done.9
  68.7 4.7 %collective-permute-start.10 = (bf16[128,256]{1,0:T(8,128)(2,1)S(1)}, bf16[128,256]{1,0:T(8,128)(2,1)S(1)}, u32[]{:S(2)}, u32[]{:S(2)}) collective-permute-start(bf16[128,256]{1,0:T(8,128)(2,1)S(1)} %add_convert_fusion.2), channel_id=1, source_target_pairs={{0,128},{64,192},{128,0},{192,64},{1,129},{65,193},{129,1},{193,65... | collective-permute-start | bytes 196616 | tf_op jit(solution)/shard_map/ppermute | solution.py:31
  73.3 0.0 collective-permute-done.3.refs_3_
  73.3 0.0 collective-permute-done.4.refs_4_
  73.3 0.0 collective-permute-done.5.refs_5_
  73.4 0.0 all-to-all-done
  73.4 3.0 %shard_map.114 = (f32[2,256,256]{2,1,0:T(8,128)S(1)}, f32[2,256,256]{2,1,0:T(8,128)S(1)}, bf16[2,256,256]{2,1,0:T(8,128)(2,1)S(1)}, bf16[2,256,256]{2,1,0:T(8,128)(2,1)S(1)}) custom-call(s32[4]{0:T(128)S(1)} %pad_add_fusion.refs_0_, bf16[1024,1024]{1,0:T(8,128)(2,1)} %bitcast.4.refs_1_, bf16[256,512]{1,0:T(8,128)(2,1)S(1)} %constant_dynamic-update-slice_fusion.refs_2_, ...), custom_call_target="tpu_custom_call" | custom-call | flops 1073741824 | bytes 4718608 | tf_op jit(solution)/shard_map/pallas_call | solution.py:48
  76.3 1.9 %collective-permute-start.6 = (bf16[2,256,256]{2,1,0:T(8,128)(2,1)S(1)}, bf16[2,256,256]{2,1,0:T(8,128)(2,1)S(1)}, u32[]{:S(2)}, u32[]{:S(2)}) collective-permute-start(bf16[2,256,256]{2,1,0:T(8,128)(2,1)S(1)} %get-tuple-element.17), channel_id=1, source_target_pairs={{0,8},{8,0},{16,24},{24,16},{1,9},{9,1},{17,25},{25,17},{2,10},{10... | collective-permute-start | bytes 786440 | tf_op jit(solution)/shard_map/ppermute | solution.py:27
  78.3 0.0 collective-permute-done.10
  78.3 9.8 %collective-permute-start.7 = (bf16[2,256,256]{2,1,0:T(8,128)(2,1)S(1)}, bf16[2,256,256]{2,1,0:T(8,128)(2,1)S(1)}, u32[]{:S(2)}, u32[]{:S(2)}) collective-permute-start(bf16[2,256,256]{2,1,0:T(8,128)(2,1)S(1)} %get-tuple-element.19), channel_id=1, source_target_pairs={{0,16},{8,24},{16,0},{24,8},{1,17},{9,25},{17,1},{25,9},{2,18},{10... | collective-permute-start | bytes 786440 | tf_op jit(solution)/shard_map/ppermute | solution.py:27
  88.1 18.2 %collective-permute-done.8.refs_3_ = bf16[2,256,512]{2,1,0:T(8,128)(2,1)S(1)} collective-permute-done((bf16[2,256,512]{2,1,0:T(8,128)(2,1)S(1)}, bf16[2,256,512]{2,1,0:T(8,128)(2,1)S(1)}, u32[]{:S(2)}, u32[]{:S(2)}) %collective-permute-start.8) | collective-permute-done | bytes 524320 | tf_op jit(solution)/shard_map/ppermute | solution.py:27
  106.3 3.8 %shard_map.115 = bf16[1024,512]{1,0:T(8,128)(2,1)} custom-call(s32[4]{0:T(128)S(1)} %pad_add_fusion.refs_0_, bf16[1024,1024]{1,0:T(8,128)(2,1)} %bitcast.4.refs_1_, bf16[2,256,512]{2,1,0:T(8,128)(2,1)S(1)} %pad_maximum_fusion.refs_2_, bf16[2,256,512]{2,1,0:T(8,128)(2,1)S(1)} %collective-permute-done.8.refs_3_), custom_call_target="tpu_custom_call" | custom-call | flops 1073741824 | bytes 4194320 | tf_op jit(solution)/shard_map/pallas_call | solution.py:48
  110.1 1.8 %collective-permute-done.6 = bf16[2,256,256]{2,1,0:T(8,128)(2,1)S(1)} collective-permute-done((bf16[2,256,256]{2,1,0:T(8,128)(2,1)S(1)}, bf16[2,256,256]{2,1,0:T(8,128)(2,1)S(1)}, u32[]{:S(2)}, u32[]{:S(2)}) %collective-permute-start.6) | collective-permute-done | bytes 262176 | tf_op jit(solution)/shard_map/ppermute | solution.py:27
  111.9 0.1 convert_add_fusion.1
  112.0 0.7 fusion.17
  112.7 0.0 collective-permute-done.7
  112.7 0.1 convert_add_fusion
  112.7 0.0 copy-start.5
  112.7 0.0 copy-start.6
  112.7 0.7 fusion.18
  113.4 3.9 %all-to-all-start.1 = ((bf16[8,128,512]{2,1,0:T(8,128)(2,1)}), bf16[8,128,512]{2,1,0:T(8,128)(2,1)S(1)}, u32[]{:S(2)}, u32[]{:S(2)}) async-start(bf16[8,128,512]{2,1,0:T(8,128)(2,1)} %bitcast.12), calls=%async_computation.1 | async-start | bytes 2097152 | tf_op jit(solution)/shard_map/all_to_all | solution.py:43
  117.3 21.1 %collective-permute-start.13 = (bf16[128,256]{1,0:T(8,128)(2,1)S(1)}, bf16[128,256]{1,0:T(8,128)(2,1)}, u32[]{:S(2)}, u32[]{:S(2)}) collective-permute-start(bf16[128,256]{1,0:T(8,128)(2,1)S(1)} %add_convert_fusion.1), channel_id=1, source_target_pairs={{0,256},{256,0},{1,257},{257,1},{2,258},{258,2},{3,259},{259,3},{4... | collective-permute-start | bytes 196616 | tf_op jit(solution)/shard_map/ppermute | solution.py:31
  138.4 0.1 reduce
  138.5 1.9 %collective-permute-start.12 = (bf16[256,256]{1,0:T(8,128)(2,1)}, bf16[256,256]{1,0:T(8,128)(2,1)S(1)}, u32[]{:S(2)}, u32[]{:S(2)}) collective-permute-start(bf16[256,256]{1,0:T(8,128)(2,1)} %fusion.18), channel_id=1, source_target_pairs={{0,8},{8,0},{16,24},{24,16},{1,9},{9,1},{17,25},{25,17},{2,10},{10... | collective-permute-start | bytes 393224 | tf_op jit(solution)/shard_map/ppermute | solution.py:27
  140.4 4.6 %collective-permute-start.11 = (bf16[256,256]{1,0:T(8,128)(2,1)}, bf16[256,256]{1,0:T(8,128)(2,1)S(1)}, u32[]{:S(2)}, u32[]{:S(2)}) collective-permute-start(bf16[256,256]{1,0:T(8,128)(2,1)} %fusion.17), channel_id=1, source_target_pairs={{0,16},{8,24},{16,0},{24,8},{1,17},{9,25},{17,1},{25,9},{2,18},{10... | collective-permute-start | bytes 393224 | tf_op jit(solution)/shard_map/ppermute | solution.py:27
  145.0 7.9 %collective-permute-done.13 = bf16[128,256]{1,0:T(8,128)(2,1)} collective-permute-done((bf16[128,256]{1,0:T(8,128)(2,1)S(1)}, bf16[128,256]{1,0:T(8,128)(2,1)}, u32[]{:S(2)}, u32[]{:S(2)}) %collective-permute-start.13) | collective-permute-done | bytes 65568 | tf_op jit(solution)/shard_map/ppermute | solution.py:31
  152.9 0.9 add_convert_fusion
  153.8 5.9 %collective-permute-start.14 = (bf16[128,256]{1,0:T(8,128)(2,1)S(1)}, bf16[128,256]{1,0:T(8,128)(2,1)S(1)}, u32[]{:S(2)}, u32[]{:S(2)}) collective-permute-start(bf16[128,256]{1,0:T(8,128)(2,1)S(1)} %add_convert_fusion), channel_id=1, source_target_pairs={{0,32},{32,0},{1,33},{33,1},{2,34},{34,2},{3,35},{35,3},{4,36},{36... | collective-permute-start | bytes 196616 | tf_op jit(solution)/shard_map/ppermute | solution.py:31
  159.7 0.0 collective-permute-done.12
  159.7 0.0 collective-permute-done.11
  159.8 0.0 copy-start.8
  159.8 0.0 copy-start.9
  159.8 0.5 multiply_bitcast_fusion
  160.3 0.1 fusion.7
  160.4 0.1 collective-permute-done.14
  160.6 0.2 copy-done.8
  160.8 0.1 copy-done.9
  160.8 1.0 bitcast_dynamic-update-slice_fusion
  161.8 0.0 all-to-all-done.1
  161.8 0.1 convert_reduce_fusion
  161.9 0.7 multiply_convert_fusion.2
  (19 shorter events, 0.2 us)
Async XLA Ops:
  0.6 1.6 copy-start
  2.5 1.3 copy-start.2
  3.8 7.4 %copy-start.4 = (f32[1,256,512]{2,1,0:T(8,128)S(1)}, f32[1,256,512]{2,1,0:T(8,128)}, u32[]{:S(2)}) copy-start(f32[1,256,512]{2,1,0:T(8,128)} %param.12) | copy-start | bytes 1572868
  3.8 20.2 %copy-start.1 = (bf16[128,8192]{1,0:T(8,128)(2,1)S(1)}, bf16[128,8192]{1,0:T(8,128)(2,1)}, u32[]{:S(2)}) copy-start(bf16[128,8192]{1,0:T(8,128)(2,1)} %hidden_ref.1) | copy-start | bytes 6291460
  3.8 20.2 %copy-start.3 = (bf16[128,512]{1,0:T(8,128)(2,1)S(1)}, bf16[128,512]{1,0:T(8,128)(2,1)}, u32[]{:S(2)}) copy-start(bf16[128,512]{1,0:T(8,128)(2,1)} %grad_ref.1) | copy-start | bytes 393220
  3.8 69.6 %all-to-all-start = ((bf16[8,128,1024]{2,1,0:T(8,128)(2,1)}), bf16[8,128,1024]{2,1,0:T(8,128)(2,1)}, u32[]{:S(2)}, u32[]{:S(2)}) async-start(bf16[8,128,1024]{2,1,0:T(8,128)(2,1)} %copy-done.2), calls=%async_computation | async-start | bytes 4194304 | tf_op jit(solution)/shard_map/all_to_all | solution.py:43
  11.3 38.5 %collective-permute-start = (bf16[256,512]{1,0:T(8,128)(2,1)S(1)}, bf16[256,512]{1,0:T(8,128)(2,1)}, u32[]{:S(2)}, u32[]{:S(2)}) collective-permute-start(bf16[256,512]{1,0:T(8,128)(2,1)S(1)} %multiply_convert_fusion), channel_id=1, source_target_pairs={{0,16},{8,24},{16,0},{24,8},{1,17},{9,25},{17,1},{25,9},{2,18},{10... | collective-permute-start | bytes 786440 | tf_op jit(solution)/shard_map/ppermute | solution.py:27
  20.9 7.5 %collective-permute-start.1 = (bf16[128,256]{1,0:T(8,128)(2,1)S(1)}, bf16[128,256]{1,0:T(8,128)(2,1)S(1)}, u32[]{:S(2)}, u32[]{:S(2)}) collective-permute-start(bf16[128,256]{1,0:T(8,128)(2,1)S(1)} %dynamic-slice_bitcast_fusion), channel_id=1, source_target_pairs={{0,32},{32,0},{1,33},{33,1},{2,34},{34,2},{3,35},{35,3},{4,36},{36... | collective-permute-start | bytes 196616 | tf_op jit(solution)/shard_map/ppermute | solution.py:31
  24.5 14.8 %collective-permute-start.2 = (bf16[128,512]{1,0:T(8,128)(2,1)S(1)}, bf16[128,512]{1,0:T(8,128)(2,1)S(1)}, u32[]{:S(2)}, u32[]{:S(2)}) collective-permute-start(bf16[128,512]{1,0:T(8,128)(2,1)S(1)} %get-tuple-element.14), channel_id=1, source_target_pairs={{0,4},{4,0},{1,5},{5,1},{2,6},{6,2},{3,7},{7,3},{8,12},{12,8},{9,1... | collective-permute-start | bytes 393224 | tf_op jit(solution)/shard_map/ppermute | solution.py:31
  28.4 40.3 %collective-permute-start.9 = (bf16[128,256]{1,0:T(8,128)(2,1)S(1)}, bf16[128,256]{1,0:T(8,128)(2,1)S(1)}, u32[]{:S(2)}, u32[]{:S(2)}) collective-permute-start(bf16[128,256]{1,0:T(8,128)(2,1)S(1)} %fusion.19), channel_id=1, source_target_pairs={{0,64},{64,0},{128,192},{192,128},{1,65},{65,1},{129,193},{193,129... | collective-permute-start | bytes 196616 | tf_op jit(solution)/shard_map/ppermute | solution.py:31
  39.3 34.1 %collective-permute-start.3 = (bf16[256,512]{1,0:T(8,128)(2,1)S(1)}, bf16[256,512]{1,0:T(8,128)(2,1)S(1)}, u32[]{:S(2)}, u32[]{:S(2)}) collective-permute-start(bf16[256,512]{1,0:T(8,128)(2,1)S(1)} %constant_dynamic-update-slice_fusion.refs_2_), channel_id=1, source_target_pairs={{0,1},{1,2},{2,3},{3,0},{4,5},{5,6},{6,7},{7,4},{8,9},{9,10},{10,1... | collective-permute-start | bytes 786440 | tf_op jit(solution)/shard_map/ppermute | solution.py:145
  42.3 31.1 %collective-permute-start.4 = (bf16[256,512]{1,0:T(8,128)(2,1)S(1)}, bf16[256,512]{1,0:T(8,128)(2,1)S(1)}, u32[]{:S(2)}, u32[]{:S(2)}) collective-permute-start(bf16[256,512]{1,0:T(8,128)(2,1)S(1)} %constant_dynamic-update-slice_fusion.refs_2_), channel_id=1, source_target_pairs={{0,2},{1,3},{2,0},{3,1},{4,6},{5,7},{6,4},{7,5},{8,10},{9,11},{10,... | collective-permute-start | bytes 786440 | tf_op jit(solution)/shard_map/ppermute | solution.py:145
  46.7 26.7 %collective-permute-start.5 = (bf16[256,512]{1,0:T(8,128)(2,1)S(1)}, bf16[256,512]{1,0:T(8,128)(2,1)S(1)}, u32[]{:S(2)}, u32[]{:S(2)}) collective-permute-start(bf16[256,512]{1,0:T(8,128)(2,1)S(1)} %constant_dynamic-update-slice_fusion.refs_2_), channel_id=1, source_target_pairs={{0,3},{1,0},{2,1},{3,2},{4,7},{5,4},{6,5},{7,6},{8,11},{9,8},{10,9... | collective-permute-start | bytes 786440 | tf_op jit(solution)/shard_map/ppermute | solution.py:145
  50.8 55.5 %collective-permute-start.8 = (bf16[2,256,512]{2,1,0:T(8,128)(2,1)S(1)}, bf16[2,256,512]{2,1,0:T(8,128)(2,1)S(1)}, u32[]{:S(2)}, u32[]{:S(2)}) collective-permute-start(bf16[2,256,512]{2,1,0:T(8,128)(2,1)S(1)} %pad_maximum_fusion.refs_2_), channel_id=1, source_target_pairs={{0,8},{8,0},{16,24},{24,16},{1,9},{9,1},{17,25},{25,17},{2,10},{10... | collective-permute-start | bytes 1572872 | tf_op jit(solution)/shard_map/ppermute | solution.py:27
  68.7 9.6 %collective-permute-start.10 = (bf16[128,256]{1,0:T(8,128)(2,1)S(1)}, bf16[128,256]{1,0:T(8,128)(2,1)S(1)}, u32[]{:S(2)}, u32[]{:S(2)}) collective-permute-start(bf16[128,256]{1,0:T(8,128)(2,1)S(1)} %add_convert_fusion.2), channel_id=1, source_target_pairs={{0,128},{64,192},{128,0},{192,64},{1,129},{65,193},{129,1},{193,65... | collective-permute-start | bytes 196616 | tf_op jit(solution)/shard_map/ppermute | solution.py:31
  76.3 35.6 %collective-permute-start.6 = (bf16[2,256,256]{2,1,0:T(8,128)(2,1)S(1)}, bf16[2,256,256]{2,1,0:T(8,128)(2,1)S(1)}, u32[]{:S(2)}, u32[]{:S(2)}) collective-permute-start(bf16[2,256,256]{2,1,0:T(8,128)(2,1)S(1)} %get-tuple-element.17), channel_id=1, source_target_pairs={{0,8},{8,0},{16,24},{24,16},{1,9},{9,1},{17,25},{25,17},{2,10},{10... | collective-permute-start | bytes 786440 | tf_op jit(solution)/shard_map/ppermute | solution.py:27
  78.3 34.3 %collective-permute-start.7 = (bf16[2,256,256]{2,1,0:T(8,128)(2,1)S(1)}, bf16[2,256,256]{2,1,0:T(8,128)(2,1)S(1)}, u32[]{:S(2)}, u32[]{:S(2)}) collective-permute-start(bf16[2,256,256]{2,1,0:T(8,128)(2,1)S(1)} %get-tuple-element.19), channel_id=1, source_target_pairs={{0,16},{8,24},{16,0},{24,8},{1,17},{9,25},{17,1},{25,9},{2,18},{10... | collective-permute-start | bytes 786440 | tf_op jit(solution)/shard_map/ppermute | solution.py:27
  112.7 47.1 %copy-start.5 = (bf16[1,256,512]{2,1,0:T(8,128)(2,1)S(1)}, bf16[1,256,512]{2,1,0:T(8,128)(2,1)}, u32[]{:S(2)}) copy-start(bf16[1,256,512]{2,1,0:T(8,128)(2,1)} %param.14) | copy-start | bytes 786436
  112.7 47.1 %copy-start.6 = (f32[1,256,512]{2,1,0:T(8,128)S(1)}, f32[1,256,512]{2,1,0:T(8,128)}, u32[]{:S(2)}) copy-start(f32[1,256,512]{2,1,0:T(8,128)} %param.13) | copy-start | bytes 1572868
  113.4 48.4 %all-to-all-start.1 = ((bf16[8,128,512]{2,1,0:T(8,128)(2,1)}), bf16[8,128,512]{2,1,0:T(8,128)(2,1)S(1)}, u32[]{:S(2)}, u32[]{:S(2)}) async-start(bf16[8,128,512]{2,1,0:T(8,128)(2,1)} %bitcast.12), calls=%async_computation.1 | async-start | bytes 2097152 | tf_op jit(solution)/shard_map/all_to_all | solution.py:43
  117.3 35.6 %collective-permute-start.13 = (bf16[128,256]{1,0:T(8,128)(2,1)S(1)}, bf16[128,256]{1,0:T(8,128)(2,1)}, u32[]{:S(2)}, u32[]{:S(2)}) collective-permute-start(bf16[128,256]{1,0:T(8,128)(2,1)S(1)} %add_convert_fusion.1), channel_id=1, source_target_pairs={{0,256},{256,0},{1,257},{257,1},{2,258},{258,2},{3,259},{259,3},{4... | collective-permute-start | bytes 196616 | tf_op jit(solution)/shard_map/ppermute | solution.py:31
  138.5 21.2 %collective-permute-start.12 = (bf16[256,256]{1,0:T(8,128)(2,1)}, bf16[256,256]{1,0:T(8,128)(2,1)S(1)}, u32[]{:S(2)}, u32[]{:S(2)}) collective-permute-start(bf16[256,256]{1,0:T(8,128)(2,1)} %fusion.18), channel_id=1, source_target_pairs={{0,8},{8,0},{16,24},{24,16},{1,9},{9,1},{17,25},{25,17},{2,10},{10... | collective-permute-start | bytes 393224 | tf_op jit(solution)/shard_map/ppermute | solution.py:27
  140.4 19.3 %collective-permute-start.11 = (bf16[256,256]{1,0:T(8,128)(2,1)}, bf16[256,256]{1,0:T(8,128)(2,1)S(1)}, u32[]{:S(2)}, u32[]{:S(2)}) collective-permute-start(bf16[256,256]{1,0:T(8,128)(2,1)} %fusion.17), channel_id=1, source_target_pairs={{0,16},{8,24},{16,0},{24,8},{1,17},{9,25},{17,1},{25,9},{2,18},{10... | collective-permute-start | bytes 393224 | tf_op jit(solution)/shard_map/ppermute | solution.py:27
  153.8 6.8 %collective-permute-start.14 = (bf16[128,256]{1,0:T(8,128)(2,1)S(1)}, bf16[128,256]{1,0:T(8,128)(2,1)S(1)}, u32[]{:S(2)}, u32[]{:S(2)}) collective-permute-start(bf16[128,256]{1,0:T(8,128)(2,1)S(1)} %add_convert_fusion), channel_id=1, source_target_pairs={{0,32},{32,0},{1,33},{33,1},{2,34},{34,2},{3,35},{35,3},{4,36},{36... | collective-permute-start | bytes 196616 | tf_op jit(solution)/shard_map/ppermute | solution.py:31
  159.8 1.0 copy-start.8
  159.8 1.0 copy-start.9
  161.8 0.9 copy-start.7

commit v2 on v1

v2 whole, which is shorter than its diff:
```python
import jax
import jax.numpy as jnp
from jax import lax
from jax.experimental import pallas as pl
from jax.experimental.pallas import tpu as pltpu
from jax.sharding import Mesh, PartitionSpec as P

NORM_EPS = 1e-05
ADAM_EPS = 1e-08
INNER_RATE = 0.6

REP = ("zh", "x", "c")
FSDP = ("zq", "zp", "y")
NEAR = ("zp", "y")
VMEM = pl.BlockSpec(memory_space=pltpu.VMEM)
SMEM = pl.BlockSpec(memory_space=pltpu.SMEM)
LAST_COST = 1 << 36
PARAMS = pltpu.CompilerParams(vmem_limit_bytes=8 * 1024 * 1024)


def outer_step(mean_cols, anchor_part, momentum_part):
    delta = anchor_part - mean_cols
    momentum_next = 0.9 * momentum_part + delta
    return (anchor_part - 0.7 * (delta + 0.9 * momentum_next), momentum_next)


def swap(value, bit, name):
    with jax.named_scope(name):
        return lax.ppermute(value, "zq", [(i, i ^ bit) for i in range(4)])


def flip(value, axis, bit=1, name="rep_sum"):
    with jax.named_scope(name):
        return lax.ppermute(value, axis, [(i, i ^ bit) for i in range(lax.axis_size(axis))])


def add(a, b):
    return (a.astype(jnp.float32) + b.astype(jnp.float32)).astype(jnp.bfloat16)


def exchange(value, axes):
    return lax.all_to_all(value, axes, split_axis=0, concat_axis=0, tiled=True)


def kernel_call(body, outs, args, flops=0, scalars=0, scratch=(), behind=()):
    moved = sum(a.size * a.dtype.itemsize for a in (*args, *outs))
    given = len(args)

    def run(*refs):
        body(*refs[:given], *refs[given + len(behind) :])

    args = (*args, *behind)
    return pl.pallas_call(
        run,
        out_shape=outs,
        in_specs=[SMEM] * scalars + [VMEM] * (given - scalars) + [pl.BlockSpec(memory_space=pl.ANY)] * len(behind),
        out_specs=[VMEM] * len(outs),
        scratch_shapes=list(scratch),
        compiler_params=PARAMS,
        cost_estimate=pl.CostEstimate(flops=flops, bytes_accessed=moved, transcendentals=0),
    )(*args)


def prepare(far, near, rows, hidden_ref, grad_ref, tiles_ref, factor_ref):
    tokens, features = hidden_ref.shape
    wide = far * rows
    total = jnp.zeros((tokens, rows), jnp.float32)
    for a in range(near):
        for q in range(far):
            part = hidden_ref[:, (q * near + a) * rows : (q * near + a + 1) * rows]
            tiles_ref[a, :, q * rows : (q + 1) * rows] = part
            part = part.astype(jnp.float32)
            total = total + part * part
    factor = lax.rsqrt(jnp.sum(total, axis=1, keepdims=True) / features + NORM_EPS)
    factor_ref[...] = factor
    scaled = (grad_ref[...].astype(jnp.float32) * factor).astype(jnp.bfloat16)
    for a in range(near):
        tiles_ref[a, :, wide:] = scaled


def block_of(place_ref, dh, dl, rows):
    block = (place_ref[0] ^ dh) * 2 + (place_ref[1] ^ dl)
    return pl.ds(pl.multiple_of(block * rows, rows), rows)


def gradient_blocks(rows, wide, place_ref, tiles_ref, far_ref, part_ref, keep_ref, send_ref, last_ref, part_out):
    for dl in (1, 0):
        for dh in range(2):
            left = tiles_ref[:, block_of(place_ref, dh, dl, rows)]
            value = lax.dot_general(left, tiles_ref[:, wide:], (((0,), (0,)), ((), ())), preferred_element_type=jnp.float32)
            if dl:
                send_ref[dh] = value.astype(jnp.bfloat16)
            else:
                keep_ref[dh] = value
    last_ref[...] = far_ref[...]
    part_out[...] = part_ref[...]


def first_sum(keep_ref, got_ref, mine_ref, send_ref):
    mine_ref[...] = keep_ref[0] + got_ref[0].astype(jnp.float32)
    send_ref[...] = (keep_ref[1] + got_ref[1].astype(jnp.float32)).astype(jnp.bfloat16)


def second_sum(mine_ref, got_ref, grad_ref):
    grad_ref[...] = mine_ref[...] + got_ref[...].astype(jnp.float32)


def key_sum(partial_ref, factor_ref, keys_ref):
    total = partial_ref[0].astype(jnp.float32)
    for i in range(1, partial_ref.shape[0]):
        total = total + partial_ref[i].astype(jnp.float32)
    keys_ref[...] = (total * factor_ref[...]).astype(jnp.bfloat16)


def key_partials(rows, multiplier, place_ref, tiles_ref, *refs):
    total = None
    for dh in range(2):
        for dl in range(2):
            left = tiles_ref[:, block_of(place_ref, dh, dl, rows)]
            right = refs[2 * dh + dl][...]
            value = jnp.dot(left, right, preferred_element_type=jnp.float32)
            total = value if total is None else total + value
    refs[4][...] = (total * multiplier).astype(jnp.bfloat16)


def on_device(
    hidden_in, gain, key_grad, weights, first_moment, second_moment, anchor, momentum, fragment
):
    tokens, features = hidden_in.shape
    key_width = key_grad.shape[1]
    multiplier = float(features) ** (-0.5)
    weight_now = weights[0]
    rows = weight_now.shape[0]
    near = lax.axis_size(NEAR)
    far = lax.axis_size("zq")
    far_index = lax.axis_index("zq")
    place = jnp.stack([far_index >> 1, far_index & 1, lax.axis_index("zp")]).astype(jnp.int32)
    shape = jax.ShapeDtypeStruct
    f32, b16 = jnp.float32, jnp.bfloat16

    wide = far * rows
    tiles, factor = kernel_call(
        lambda *refs: prepare(far, near, rows, *refs),
        [shape((near, tokens, wide + key_width), b16), shape((tokens, 1), f32)],
        (hidden_in, key_grad),
    )
    tiles = exchange(tiles, NEAR).reshape(near * tokens, wide + key_width)

    frag_width = anchor.shape[1]
    col_offset = fragment[0] * frag_width
    start_cols = lax.dynamic_slice_in_dim(weight_now, col_offset, frag_width, 1).astype(b16)
    core = lax.axis_index("c")
    mine = lax.dynamic_slice_in_dim(start_cols, core * (rows // 2), rows // 2, 0)
    theirs = lax.dynamic_slice_in_dim(start_cols, (1 - core) * (rows // 2), rows // 2, 0)
    part = add(mine, flip(theirs, "c"))

    part = add(part, flip(part, "x", 1))

    own_gain = lax.dynamic_slice_in_dim(gain, lax.axis_index(FSDP) * rows, rows, 0)[:, None]
    weight_low = (weight_now * own_gain).astype(b16)
    near_low = swap(weight_low, 1, "weights_near")
    far_low = swap(weight_low, 2, "weights_far")

    flops = 2 * near * tokens * far * rows * key_width
    keep, send, last_low, part = kernel_call(
        lambda *refs: gradient_blocks(rows, wide, *refs),
        [shape((2, rows, key_width), f32), shape((2, rows, key_width), b16), shape(far_low.shape, b16), shape(part.shape, b16)],
        (place, tiles, far_low, part),
        flops,
        1,
        behind=(near_low,),
    )
    got = swap(send, 1, "gradient_near")
    last_low = swap(last_low, 1, "weights_last")
    part = add(part, flip(part, "x", 2))
    part = add(part, flip(part, "zh"))
    other = flip(part, "c")
    summed_cols = jnp.where(core == 0, jnp.concatenate([part, other]), jnp.concatenate([other, part])).astype(f32)
    mine, rest = kernel_call(
        first_sum, [shape((rows, key_width), f32), shape((rows, key_width), b16)], (keep, got)
    )
    last = swap(rest, 2, "gradient_far")
    (grad_sum,) = kernel_call(second_sum, [shape((rows, key_width), f32)], (mine, last), LAST_COST)
    gradient = grad_sum * (multiplier * own_gain)
    moment_next = 0.9 * first_moment[0] + 0.1 * gradient
    second_next = 0.95 * second_moment[0].astype(f32) + 0.05 * gradient * gradient
    inner = weight_now - INNER_RATE * (
        moment_next / (jnp.sqrt(second_next) + ADAM_EPS) + 0.1 * weight_now
    )
    (partial_keys,) = kernel_call(
        lambda *refs: key_partials(rows, multiplier, *refs),
        [shape((near * tokens, key_width), b16)],
        (place, tiles, weight_low, near_low, far_low, last_low),
        flops,
        1,
    )
    partial_keys = exchange(partial_keys.reshape(near, tokens, key_width), NEAR)
    (keys,) = kernel_call(key_sum, [shape((tokens, key_width), b16)], (partial_keys, factor))

    replicas = lax.axis_size(REP)
    fresh, momentum_out = outer_step(summed_cols / replicas, anchor, momentum)
    current = lax.dynamic_slice_in_dim(inner, col_offset, frag_width, 1)
    merged = 0.5 * current + 0.5 * fresh
    weights_out = lax.dynamic_update_slice_in_dim(inner, merged, col_offset, 1)
    return (keys, weights_out[None], momentum_out)


def solution(mesh):
    fine = Mesh(mesh.devices.reshape(2, 4, 2, 4, 2, 4), REP + FSDP)
    both = REP + FSDP
    return jax.shard_map(
        on_device,
        mesh=fine,
        in_specs=(
            P(both, None),
            P(),
            P(both, None),
            P(REP, FSDP, None),
            P(REP, FSDP, None),
            P(REP, FSDP, None),
            P(FSDP, None),
            P(FSDP, None),
            P(),
        ),
        out_specs=(P(both, None), P(REP, FSDP, None), P(FSDP, None)),
        check_vma=False,
    )
```

time: 166 us -> 156 us (0.940); the launches traced: 163 us -> 155 us
  starting transfers between devices: 107 us -> 91.6 us
  local copies, waits for them, and re-layouts: 4.59 us -> 12 us
  Pallas kernels: 7.5 us -> 9.37 us
    ppermute x6 -> x5, waiting for transfers between devices: 15.7 us -> 4.06 us  [flip(): lax.ppermute(value, axis, [(i, i ^ bit) for i in range(lax.axis_size(axis...]
    ppermute x3 -> x0, starting transfers between devices: 10.5 us -> none  [on_device(): lax.ppermute(both_grad, 'y', [(i, (i + k) % 4) for i in range(4)])]
    ppermute x6 -> x5, starting transfers between devices: 41.5 us -> 31.3 us  [flip(): lax.ppermute(value, axis, [(i, i ^ bit) for i in range(lax.axis_size(axis...]
    unnamed x21 -> x33, local copies, waits for them, and re-layouts: 3.2 us -> 10.4 us
    all_to_all x2, waiting for transfers between devices: 0.01 us -> 5.9 us  [exchange(): return lax.all_to_all(value, axes, split_axis=0, concat_axis=0, tiled=True)]
    ppermute x6 -> x5, starting transfers between devices: 44.9 us -> 49.9 us  [swap(): return lax.ppermute(value, 'zq', [(i, i ^ bit) for i in range(4)])]
    ppermute x6 -> x5, waiting for transfers between devices: 20 us -> 24.7 us  [swap(): return lax.ppermute(value, 'zq', [(i, i ^ bit) for i in range(4)])]
    pallas_call x4 -> x6, Pallas kernels: 7.5 us -> 9.37 us  [kernel_call(): pl.pallas_call(run, out_shape=outs, in_specs=[SMEM] * scalars + [VMEM] *...]
  transfers between devices with their start and end apart: 17 -> 12, of which waited for: 5 -> 8; matrix products, arithmetic and copies ran while one was open for 3% -> 5% of each run, Pallas kernels for 4% -> 3%
where the time goes in v2:
time: 156 us; the launch traced here: 155 us
  starting transfers between devices  91.6 us (59%)
  waiting for transfers between devices  34.7 us (22%)
  local copies, waits for them, and re-layouts  12 us (8%)
  Pallas kernels  9.37 us (6%)
  other arithmetic  5.96 us (4%)
  between operations  1.57 us (1%)
    ppermute x5, starting transfers between devices, swap(): return lax.ppermute(value, 'zq', [(i, i ^ bit) for i in range(4)])  49.9 us
    ppermute x5, starting transfers between devices, flip(): lax.ppermute(value, axis, [(i, i ^ bit) for i in range(lax.axis_size(axis...  31.3 us
    ppermute x5, waiting for transfers between devices, swap(): return lax.ppermute(value, 'zq', [(i, i ^ bit) for i in range(4)])  24.7 us
    unnamed x33, local copies, waits for them, and re-layouts  10.4 us
    all_to_all x2, starting transfers between devices, exchange(): return lax.all_to_all(value, axes, split_axis=0, concat_axis=0, tiled=True)  10.3 us
    pallas_call x6, Pallas kernels, kernel_call(): pl.pallas_call(run, out_shape=outs, in_specs=[SMEM] * scalars + [VMEM] *...  9.37 us
    all_to_all x2, waiting for transfers between devices, exchange(): return lax.all_to_all(value, axes, split_axis=0, concat_axis=0, tiled=True)  5.9 us
    ppermute x5, waiting for transfers between devices, flip(): lax.ppermute(value, axis, [(i, i ^ bit) for i in range(lax.axis_size(axis...  4.06 us
  transfers between devices with their start and end apart: 12, of which 8 were waited for; matrix products, arithmetic and copies ran while one was open for 5% of the time, Pallas kernels for 3%

profile of v2, /device:TPU:1, one launch (start us, length us, event | category | flops | bytes accessed | tf_op | source)
XLA Modules:
  0.0 155.2 jit_solution(1190095763827852692)
XLA Ops:
  0.6 0.0 copy-start.2
  0.6 1.6 %copy-done.2 = bf16[128,8192]{1,0:T(8,128)(2,1)S(1)} copy-done((bf16[128,8192]{1,0:T(8,128)(2,1)S(1)}, bf16[128,8192]{1,0:T(8,128)(2,1)}, u32[]{:S(2)}) %copy-start.2) | copy-done | bytes 2097176
  2.2 0.0 copy-start.5
  2.2 0.9 copy-done.5
  3.1 0.5 shard_map.112
  3.6 0.0 copy-start.1
  3.6 1.6 %copy-done.1 = bf16[8,128,1536]{2,1,0:T(8,128)(2,1)} copy-done((bf16[8,128,1536]{2,1,0:T(8,128)(2,1)}, bf16[8,128,1536]{2,1,0:T(8,128)(2,1)S(1)}, u32[]{:S(2)}) %copy-start.1) | copy-done | bytes 3145752
  5.2 6.4 %all-to-all-start = ((bf16[8,128,1536]{2,1,0:T(8,128)(2,1)}), bf16[8,128,1536]{2,1,0:T(8,128)(2,1)S(1)}, u32[]{:S(2)}, u32[]{:S(2)}) async-start(bf16[8,128,1536]{2,1,0:T(8,128)(2,1)} %copy-done.1), calls=%async_computation | async-start | bytes 6291456 | tf_op jit(solution)/shard_map/all_to_all | solution.py:42
  12.3 1.0 dynamic-slice_convert_fusion
  13.2 0.0 copy-start.9
  13.2 0.6 copy-done.9
  13.9 0.6 dynamic-slice_bitcast_fusion
  14.5 6.1 %collective-permute-start.2 = (bf16[128,256]{1,0:T(8,128)(2,1)}, bf16[128,256]{1,0:T(8,128)(2,1)S(1)}, u32[]{:S(2)}, u32[]{:S(2)}) collective-permute-start(bf16[128,256]{1,0:T(8,128)(2,1)} %dynamic-slice_bitcast_fusion), channel_id=1, source_target_pairs={{0,32},{32,0},{1,33},{33,1},{2,34},{34,2},{3,35},{35,3},{4,36},{36... | collective-permute-start | bytes 196616 | tf_op jit(solution)/shard_map/rep_sum/ppermute | solution.py:34
  20.6 0.8 broadcast_multiply_fusion
  21.4 1.1 fusion.7.refs_2_
  22.5 1.9 %collective-permute-start = (bf16[256,512]{1,0:T(8,128)(2,1)S(1)}, bf16[256,512]{1,0:T(8,128)(2,1)}, u32[]{:S(2)}, u32[]{:S(2)}) collective-permute-start(bf16[256,512]{1,0:T(8,128)(2,1)S(1)} %fusion.7.refs_2_), channel_id=1, source_target_pairs={{0,8},{8,0},{16,24},{24,16},{1,9},{9,1},{17,25},{25,17},{2,10},{10... | collective-permute-start | bytes 786440 | tf_op jit(solution)/shard_map/weights_near/ppermute | solution.py:29
  24.4 8.6 %collective-permute-start.1 = (bf16[256,512]{1,0:T(8,128)(2,1)S(1)}, bf16[256,512]{1,0:T(8,128)(2,1)}, u32[]{:S(2)}, u32[]{:S(2)}) collective-permute-start(bf16[256,512]{1,0:T(8,128)(2,1)S(1)} %fusion.7.refs_2_), channel_id=1, source_target_pairs={{0,16},{8,24},{16,0},{24,8},{1,17},{9,25},{17,1},{25,9},{2,18},{10... | collective-permute-start | bytes 786440 | tf_op jit(solution)/shard_map/weights_far/ppermute | solution.py:29
  33.0 0.0 collective-permute-done.2
  33.1 0.9 fusion.8
  33.9 3.1 %collective-permute-start.3 = (bf16[128,256]{1,0:T(8,128)(2,1)S(1)}, bf16[128,256]{1,0:T(8,128)(2,1)S(1)}, u32[]{:S(2)}, u32[]{:S(2)}) collective-permute-start(bf16[128,256]{1,0:T(8,128)(2,1)S(1)} %fusion.8), channel_id=1, source_target_pairs={{0,64},{64,0},{128,192},{192,128},{1,65},{65,1},{129,193},{193,129... | collective-permute-start | bytes 196616 | tf_op jit(solution)/shard_map/rep_sum/ppermute | solution.py:34
  37.1 0.1 pad_add_fusion.refs_0_
  37.1 2.2 %collective-permute-done.3 = bf16[128,256]{1,0:T(8,128)(2,1)S(1)} collective-permute-done((bf16[128,256]{1,0:T(8,128)(2,1)S(1)}, bf16[128,256]{1,0:T(8,128)(2,1)S(1)}, u32[]{:S(2)}, u32[]{:S(2)}) %collective-permute-start.3) | collective-permute-done | bytes 65568 | tf_op jit(solution)/shard_map/rep_sum/ppermute | solution.py:34
  39.4 8.0 %collective-permute-done.refs_4_.refs_3_ = bf16[256,512]{1,0:T(8,128)(2,1)} collective-permute-done((bf16[256,512]{1,0:T(8,128)(2,1)S(1)}, bf16[256,512]{1,0:T(8,128)(2,1)}, u32[]{:S(2)}, u32[]{:S(2)}) %collective-permute-start) | collective-permute-done | bytes 262176 | tf_op jit(solution)/shard_map/weights_near/ppermute | solution.py:29
  47.4 5.6 %collective-permute-done.1.refs_2_.refs_4_ = bf16[256,512]{1,0:T(8,128)(2,1)} collective-permute-done((bf16[256,512]{1,0:T(8,128)(2,1)S(1)}, bf16[256,512]{1,0:T(8,128)(2,1)}, u32[]{:S(2)}, u32[]{:S(2)}) %collective-permute-start.1) | collective-permute-done | bytes 262176 | tf_op jit(solution)/shard_map/weights_far/ppermute | solution.py:29
  53.0 2.0 %all-to-all-done = bf16[8,128,1536]{2,1,0:T(8,128)(2,1)S(1)} async-done(((bf16[8,128,1536]{2,1,0:T(8,128)(2,1)}), bf16[8,128,1536]{2,1,0:T(8,128)(2,1)S(1)}, u32[]{:S(2)}, u32[]{:S(2)}) %all-to-all-start) | async-done | bytes 3145760 | tf_op jit(solution)/shard_map/all_to_all | solution.py:42
  54.9 2.8 %shard_map.113 = (f32[2,256,512]{2,1,0:T(8,128)S(1)}, bf16[2,256,512]{2,1,0:T(8,128)(2,1)}, bf16[256,512]{1,0:T(8,128)(2,1)}, bf16[128,256]{1,0:T(8,128)(2,1)S(1)}) custom-call(s32[3]{0:T(128)S(1)} %pad_add_fusion.refs_0_, bf16[1024,1536]{1,0:T(8,128)(2,1)S(1)} %bitcast.28, bf16[256,512]{1,0:T(8,128)(2,1)} %collective-permute-done.1.refs_2_.refs_4_, ...), custom_call_target="tpu_custom_call" | custom-call | flops 1073741824 | bytes 5373964 | tf_op jit(solution)/shard_map/pallas_call | solution.py:53
  57.8 0.0 copy-start.3
  57.8 1.0 copy-done.3
  58.8 17.4 %collective-permute-start.5 = (bf16[2,256,512]{2,1,0:T(8,128)(2,1)}, bf16[2,256,512]{2,1,0:T(8,128)(2,1)}, u32[]{:S(2)}, u32[]{:S(2)}) collective-permute-start(bf16[2,256,512]{2,1,0:T(8,128)(2,1)} %get-tuple-element.15), channel_id=1, source_target_pairs={{0,8},{8,0},{16,24},{24,16},{1,9},{9,1},{17,25},{25,17},{2,10},{10... | collective-permute-start | bytes 1572872 | tf_op jit(solution)/shard_map/gradient_near/ppermute | solution.py:29
  76.2 4.7 %collective-permute-start.7 = (bf16[128,256]{1,0:T(8,128)(2,1)S(1)}, bf16[128,256]{1,0:T(8,128)(2,1)S(1)}, u32[]{:S(2)}, u32[]{:S(2)}) collective-permute-start(bf16[128,256]{1,0:T(8,128)(2,1)S(1)} %get-tuple-element.18), channel_id=1, source_target_pairs={{0,128},{64,192},{128,0},{192,64},{1,129},{65,193},{129,1},{193,65... | collective-permute-start | bytes 196616 | tf_op jit(solution)/shard_map/rep_sum/ppermute | solution.py:34
  80.9 1.9 %collective-permute-done.7 = bf16[128,256]{1,0:T(8,128)(2,1)S(1)} collective-permute-done((bf16[128,256]{1,0:T(8,128)(2,1)S(1)}, bf16[128,256]{1,0:T(8,128)(2,1)S(1)}, u32[]{:S(2)}, u32[]{:S(2)}) %collective-permute-start.7) | collective-permute-done | bytes 65568 | tf_op jit(solution)/shard_map/rep_sum/ppermute | solution.py:34
  82.7 0.0 copy-start.15
  82.7 12.7 %collective-permute-start.8 = (bf16[128,256]{1,0:T(8,128)(2,1)S(1)}, bf16[128,256]{1,0:T(8,128)(2,1)}, u32[]{:S(2)}, u32[]{:S(2)}) collective-permute-start(bf16[128,256]{1,0:T(8,128)(2,1)S(1)} %add_convert_fusion.1), channel_id=1, source_target_pairs={{0,256},{256,0},{1,257},{257,1},{2,258},{258,2},{3,259},{259,3},{4... | collective-permute-start | bytes 196616 | tf_op jit(solution)/shard_map/rep_sum/ppermute | solution.py:34
  95.5 1.9 %collective-permute-start.4 = (bf16[256,512]{1,0:T(8,128)(2,1)}, bf16[256,512]{1,0:T(8,128)(2,1)}, u32[]{:S(2)}, u32[]{:S(2)}) collective-permute-start(bf16[256,512]{1,0:T(8,128)(2,1)} %get-tuple-element.12), channel_id=1, source_target_pairs={{0,8},{8,0},{16,24},{24,16},{1,9},{9,1},{17,25},{25,17},{2,10},{10... | collective-permute-start | bytes 786440 | tf_op jit(solution)/shard_map/weights_last/ppermute | solution.py:29
  97.4 1.0 collective-permute-done.5.refs_1_
  98.4 1.2 copy-done.4
  99.6 1.8 %shard_map.116 = (f32[256,512]{1,0:T(8,128)S(1)}, bf16[256,512]{1,0:T(8,128)(2,1)}) custom-call(f32[2,256,512]{2,1,0:T(8,128)S(1)} %copy-done.4, bf16[2,256,512]{2,1,0:T(8,128)(2,1)} %collective-permute-done.5.refs_1_), custom_call_target="tpu_custom_call" | custom-call | bytes 2359296 | tf_op jit(solution)/shard_map/pallas_call | solution.py:53
  101.5 0.8 copy-done.6
  102.3 20.1 %collective-permute-start.6 = (bf16[256,512]{1,0:T(8,128)(2,1)}, bf16[256,512]{1,0:T(8,128)(2,1)}, u32[]{:S(2)}, u32[]{:S(2)}) collective-permute-start(bf16[256,512]{1,0:T(8,128)(2,1)} %get-tuple-element.17), channel_id=1, source_target_pairs={{0,16},{8,24},{16,0},{24,8},{1,17},{9,25},{17,1},{25,9},{2,18},{10... | collective-permute-start | bytes 786440 | tf_op jit(solution)/shard_map/gradient_far/ppermute | solution.py:29
  122.4 0.0 copy-done.15
  122.4 0.0 collective-permute-done.8
  122.4 0.9 add_convert_fusion
  123.3 4.8 %collective-permute-start.9 = (bf16[128,256]{1,0:T(8,128)(2,1)S(1)}, bf16[128,256]{1,0:T(8,128)(2,1)}, u32[]{:S(2)}, u32[]{:S(2)}) collective-permute-start(bf16[128,256]{1,0:T(8,128)(2,1)S(1)} %add_convert_fusion), channel_id=1, source_target_pairs={{0,32},{32,0},{1,33},{33,1},{2,34},{34,2},{3,35},{35,3},{4,36},{36... | collective-permute-start | bytes 196616 | tf_op jit(solution)/shard_map/rep_sum/ppermute | solution.py:34
  128.1 0.0 collective-permute-done.4.refs_5_
  128.1 2.4 %shard_map.114 = bf16[1024,512]{1,0:T(8,128)(2,1)S(1)} custom-call(s32[3]{0:T(128)S(1)} %pad_add_fusion.refs_0_, bf16[1024,1536]{1,0:T(8,128)(2,1)S(1)} %bitcast.29, bf16[256,512]{1,0:T(8,128)(2,1)S(1)} %fusion.7.refs_2_, bf16[256,512]{1,0:T(8,128)(2,1)} %collective-permute-done.refs_4_.refs_3_, bf16[256,512]{1,0:T(8,128)(2,1)} %collective-permute-done.1.refs_2_.refs_4_, ...), custom_call_target="tpu_custom_call" | custom-call | flops 1073741824 | bytes 5242892 | tf_op jit(solution)/shard_map/pallas_call | solution.py:53
  130.4 0.0 copy-start
  130.4 1.0 copy-done
  131.4 4.0 %all-to-all-start.1 = ((bf16[8,128,512]{2,1,0:T(8,128)(2,1)}), bf16[8,128,512]{2,1,0:T(8,128)(2,1)S(1)}, u32[]{:S(2)}, u32[]{:S(2)}) async-start(bf16[8,128,512]{2,1,0:T(8,128)(2,1)} %bitcast.30), calls=%async_computation.1 | async-start | bytes 2097152 | tf_op jit(solution)/shard_map/all_to_all | solution.py:42
  135.4 10.1 %collective-permute-done.6.refs_1_ = bf16[256,512]{1,0:T(8,128)(2,1)} collective-permute-done((bf16[256,512]{1,0:T(8,128)(2,1)}, bf16[256,512]{1,0:T(8,128)(2,1)}, u32[]{:S(2)}, u32[]{:S(2)}) %collective-permute-start.6) | collective-permute-done | bytes 262176 | tf_op jit(solution)/shard_map/gradient_far/ppermute | solution.py:29
  145.5 1.0 copy-done.7
  146.5 1.1 shard_map.117
  147.6 0.0 copy-start.13
  147.6 0.0 copy-start.14
  147.6 0.0 copy-done.8
  147.6 0.1 copy-done.11
  147.8 0.1 copy-done.12
  147.8 0.5 fusion.6
  148.3 0.0 collective-permute-done.9
  148.4 0.3 copy-done.13
  148.6 0.1 copy-done.14
  148.7 1.7 %bitcast_dynamic-update-slice_fusion = (f32[1,256,512]{2,1,0:T(8,128)S(1)}, f32[256,256]{1,0:T(8,128)}) fusion(f32[1,256,512]{2,1,0:T(8,128)S(1)} %copy.12, s32[]{:T(128)S(6)} %select_n.23, f32[256,256]{1,0:T(8,128)S(1)} %copy-done.13, f32[256,512]{1,0:T(8,128)S(1)} %fusion.6, bf16[128,256]{1,0:T(8,128)(2,1)S(1)} %add_convert_fusion, ...), kind=kLoop, calls=%fused_computation.12 | loop fusion | flops 1310720 | bytes 1441797 | tf_op jit(solution)/shard_map/dynamic_update_slice | solution.py:204
  150.4 4.0 %all-to-all-done.1.refs_0_ = bf16[8,128,512]{2,1,0:T(8,128)(2,1)S(1)} async-done(((bf16[8,128,512]{2,1,0:T(8,128)(2,1)}), bf16[8,128,512]{2,1,0:T(8,128)(2,1)S(1)}, u32[]{:S(2)}, u32[]{:S(2)}) %all-to-all-start.1) | async-done | bytes 1048608 | tf_op jit(solution)/shard_map/all_to_all | solution.py:42
  154.4 0.8 shard_map.115
  155.2 0.0 copy-done.10
  (10 shorter events, 0.1 us)
Async XLA Ops:
  0.6 1.6 %copy-start.2 = (bf16[128,8192]{1,0:T(8,128)(2,1)S(1)}, bf16[128,8192]{1,0:T(8,128)(2,1)}, u32[]{:S(2)}) copy-start(bf16[128,8192]{1,0:T(8,128)(2,1)} %refs_0_.1) | copy-start | bytes 6291460
  2.2 0.9 copy-start.5
  3.6 1.6 %copy-start.1 = (bf16[8,128,1536]{2,1,0:T(8,128)(2,1)}, bf16[8,128,1536]{2,1,0:T(8,128)(2,1)S(1)}, u32[]{:S(2)}) copy-start(bf16[8,128,1536]{2,1,0:T(8,128)(2,1)S(1)} %get-tuple-element.11) | copy-start | bytes 9437188
  5.2 49.7 %all-to-all-start = ((bf16[8,128,1536]{2,1,0:T(8,128)(2,1)}), bf16[8,128,1536]{2,1,0:T(8,128)(2,1)S(1)}, u32[]{:S(2)}, u32[]{:S(2)}) async-start(bf16[8,128,1536]{2,1,0:T(8,128)(2,1)} %copy-done.1), calls=%async_computation | async-start | bytes 6291456 | tf_op jit(solution)/shard_map/all_to_all | solution.py:42
  13.2 0.7 copy-start.9
  14.5 18.5 %collective-permute-start.2 = (bf16[128,256]{1,0:T(8,128)(2,1)}, bf16[128,256]{1,0:T(8,128)(2,1)S(1)}, u32[]{:S(2)}, u32[]{:S(2)}) collective-permute-start(bf16[128,256]{1,0:T(8,128)(2,1)} %dynamic-slice_bitcast_fusion), channel_id=1, source_target_pairs={{0,32},{32,0},{1,33},{33,1},{2,34},{34,2},{3,35},{35,3},{4,36},{36... | collective-permute-start | bytes 196616 | tf_op jit(solution)/shard_map/rep_sum/ppermute | solution.py:34
  22.5 24.9 %collective-permute-start = (bf16[256,512]{1,0:T(8,128)(2,1)S(1)}, bf16[256,512]{1,0:T(8,128)(2,1)}, u32[]{:S(2)}, u32[]{:S(2)}) collective-permute-start(bf16[256,512]{1,0:T(8,128)(2,1)S(1)} %fusion.7.refs_2_), channel_id=1, source_target_pairs={{0,8},{8,0},{16,24},{24,16},{1,9},{9,1},{17,25},{25,17},{2,10},{10... | collective-permute-start | bytes 786440 | tf_op jit(solution)/shard_map/weights_near/ppermute | solution.py:29
  24.4 28.5 %collective-permute-start.1 = (bf16[256,512]{1,0:T(8,128)(2,1)S(1)}, bf16[256,512]{1,0:T(8,128)(2,1)}, u32[]{:S(2)}, u32[]{:S(2)}) collective-permute-start(bf16[256,512]{1,0:T(8,128)(2,1)S(1)} %fusion.7.refs_2_), channel_id=1, source_target_pairs={{0,16},{8,24},{16,0},{24,8},{1,17},{9,25},{17,1},{25,9},{2,18},{10... | collective-permute-start | bytes 786440 | tf_op jit(solution)/shard_map/weights_far/ppermute | solution.py:29
  33.9 5.4 %collective-permute-start.3 = (bf16[128,256]{1,0:T(8,128)(2,1)S(1)}, bf16[128,256]{1,0:T(8,128)(2,1)S(1)}, u32[]{:S(2)}, u32[]{:S(2)}) collective-permute-start(bf16[128,256]{1,0:T(8,128)(2,1)S(1)} %fusion.8), channel_id=1, source_target_pairs={{0,64},{64,0},{128,192},{192,128},{1,65},{65,1},{129,193},{193,129... | collective-permute-start | bytes 196616 | tf_op jit(solution)/shard_map/rep_sum/ppermute | solution.py:34
  57.8 1.0 copy-start.3
  58.8 39.7 %collective-permute-start.5 = (bf16[2,256,512]{2,1,0:T(8,128)(2,1)}, bf16[2,256,512]{2,1,0:T(8,128)(2,1)}, u32[]{:S(2)}, u32[]{:S(2)}) collective-permute-start(bf16[2,256,512]{2,1,0:T(8,128)(2,1)} %get-tuple-element.15), channel_id=1, source_target_pairs={{0,8},{8,0},{16,24},{24,16},{1,9},{9,1},{17,25},{25,17},{2,10},{10... | collective-permute-start | bytes 1572872 | tf_op jit(solution)/shard_map/gradient_near/ppermute | solution.py:29
  76.2 6.5 %collective-permute-start.7 = (bf16[128,256]{1,0:T(8,128)(2,1)S(1)}, bf16[128,256]{1,0:T(8,128)(2,1)S(1)}, u32[]{:S(2)}, u32[]{:S(2)}) collective-permute-start(bf16[128,256]{1,0:T(8,128)(2,1)S(1)} %get-tuple-element.18), channel_id=1, source_target_pairs={{0,128},{64,192},{128,0},{192,64},{1,129},{65,193},{129,1},{193,65... | collective-permute-start | bytes 196616 | tf_op jit(solution)/shard_map/rep_sum/ppermute | solution.py:34
  82.7 39.6 %copy-start.15 = (bf16[128,256]{1,0:T(8,128)(2,1)}, bf16[128,256]{1,0:T(8,128)(2,1)S(1)}, u32[]{:S(2)}) copy-start(bf16[128,256]{1,0:T(8,128)(2,1)S(1)} %add_convert_fusion.1) | copy-start | bytes 196612
  82.7 39.6 %collective-permute-start.8 = (bf16[128,256]{1,0:T(8,128)(2,1)S(1)}, bf16[128,256]{1,0:T(8,128)(2,1)}, u32[]{:S(2)}, u32[]{:S(2)}) collective-permute-start(bf16[128,256]{1,0:T(8,128)(2,1)S(1)} %add_convert_fusion.1), channel_id=1, source_target_pairs={{0,256},{256,0},{1,257},{257,1},{2,258},{258,2},{3,259},{259,3},{4... | collective-permute-start | bytes 196616 | tf_op jit(solution)/shard_map/rep_sum/ppermute | solution.py:34
  95.5 32.6 %collective-permute-start.4 = (bf16[256,512]{1,0:T(8,128)(2,1)}, bf16[256,512]{1,0:T(8,128)(2,1)}, u32[]{:S(2)}, u32[]{:S(2)}) collective-permute-start(bf16[256,512]{1,0:T(8,128)(2,1)} %get-tuple-element.12), channel_id=1, source_target_pairs={{0,8},{8,0},{16,24},{24,16},{1,9},{9,1},{17,25},{25,17},{2,10},{10... | collective-permute-start | bytes 786440 | tf_op jit(solution)/shard_map/weights_last/ppermute | solution.py:29
  98.4 1.2 copy-start.4
  101.5 0.8 copy-start.6
  102.3 43.2 %collective-permute-start.6 = (bf16[256,512]{1,0:T(8,128)(2,1)}, bf16[256,512]{1,0:T(8,128)(2,1)}, u32[]{:S(2)}, u32[]{:S(2)}) collective-permute-start(bf16[256,512]{1,0:T(8,128)(2,1)} %get-tuple-element.17), channel_id=1, source_target_pairs={{0,16},{8,24},{16,0},{24,8},{1,17},{9,25},{17,1},{25,9},{2,18},{10... | collective-permute-start | bytes 786440 | tf_op jit(solution)/shard_map/gradient_far/ppermute | solution.py:29
  123.3 25.1 %collective-permute-start.9 = (bf16[128,256]{1,0:T(8,128)(2,1)S(1)}, bf16[128,256]{1,0:T(8,128)(2,1)}, u32[]{:S(2)}, u32[]{:S(2)}) collective-permute-start(bf16[128,256]{1,0:T(8,128)(2,1)S(1)} %add_convert_fusion), channel_id=1, source_target_pairs={{0,32},{32,0},{1,33},{33,1},{2,34},{34,2},{3,35},{35,3},{4,36},{36... | collective-permute-start | bytes 196616 | tf_op jit(solution)/shard_map/rep_sum/ppermute | solution.py:34
  130.4 1.0 copy-start
  131.4 23.0 %all-to-all-start.1 = ((bf16[8,128,512]{2,1,0:T(8,128)(2,1)}), bf16[8,128,512]{2,1,0:T(8,128)(2,1)S(1)}, u32[]{:S(2)}, u32[]{:S(2)}) async-start(bf16[8,128,512]{2,1,0:T(8,128)(2,1)} %bitcast.30), calls=%async_computation.1 | async-start | bytes 2097152 | tf_op jit(solution)/shard_map/all_to_all | solution.py:42
  145.5 1.0 copy-start.7
  146.5 1.1 copy-start.8
  146.5 1.3 copy-start.11
  146.5 1.3 copy-start.12
  147.6 1.0 copy-start.13
  147.6 1.1 copy-start.14
  150.4 4.8 %copy-start.10 = (f32[1,256,512]{2,1,0:T(8,128)}, f32[1,256,512]{2,1,0:T(8,128)S(1)}, u32[]{:S(2)}) copy-start(f32[1,256,512]{2,1,0:T(8,128)S(1)} %get-tuple-element.19) | copy-start | bytes 1572868

commit v3 on v2

--- a/solution.py
+++ b/solution.py
@@ -14,7 +14,9 @@
 NEAR = ("zp", "y")
 VMEM = pl.BlockSpec(memory_space=pltpu.VMEM)
 SMEM = pl.BlockSpec(memory_space=pltpu.SMEM)
-LAST_COST = 1 << 36
+LAST_COST = 1 << 30
+KEYS_COST = 1 << 30
+RELAY_COST = 1 << 38
 PARAMS = pltpu.CompilerParams(vmem_limit_bytes=8 * 1024 * 1024)
 
 
@@ -42,12 +44,12 @@
     return lax.all_to_all(value, axes, split_axis=0, concat_axis=0, tiled=True)
 
 
-def kernel_call(body, outs, args, flops=0, scalars=0, scratch=(), behind=()):
+def kernel_call(body, outs, args, flops=0, scalars=0, scratch=(), behind=(), read=0):
     moved = sum(a.size * a.dtype.itemsize for a in (*args, *outs))
     given = len(args)
 
     def run(*refs):
-        body(*refs[:given], *refs[given + len(behind) :])
+        body(*refs[: given + read], *refs[given + len(behind) :])
 
     args = (*args, *behind)
     return pl.pallas_call(
@@ -61,9 +63,12 @@
     )(*args)
 
 
-def prepare(far, near, rows, hidden_ref, grad_ref, tiles_ref, factor_ref):
+def copy(from_ref, to_ref):
+    to_ref[...] = from_ref[...]
+
+
+def prepare(far, near, rows, hidden_ref, grad_ref, tiles_ref, scaled_ref, factor_ref):
     tokens, features = hidden_ref.shape
-    wide = far * rows
     total = jnp.zeros((tokens, rows), jnp.float32)
     for a in range(near):
         for q in range(far):
@@ -73,9 +78,13 @@
             total = total + part * part
     factor = lax.rsqrt(jnp.sum(total, axis=1, keepdims=True) / features + NORM_EPS)
     factor_ref[...] = factor
-    scaled = (grad_ref[...].astype(jnp.float32) * factor).astype(jnp.bfloat16)
-    for a in range(near):
-        tiles_ref[a, :, wide:] = scaled
+    scaled_ref[...] = (grad_ref[...].astype(jnp.float32) * factor).astype(jnp.bfloat16)
+
+
+def join_pair(own_ref, other_ref, tiles_ref, both_ref, same_ref):
+    tokens = own_ref.shape[0]
+    both_ref[:tokens] = own_ref[...]
+    both_ref[tokens:] = other_ref[...]
 
 
 def block_of(place_ref, dh, dl, rows):
@@ -83,17 +92,29 @@
     return pl.ds(pl.multiple_of(block * rows, rows), rows)
 
 
-def gradient_blocks(rows, wide, place_ref, tiles_ref, far_ref, part_ref, keep_ref, send_ref, last_ref, part_out):
+def gradient_blocks(rows, place_ref, tiles_ref, part_ref, g0, g1, g2, g3, *refs):
+    keep_ref, send_ref, part_out, grad_ref, sems = refs[-5:]
+    tokens = g0.shape[0] // 2
+    copies = []
+    for turn, piece in enumerate((g0, g1, g2, g3)):
+        for j in range(2):
+            source = (place_ref[2] ^ j) * 4 + ((place_ref[3] + 4 - turn) & 3)
+            where = pl.ds(pl.multiple_of(source * tokens, tokens), tokens)
+            copies.append(
+                pltpu.make_async_copy(piece.at[j * tokens : (j + 1) * tokens], grad_ref.at[where], sems.at[2 * turn + j])
+            )
+            copies[-1].start()
+    part_out[...] = part_ref[...]
+    for copy_in in copies:
+        copy_in.wait()
     for dl in (1, 0):
         for dh in range(2):
             left = tiles_ref[:, block_of(place_ref, dh, dl, rows)]
-            value = lax.dot_general(left, tiles_ref[:, wide:], (((0,), (0,)), ((), ())), preferred_element_type=jnp.float32)
+            value = lax.dot_general(left, grad_ref[...], (((0,), (0,)), ((), ())), preferred_element_type=jnp.float32)
             if dl:
                 send_ref[dh] = value.astype(jnp.bfloat16)
             else:
                 keep_ref[dh] = value
-    last_ref[...] = far_ref[...]
-    part_out[...] = part_ref[...]
 
 
 def first_sum(keep_ref, got_ref, mine_ref, send_ref):
@@ -105,11 +126,18 @@
     grad_ref[...] = mine_ref[...] + got_ref[...].astype(jnp.float32)
 
 
-def key_sum(partial_ref, factor_ref, keys_ref):
-    total = partial_ref[0].astype(jnp.float32)
-    for i in range(1, partial_ref.shape[0]):
-        total = total + partial_ref[i].astype(jnp.float32)
-    keys_ref[...] = (total * factor_ref[...]).astype(jnp.bfloat16)
+def key_halves(place_ref, partial_ref, mine_ref, send_ref):
+    tokens = mine_ref.shape[0]
+    for turn, out_ref in ((0, mine_ref), (1, send_ref)):
+        where = pl.ds(pl.multiple_of((place_ref[2] ^ turn) * tokens, tokens), tokens)
+        total = partial_ref[0, where, :].astype(jnp.float32)
+        for y in range(1, partial_ref.shape[0]):
+            total = total + partial_ref[y, where, :].astype(jnp.float32)
+        out_ref[...] = total.astype(out_ref.dtype)
+
+
+def key_sum(mine_ref, got_ref, factor_ref, keys_ref):
+    keys_ref[...] = ((mine_ref[...] + got_ref[...].astype(jnp.float32)) * factor_ref[...]).astype(jnp.bfloat16)
 
 
 def key_partials(rows, multiplier, place_ref, tiles_ref, *refs):
@@ -120,7 +148,12 @@
             right = refs[2 * dh + dl][...]
             value = jnp.dot(left, right, preferred_element_type=jnp.float32)
             total = value if total is None else total + value
-    refs[4][...] = (total * multiplier).astype(jnp.bfloat16)
+    total = (total * multiplier).astype(jnp.bfloat16)
+    out_ref = refs[4]
+    tokens = out_ref.shape[1] // 2
+    for zp in range(2):
+        for y in range(4):
+            out_ref[y, zp * tokens : (zp + 1) * tokens, :] = total[(zp * 4 + y) * tokens : (zp * 4 + y + 1) * tokens]
 
 
 def on_device(
@@ -134,17 +167,29 @@
     near = lax.axis_size(NEAR)
     far = lax.axis_size("zq")
     far_index = lax.axis_index("zq")
-    place = jnp.stack([far_index >> 1, far_index & 1, lax.axis_index("zp")]).astype(jnp.int32)
+    place = jnp.stack([far_index >> 1, far_index & 1, lax.axis_index("zp"), lax.axis_index("y")]).astype(jnp.int32)
     shape = jax.ShapeDtypeStruct
     f32, b16 = jnp.float32, jnp.bfloat16
 
     wide = far * rows
-    tiles, factor = kernel_call(
+    tiles, scaled, factor = kernel_call(
         lambda *refs: prepare(far, near, rows, *refs),
-        [shape((near, tokens, wide + key_width), b16), shape((tokens, 1), f32)],
+        [shape((near, tokens, wide), b16), shape(key_grad.shape, b16), shape((tokens, 1), f32)],
         (hidden_in, key_grad),
     )
-    tiles = exchange(tiles, NEAR).reshape(near * tokens, wide + key_width)
+    other = flip(scaled, "zp", name="cotangent_pair")
+    anywhere = pl.BlockSpec(memory_space=pl.ANY)
+    both, tiles = pl.pallas_call(
+        join_pair,
+        out_shape=[shape((2 * tokens, key_width), b16), shape(tiles.shape, b16)],
+        in_specs=[VMEM, VMEM, anywhere],
+        out_specs=[VMEM, anywhere],
+        input_output_aliases={2: 1},
+        compiler_params=PARAMS,
+    )(scaled, other, tiles)
+    tiles = exchange(tiles, NEAR).reshape(near * tokens, wide)
+    with jax.named_scope("cotangent_y"):
+        turned = [lax.ppermute(both, "y", [(i, (i + k) % 4) for i in range(4)]) for k in (1, 2, 3)]
 
     frag_width = anchor.shape[1]
     col_offset = fragment[0] * frag_width
@@ -155,31 +200,45 @@
     part = add(mine, flip(theirs, "c"))
 
     part = add(part, flip(part, "x", 1))
+    part = add(part, flip(part, "x", 2))
 
     own_gain = lax.dynamic_slice_in_dim(gain, lax.axis_index(FSDP) * rows, rows, 0)[:, None]
     weight_low = (weight_now * own_gain).astype(b16)
     near_low = swap(weight_low, 1, "weights_near")
     far_low = swap(weight_low, 2, "weights_far")
+    (relayed,) = kernel_call(copy, [shape(far_low.shape, b16)], (far_low,), RELAY_COST)
+    last_low = swap(relayed, 1, "weights_last")
 
     flops = 2 * near * tokens * far * rows * key_width
-    keep, send, last_low, part = kernel_call(
-        lambda *refs: gradient_blocks(rows, wide, *refs),
-        [shape((2, rows, key_width), f32), shape((2, rows, key_width), b16), shape(far_low.shape, b16), shape(part.shape, b16)],
-        (place, tiles, far_low, part),
+    keep, send, part = kernel_call(
+        lambda *refs: gradient_blocks(rows, *refs),
+        [shape((2, rows, key_width), f32), shape((2, rows, key_width), b16), shape(part.shape, b16)],
+        (place, tiles, part),
         flops,
         1,
-        behind=(near_low,),
+        [pltpu.VMEM((near * tokens, key_width), b16), pltpu.SemaphoreType.DMA((8,))],
+        behind=(both, *turned, near_low, last_low),
+        read=4,
     )
     got = swap(send, 1, "gradient_near")
-    last_low = swap(last_low, 1, "weights_last")
-    part = add(part, flip(part, "x", 2))
-    part = add(part, flip(part, "zh"))
-    other = flip(part, "c")
+    (partial_keys,) = kernel_call(
+        lambda *refs: key_partials(rows, multiplier, *refs),
+        [shape((near // 2, 2 * tokens, key_width), b16)],
+        (place, tiles, weight_low, near_low, far_low, last_low),
+        KEYS_COST,
+        1,
+        behind=(send,),
+    )
+    mine, rest = kernel_call(
+        first_sum,
+        [shape((rows, key_width), f32), shape((rows, key_width), b16)],
+        (keep, got),
+        behind=(partial_keys,),
+    )
+    last = swap(rest, 2, "gradient_far")
+    part = add(part, flip(part, "zh", name="rep_far"))
+    other = flip(part, "c", name="rep_back")
     summed_cols = jnp.where(core == 0, jnp.concatenate([part, other]), jnp.concatenate([other, part])).astype(f32)
-    mine, rest = kernel_call(
-        first_sum, [shape((rows, key_width), f32), shape((rows, key_width), b16)], (keep, got)
-    )
-    last = swap(rest, 2, "gradient_far")
     (grad_sum,) = kernel_call(second_sum, [shape((rows, key_width), f32)], (mine, last), LAST_COST)
     gradient = grad_sum * (multiplier * own_gain)
     moment_next = 0.9 * first_moment[0] + 0.1 * gradient
@@ -187,15 +246,15 @@
     inner = weight_now - INNER_RATE * (
         moment_next / (jnp.sqrt(second_next) + ADAM_EPS) + 0.1 * weight_now
     )
-    (partial_keys,) = kernel_call(
-        lambda *refs: key_partials(rows, multiplier, *refs),
-        [shape((near * tokens, key_width), b16)],
-        (place, tiles, weight_low, near_low, far_low, last_low),
-        flops,
-        1,
-    )
-    partial_keys = exchange(partial_keys.reshape(near, tokens, key_width), NEAR)
-    (keys,) = kernel_call(key_sum, [shape((tokens, key_width), b16)], (partial_keys, factor))
+    partial_keys = exchange(partial_keys, "y")
+    own_keys, pair_keys = kernel_call(
+        key_halves,
+        [shape((tokens, key_width), f32), shape((tokens, key_width), b16)],
+        (place, partial_keys),
+        scalars=1,
+    )
+    pair_keys = flip(pair_keys, "zp", name="keys_pair")
+    (keys,) = kernel_call(key_sum, [shape((tokens, key_width), b16)], (own_keys, pair_keys, factor))
 
     replicas = lax.axis_size(REP)
     fresh, momentum_out = outer_step(summed_cols / replicas, anchor, momentum)

time: 156 us -> 150 us (0.962)
  starting transfers between devices: 91.6 us -> 71.5 us
  waiting for transfers between devices: 34.7 us -> 54 us
  local copies, waits for them, and re-layouts: 12 us -> 4 us
  Pallas kernels: 9.37 us -> 12.2 us
    ppermute x5, starting transfers between devices: 49.9 us -> 19.6 us  [swap(): return lax.ppermute(value, 'zq', [(i, i ^ bit) for i in range(4)])]
    ppermute x0 -> x3, waiting for transfers between devices: none -> 16 us  [on_device(): lax.ppermute(both, 'y', [(i, (i + k) % 4) for i in range(4)])]
    ppermute x0 -> x3, starting transfers between devices: none -> 10.1 us  [on_device(): lax.ppermute(both, 'y', [(i, (i + k) % 4) for i in range(4)])]
    unnamed x33 -> x21, local copies, waits for them, and re-layouts: 10.4 us -> 3.02 us
    ppermute x5, waiting for transfers between devices: 24.7 us -> 31.7 us  [swap(): return lax.ppermute(value, 'zq', [(i, i ^ bit) for i in range(4)])]
    all_to_all x2, waiting for transfers between devices: 5.9 us -> 2.99 us  [exchange(): return lax.all_to_all(value, axes, split_axis=0, concat_axis=0, tiled=True)]
    ppermute x5 -> x7, starting transfers between devices: 31.3 us -> 33.8 us  [flip(): lax.ppermute(value, axis, [(i, i ^ bit) for i in range(lax.axis_size(axis...]
    all_to_all x2, starting transfers between devices: 10.3 us -> 8 us  [exchange(): return lax.all_to_all(value, axes, split_axis=0, concat_axis=0, tiled=True)]
  transfers between devices with their start and end apart: 12 -> 17, of which waited for: 8 -> 6; matrix products, arithmetic and copies ran while one was open for 5% -> 4% of each run, Pallas kernels for 3% -> 5%
where the time goes in v3:
time: 150 us; the launch traced here: 149 us
  starting transfers between devices  71.5 us (48%)
  waiting for transfers between devices  54 us (36%)
  Pallas kernels  12.2 us (8%)
  other arithmetic  5.94 us (4%)
  local copies, waits for them, and re-layouts  4 us (3%)
  between operations  1.67 us (1%)
    ppermute x7, starting transfers between devices, flip(): lax.ppermute(value, axis, [(i, i ^ bit) for i in range(lax.axis_size(axis...  33.8 us
    ppermute x5, waiting for transfers between devices, swap(): return lax.ppermute(value, 'zq', [(i, i ^ bit) for i in range(4)])  31.7 us
    ppermute x5, starting transfers between devices, swap(): return lax.ppermute(value, 'zq', [(i, i ^ bit) for i in range(4)])  19.6 us
    ppermute x3, waiting for transfers between devices, on_device(): lax.ppermute(both, 'y', [(i, (i + k) % 4) for i in range(4)])  16 us
    pallas_call x8, Pallas kernels, kernel_call(): pl.pallas_call(run, out_shape=outs, in_specs=[SMEM] * scalars + [VMEM] *...  11.5 us
    ppermute x3, starting transfers between devices, on_device(): lax.ppermute(both, 'y', [(i, (i + k) % 4) for i in range(4)])  10.1 us
    all_to_all x2, starting transfers between devices, exchange(): return lax.all_to_all(value, axes, split_axis=0, concat_axis=0, tiled=True)  8 us
    ppermute x7, waiting for transfers between devices, flip(): lax.ppermute(value, axis, [(i, i ^ bit) for i in range(lax.axis_size(axis...  3.41 us
  transfers between devices with their start and end apart: 17, of which 6 were waited for; matrix products, arithmetic and copies ran while one was open for 4% of the time, Pallas kernels for 5%

profile of v3, /device:TPU:1, one launch (start us, length us, event | category | flops | bytes accessed | tf_op | source)
XLA Modules:
  0.0 149.3 jit_solution(4883640411614723809)
XLA Ops:
  1.3 1.0 dynamic-slice_convert_fusion
  2.3 8.8 %collective-permute-start.4 = (bf16[128,256]{1,0:T(8,128)(2,1)S(1)}, bf16[128,256]{1,0:T(8,128)(2,1)S(1)}, u32[]{:S(2)}, u32[]{:S(2)}) collective-permute-start(bf16[128,256]{1,0:T(8,128)(2,1)S(1)} %dynamic-slice_bitcast_fusion), channel_id=1, source_target_pairs={{0,32},{32,0},{1,33},{33,1},{2,34},{34,2},{3,35},{35,3},{4,36},{36... | collective-permute-start | bytes 196616 | tf_op jit(solution)/shard_map/rep_sum/ppermute | solution.py:36
  11.1 0.0 copy-start
  11.1 1.6 %copy-done = bf16[128,8192]{1,0:T(8,128)(2,1)S(1)} copy-done((bf16[128,8192]{1,0:T(8,128)(2,1)S(1)}, bf16[128,8192]{1,0:T(8,128)(2,1)}, u32[]{:S(2)}) %copy-start) | copy-done | bytes 2097176
  12.7 0.9 copy-done.1
  13.6 1.6 %shard_map.112 = (bf16[8,128,1024]{2,1,0:T(8,128)(2,1)}, bf16[128,512]{1,0:T(8,128)(2,1)S(1)}, f32[128,1]{1,0:T(8,128)S(1)}) custom-call(bf16[128,8192]{1,0:T(8,128)(2,1)S(1)} %copy-done, bf16[128,512]{1,0:T(8,128)(2,1)S(1)} %copy-done.1), custom_call_target="tpu_custom_call" | custom-call | bytes 4456960 | tf_op jit(solution)/shard_map/pallas_call | solution.py:55
  15.2 1.9 %collective-permute-start = (bf16[128,512]{1,0:T(8,128)(2,1)S(1)}, bf16[128,512]{1,0:T(8,128)(2,1)S(1)}, u32[]{:S(2)}, u32[]{:S(2)}) collective-permute-start(bf16[128,512]{1,0:T(8,128)(2,1)S(1)} %get-tuple-element.15.own_ref), channel_id=1, source_target_pairs={{0,4},{4,0},{1,5},{5,1},{2,6},{6,2},{3,7},{7,3},{8,12},{12,8},{9,1... | collective-permute-start | bytes 393224 | tf_op jit(solution)/shard_map/cotangent_pair/ppermute | solution.py:36
  17.1 1.4 broadcast_multiply_fusion
  18.5 0.0 collective-permute-done.4
  18.5 1.9 %collective-permute-start.5 = (bf16[128,256]{1,0:T(8,128)(2,1)S(1)}, bf16[128,256]{1,0:T(8,128)(2,1)S(1)}, u32[]{:S(2)}, u32[]{:S(2)}) collective-permute-start(bf16[128,256]{1,0:T(8,128)(2,1)S(1)} %fusion.8), channel_id=1, source_target_pairs={{0,64},{64,0},{128,192},{192,128},{1,65},{65,1},{129,193},{193,129... | collective-permute-start | bytes 196616 | tf_op jit(solution)/shard_map/rep_sum/ppermute | solution.py:36
  20.4 0.0 copy-done.2
  20.4 0.8 fusion.7.refs_2_
  21.2 6.3 %collective-permute-start.2 = (bf16[256,512]{1,0:T(8,128)(2,1)}, bf16[256,512]{1,0:T(8,128)(2,1)S(1)}, u32[]{:S(2)}, u32[]{:S(2)}) collective-permute-start(bf16[256,512]{1,0:T(8,128)(2,1)} %fusion.7.refs_2_), channel_id=1, source_target_pairs={{0,16},{8,24},{16,0},{24,8},{1,17},{9,25},{17,1},{25,9},{2,18},{10... | collective-permute-start | bytes 786440 | tf_op jit(solution)/shard_map/weights_far/ppermute | solution.py:31
  27.5 4.9 %collective-permute-start.1 = (bf16[256,512]{1,0:T(8,128)(2,1)}, bf16[256,512]{1,0:T(8,128)(2,1)}, u32[]{:S(2)}, u32[]{:S(2)}) collective-permute-start(bf16[256,512]{1,0:T(8,128)(2,1)} %fusion.7.refs_2_), channel_id=1, source_target_pairs={{0,8},{8,0},{16,24},{24,16},{1,9},{9,1},{17,25},{25,17},{2,10},{10... | collective-permute-start | bytes 786440 | tf_op jit(solution)/shard_map/weights_near/ppermute | solution.py:31
  32.4 0.0 collective-permute-done.other_ref
  32.4 0.7 shard_map.113
  33.2 4.6 %collective-permute-start.9 = (bf16[256,512]{1,0:T(8,128)(2,1)}, bf16[256,512]{1,0:T(8,128)(2,1)}, u32[]{:S(2)}, u32[]{:S(2)}) collective-permute-start(bf16[256,512]{1,0:T(8,128)(2,1)} %get-tuple-element.18.refs_3_), channel_id=1, source_target_pairs={{0,3},{1,0},{2,1},{3,2},{4,7},{5,4},{6,5},{7,6},{8,11},{9,8},{10,9... | collective-permute-start | bytes 786440 | tf_op jit(solution)/shard_map/cotangent_y/ppermute | solution.py:192
  37.8 2.3 %collective-permute-start.8 = (bf16[256,512]{1,0:T(8,128)(2,1)}, bf16[256,512]{1,0:T(8,128)(2,1)}, u32[]{:S(2)}, u32[]{:S(2)}) collective-permute-start(bf16[256,512]{1,0:T(8,128)(2,1)} %get-tuple-element.18.refs_3_), channel_id=1, source_target_pairs={{0,2},{1,3},{2,0},{3,1},{4,6},{5,7},{6,4},{7,5},{8,10},{9,11},{10,... | collective-permute-start | bytes 786440 | tf_op jit(solution)/shard_map/cotangent_y/ppermute | solution.py:192
  40.1 4.3 %all-to-all-start = ((bf16[8,128,1024]{2,1,0:T(8,128)(2,1)}), bf16[8,128,1024]{2,1,0:T(8,128)(2,1)}, u32[]{:S(2)}, u32[]{:S(2)}) async-start(bf16[8,128,1024]{2,1,0:T(8,128)(2,1)} %get-tuple-element.17), calls=%async_computation | async-start | bytes 4194304 | tf_op jit(solution)/shard_map/all_to_all | solution.py:44
  44.4 0.0 collective-permute-done.5
  44.4 3.2 %collective-permute-start.7 = (bf16[256,512]{1,0:T(8,128)(2,1)}, bf16[256,512]{1,0:T(8,128)(2,1)}, u32[]{:S(2)}, u32[]{:S(2)}) collective-permute-start(bf16[256,512]{1,0:T(8,128)(2,1)} %get-tuple-element.18.refs_3_), channel_id=1, source_target_pairs={{0,1},{1,2},{2,3},{3,0},{4,5},{5,6},{6,7},{7,4},{8,9},{9,10},{10,1... | collective-permute-start | bytes 786440 | tf_op jit(solution)/shard_map/cotangent_y/ppermute | solution.py:192
  47.7 0.6 add_convert_fusion.2
  48.3 3.8 %collective-permute-done.2.refs_0_.refs_4_ = bf16[256,512]{1,0:T(8,128)(2,1)S(1)} collective-permute-done((bf16[256,512]{1,0:T(8,128)(2,1)}, bf16[256,512]{1,0:T(8,128)(2,1)S(1)}, u32[]{:S(2)}, u32[]{:S(2)}) %collective-permute-start.2) | collective-permute-done | bytes 262176 | tf_op jit(solution)/shard_map/weights_far/ppermute | solution.py:31
  52.1 3.4 %collective-permute-start.6 = (bf16[128,256]{1,0:T(8,128)(2,1)}, bf16[128,256]{1,0:T(8,128)(2,1)}, u32[]{:S(2)}, u32[]{:S(2)}) collective-permute-start(bf16[128,256]{1,0:T(8,128)(2,1)} %add_convert_fusion.2), channel_id=1, source_target_pairs={{0,128},{64,192},{128,0},{192,64},{1,129},{65,193},{129,1},{193,65... | collective-permute-start | bytes 196616 | tf_op jit(solution)/shard_map/rep_sum/ppermute | solution.py:36
  55.5 3.4 %collective-permute-done.6 = bf16[128,256]{1,0:T(8,128)(2,1)} collective-permute-done((bf16[128,256]{1,0:T(8,128)(2,1)}, bf16[128,256]{1,0:T(8,128)(2,1)}, u32[]{:S(2)}, u32[]{:S(2)}) %collective-permute-start.6) | collective-permute-done | bytes 65568 | tf_op jit(solution)/shard_map/rep_sum/ppermute | solution.py:36
  58.9 1.9 %collective-permute-start.3 = (bf16[256,512]{1,0:T(8,128)(2,1)S(1)}, bf16[256,512]{1,0:T(8,128)(2,1)S(1)}, u32[]{:S(2)}, u32[]{:S(2)}) collective-permute-start(bf16[256,512]{1,0:T(8,128)(2,1)S(1)} %shard_map.114), channel_id=1, source_target_pairs={{0,8},{8,0},{16,24},{24,16},{1,9},{9,1},{17,25},{25,17},{2,10},{10... | collective-permute-start | bytes 786440 | tf_op jit(solution)/shard_map/weights_last/ppermute | solution.py:31
  60.8 0.1 pad_add_fusion.refs_0_
  60.9 0.9 add_convert_fusion.1.refs_2_
  61.8 0.0 collective-permute-done.1.refs_7_.refs_3_
  61.8 0.0 collective-permute-done.9.refs_6_
  61.8 0.0 collective-permute-done.8.refs_5_
  61.9 16.0 %collective-permute-done.7.refs_4_ = bf16[256,512]{1,0:T(8,128)(2,1)} collective-permute-done((bf16[256,512]{1,0:T(8,128)(2,1)}, bf16[256,512]{1,0:T(8,128)(2,1)}, u32[]{:S(2)}, u32[]{:S(2)}) %collective-permute-start.7) | collective-permute-done | bytes 262176 | tf_op jit(solution)/shard_map/cotangent_y/ppermute | solution.py:192
  77.8 0.0 collective-permute-done.3.refs_8_.refs_5_
  77.8 3.0 %all-to-all-done = bf16[8,128,1024]{2,1,0:T(8,128)(2,1)} async-done(((bf16[8,128,1024]{2,1,0:T(8,128)(2,1)}), bf16[8,128,1024]{2,1,0:T(8,128)(2,1)}, u32[]{:S(2)}, u32[]{:S(2)}) %all-to-all-start) | async-done | bytes 2097184 | tf_op jit(solution)/shard_map/all_to_all | solution.py:44
  80.8 4.3 %shard_map.115 = (f32[2,256,512]{2,1,0:T(8,128)S(1)}, bf16[2,256,512]{2,1,0:T(8,128)(2,1)S(1)}, bf16[128,256]{1,0:T(8,128)(2,1)S(1)}) custom-call(s32[4]{0:T(128)S(1)} %pad_add_fusion.refs_0_, bf16[1024,1024]{1,0:T(8,128)(2,1)} %bitcast.4.refs_1_, bf16[128,256]{1,0:T(8,128)(2,1)S(1)} %add_convert_fusion.1.refs_2_, ...), custom_call_target="tpu_custom_call" | custom-call | flops 1073741824 | bytes 3801104 | tf_op jit(solution)/shard_map/pallas_call | solution.py:55
  85.1 1.9 %collective-permute-start.11 = (bf16[2,256,512]{2,1,0:T(8,128)(2,1)S(1)}, bf16[2,256,512]{2,1,0:T(8,128)(2,1)S(1)}, u32[]{:S(2)}, u32[]{:S(2)}) collective-permute-start(bf16[2,256,512]{2,1,0:T(8,128)(2,1)S(1)} %get-tuple-element.19.refs_6_), channel_id=1, source_target_pairs={{0,8},{8,0},{16,24},{24,16},{1,9},{9,1},{17,25},{25,17},{2,10},{10... | collective-permute-start | bytes 1572872 | tf_op jit(solution)/shard_map/gradient_near/ppermute | solution.py:31
  87.0 3.9 %shard_map.116.refs_2_ = bf16[4,256,512]{2,1,0:T(8,128)(2,1)} custom-call(s32[4]{0:T(128)S(1)} %pad_add_fusion.refs_0_, bf16[1024,1024]{1,0:T(8,128)(2,1)} %bitcast.4.refs_1_, bf16[256,512]{1,0:T(8,128)(2,1)} %fusion.7.refs_2_, bf16[256,512]{1,0:T(8,128)(2,1)} %collective-permute-done.1.refs_7_.refs_3_, ...), custom_call_target="tpu_custom_call" | custom-call | flops 1073741824 | bytes 4194320 | tf_op jit(solution)/shard_map/pallas_call | solution.py:55
  91.0 3.7 %all-to-all-start.1 = ((bf16[4,256,512]{2,1,0:T(8,128)(2,1)}), bf16[4,256,512]{2,1,0:T(8,128)(2,1)S(1)}, u32[]{:S(2)}, u32[]{:S(2)}) async-start(bf16[4,256,512]{2,1,0:T(8,128)(2,1)} %shard_map.116.refs_2_), calls=%async_computation.1 | async-start | bytes 2097152 | tf_op jit(solution)/shard_map/all_to_all | solution.py:44
  94.6 13.0 %collective-permute-start.13 = (bf16[128,256]{1,0:T(8,128)(2,1)S(1)}, bf16[128,256]{1,0:T(8,128)(2,1)}, u32[]{:S(2)}, u32[]{:S(2)}) collective-permute-start(bf16[128,256]{1,0:T(8,128)(2,1)S(1)} %get-tuple-element.26), channel_id=1, source_target_pairs={{0,256},{256,0},{1,257},{257,1},{2,258},{258,2},{3,259},{259,3},{4... | collective-permute-start | bytes 196616 | tf_op jit(solution)/shard_map/rep_far/ppermute | solution.py:36
  107.7 9.5 %collective-permute-done.11.refs_1_ = bf16[2,256,512]{2,1,0:T(8,128)(2,1)S(1)} collective-permute-done((bf16[2,256,512]{2,1,0:T(8,128)(2,1)S(1)}, bf16[2,256,512]{2,1,0:T(8,128)(2,1)S(1)}, u32[]{:S(2)}, u32[]{:S(2)}) %collective-permute-start.11) | collective-permute-done | bytes 524320 | tf_op jit(solution)/shard_map/gradient_near/ppermute | solution.py:31
  117.1 0.1 shard_map.119
  117.2 4.6 %collective-permute-start.12 = (bf16[256,512]{1,0:T(8,128)(2,1)S(1)}, bf16[256,512]{1,0:T(8,128)(2,1)S(1)}, u32[]{:S(2)}, u32[]{:S(2)}) collective-permute-start(bf16[256,512]{1,0:T(8,128)(2,1)S(1)} %get-tuple-element.25), channel_id=1, source_target_pairs={{0,16},{8,24},{16,0},{24,8},{1,17},{9,25},{17,1},{25,9},{2,18},{10... | collective-permute-start | bytes 786440 | tf_op jit(solution)/shard_map/gradient_far/ppermute | solution.py:31
  121.9 0.0 collective-permute-done.13
  121.9 0.9 add_convert_fusion
  122.7 2.6 %collective-permute-start.14 = (bf16[128,256]{1,0:T(8,128)(2,1)S(1)}, bf16[128,256]{1,0:T(8,128)(2,1)S(1)}, u32[]{:S(2)}, u32[]{:S(2)}) collective-permute-start(bf16[128,256]{1,0:T(8,128)(2,1)S(1)} %add_convert_fusion), channel_id=1, source_target_pairs={{0,32},{32,0},{1,33},{33,1},{2,34},{34,2},{3,35},{35,3},{4,36},{36... | collective-permute-start | bytes 196616 | tf_op jit(solution)/shard_map/rep_back/ppermute | solution.py:36
  125.4 0.0 all-to-all-done.1.refs_1_
  125.4 0.7 shard_map.117
  126.1 0.0 copy-start.3
  126.1 0.0 copy-start.5
  126.1 0.0 copy-start.6
  126.1 0.0 copy-start.9
  126.1 2.1 %collective-permute-start.10 = (bf16[128,512]{1,0:T(8,128)(2,1)S(1)}, bf16[128,512]{1,0:T(8,128)(2,1)S(1)}, u32[]{:S(2)}, u32[]{:S(2)}) collective-permute-start(bf16[128,512]{1,0:T(8,128)(2,1)S(1)} %get-tuple-element.21), channel_id=1, source_target_pairs={{0,4},{4,0},{1,5},{5,1},{2,6},{6,2},{3,7},{7,3},{8,12},{12,8},{9,1... | collective-permute-start | bytes 393224 | tf_op jit(solution)/shard_map/keys_pair/ppermute | solution.py:36
  128.2 18.4 %collective-permute-done.12.refs_1_ = bf16[256,512]{1,0:T(8,128)(2,1)S(1)} collective-permute-done((bf16[256,512]{1,0:T(8,128)(2,1)S(1)}, bf16[256,512]{1,0:T(8,128)(2,1)S(1)}, u32[]{:S(2)}, u32[]{:S(2)}) %collective-permute-start.12) | collective-permute-done | bytes 262176 | tf_op jit(solution)/shard_map/gradient_far/ppermute | solution.py:31
  146.6 0.0 copy-start.7
  146.6 0.0 copy-start.8
  146.7 0.0 copy-done.3
  146.7 0.0 copy-done.5
  146.7 0.5 fusion.6
  147.2 0.0 collective-permute-done.14
  147.2 0.4 copy-done.7
  147.6 0.1 copy-done.8
  147.7 0.8 bitcast_dynamic-update-slice_fusion
  148.5 0.0 collective-permute-done.10.refs_1_
  148.5 0.8 shard_map.118
  (11 shorter events, 0.1 us)
Async XLA Ops:
  2.3 16.2 %collective-permute-start.4 = (bf16[128,256]{1,0:T(8,128)(2,1)S(1)}, bf16[128,256]{1,0:T(8,128)(2,1)S(1)}, u32[]{:S(2)}, u32[]{:S(2)}) collective-permute-start(bf16[128,256]{1,0:T(8,128)(2,1)S(1)} %dynamic-slice_bitcast_fusion), channel_id=1, source_target_pairs={{0,32},{32,0},{1,33},{33,1},{2,34},{34,2},{3,35},{35,3},{4,36},{36... | collective-permute-start | bytes 196616 | tf_op jit(solution)/shard_map/rep_sum/ppermute | solution.py:36
  11.1 1.6 %copy-start = (bf16[128,8192]{1,0:T(8,128)(2,1)S(1)}, bf16[128,8192]{1,0:T(8,128)(2,1)}, u32[]{:S(2)}) copy-start(bf16[128,8192]{1,0:T(8,128)(2,1)} %refs_0_.1) | copy-start | bytes 6291460
  12.7 0.9 copy-start.1
  13.6 6.9 %copy-start.2 = (f32[1,256,512]{2,1,0:T(8,128)S(1)}, f32[1,256,512]{2,1,0:T(8,128)}, u32[]{:S(2)}) copy-start(f32[1,256,512]{2,1,0:T(8,128)} %param.12) | copy-start | bytes 1572868
  15.2 17.2 %collective-permute-start = (bf16[128,512]{1,0:T(8,128)(2,1)S(1)}, bf16[128,512]{1,0:T(8,128)(2,1)S(1)}, u32[]{:S(2)}, u32[]{:S(2)}) collective-permute-start(bf16[128,512]{1,0:T(8,128)(2,1)S(1)} %get-tuple-element.15.own_ref), channel_id=1, source_target_pairs={{0,4},{4,0},{1,5},{5,1},{2,6},{6,2},{3,7},{7,3},{8,12},{12,8},{9,1... | collective-permute-start | bytes 393224 | tf_op jit(solution)/shard_map/cotangent_pair/ppermute | solution.py:36
  18.5 25.9 %collective-permute-start.5 = (bf16[128,256]{1,0:T(8,128)(2,1)S(1)}, bf16[128,256]{1,0:T(8,128)(2,1)S(1)}, u32[]{:S(2)}, u32[]{:S(2)}) collective-permute-start(bf16[128,256]{1,0:T(8,128)(2,1)S(1)} %fusion.8), channel_id=1, source_target_pairs={{0,64},{64,0},{128,192},{192,128},{1,65},{65,1},{129,193},{193,129... | collective-permute-start | bytes 196616 | tf_op jit(solution)/shard_map/rep_sum/ppermute | solution.py:36
  21.2 30.9 %collective-permute-start.2 = (bf16[256,512]{1,0:T(8,128)(2,1)}, bf16[256,512]{1,0:T(8,128)(2,1)S(1)}, u32[]{:S(2)}, u32[]{:S(2)}) collective-permute-start(bf16[256,512]{1,0:T(8,128)(2,1)} %fusion.7.refs_2_), channel_id=1, source_target_pairs={{0,16},{8,24},{16,0},{24,8},{1,17},{9,25},{17,1},{25,9},{2,18},{10... | collective-permute-start | bytes 786440 | tf_op jit(solution)/shard_map/weights_far/ppermute | solution.py:31
  27.5 34.3 %collective-permute-start.1 = (bf16[256,512]{1,0:T(8,128)(2,1)}, bf16[256,512]{1,0:T(8,128)(2,1)}, u32[]{:S(2)}, u32[]{:S(2)}) collective-permute-start(bf16[256,512]{1,0:T(8,128)(2,1)} %fusion.7.refs_2_), channel_id=1, source_target_pairs={{0,8},{8,0},{16,24},{24,16},{1,9},{9,1},{17,25},{25,17},{2,10},{10... | collective-permute-start | bytes 786440 | tf_op jit(solution)/shard_map/weights_near/ppermute | solution.py:31
  33.2 28.7 %collective-permute-start.9 = (bf16[256,512]{1,0:T(8,128)(2,1)}, bf16[256,512]{1,0:T(8,128)(2,1)}, u32[]{:S(2)}, u32[]{:S(2)}) collective-permute-start(bf16[256,512]{1,0:T(8,128)(2,1)} %get-tuple-element.18.refs_3_), channel_id=1, source_target_pairs={{0,3},{1,0},{2,1},{3,2},{4,7},{5,4},{6,5},{7,6},{8,11},{9,8},{10,9... | collective-permute-start | bytes 786440 | tf_op jit(solution)/shard_map/cotangent_y/ppermute | solution.py:192
  37.8 24.1 %collective-permute-start.8 = (bf16[256,512]{1,0:T(8,128)(2,1)}, bf16[256,512]{1,0:T(8,128)(2,1)}, u32[]{:S(2)}, u32[]{:S(2)}) collective-permute-start(bf16[256,512]{1,0:T(8,128)(2,1)} %get-tuple-element.18.refs_3_), channel_id=1, source_target_pairs={{0,2},{1,3},{2,0},{3,1},{4,6},{5,7},{6,4},{7,5},{8,10},{9,11},{10,... | collective-permute-start | bytes 786440 | tf_op jit(solution)/shard_map/cotangent_y/ppermute | solution.py:192
  40.1 40.8 %all-to-all-start = ((bf16[8,128,1024]{2,1,0:T(8,128)(2,1)}), bf16[8,128,1024]{2,1,0:T(8,128)(2,1)}, u32[]{:S(2)}, u32[]{:S(2)}) async-start(bf16[8,128,1024]{2,1,0:T(8,128)(2,1)} %get-tuple-element.17), calls=%async_computation | async-start | bytes 4194304 | tf_op jit(solution)/shard_map/all_to_all | solution.py:44
  44.4 33.4 %collective-permute-start.7 = (bf16[256,512]{1,0:T(8,128)(2,1)}, bf16[256,512]{1,0:T(8,128)(2,1)}, u32[]{:S(2)}, u32[]{:S(2)}) collective-permute-start(bf16[256,512]{1,0:T(8,128)(2,1)} %get-tuple-element.18.refs_3_), channel_id=1, source_target_pairs={{0,1},{1,2},{2,3},{3,0},{4,5},{5,6},{6,7},{7,4},{8,9},{9,10},{10,1... | collective-permute-start | bytes 786440 | tf_op jit(solution)/shard_map/cotangent_y/ppermute | solution.py:192
  52.1 6.8 %collective-permute-start.6 = (bf16[128,256]{1,0:T(8,128)(2,1)}, bf16[128,256]{1,0:T(8,128)(2,1)}, u32[]{:S(2)}, u32[]{:S(2)}) collective-permute-start(bf16[128,256]{1,0:T(8,128)(2,1)} %add_convert_fusion.2), channel_id=1, source_target_pairs={{0,128},{64,192},{128,0},{192,64},{1,129},{65,193},{129,1},{193,65... | collective-permute-start | bytes 196616 | tf_op jit(solution)/shard_map/rep_sum/ppermute | solution.py:36
  58.9 18.9 %collective-permute-start.3 = (bf16[256,512]{1,0:T(8,128)(2,1)S(1)}, bf16[256,512]{1,0:T(8,128)(2,1)S(1)}, u32[]{:S(2)}, u32[]{:S(2)}) collective-permute-start(bf16[256,512]{1,0:T(8,128)(2,1)S(1)} %shard_map.114), channel_id=1, source_target_pairs={{0,8},{8,0},{16,24},{24,16},{1,9},{9,1},{17,25},{25,17},{2,10},{10... | collective-permute-start | bytes 786440 | tf_op jit(solution)/shard_map/weights_last/ppermute | solution.py:31
  85.1 32.0 %collective-permute-start.11 = (bf16[2,256,512]{2,1,0:T(8,128)(2,1)S(1)}, bf16[2,256,512]{2,1,0:T(8,128)(2,1)S(1)}, u32[]{:S(2)}, u32[]{:S(2)}) collective-permute-start(bf16[2,256,512]{2,1,0:T(8,128)(2,1)S(1)} %get-tuple-element.19.refs_6_), channel_id=1, source_target_pairs={{0,8},{8,0},{16,24},{24,16},{1,9},{9,1},{17,25},{25,17},{2,10},{10... | collective-permute-start | bytes 1572872 | tf_op jit(solution)/shard_map/gradient_near/ppermute | solution.py:31
  91.0 34.4 %all-to-all-start.1 = ((bf16[4,256,512]{2,1,0:T(8,128)(2,1)}), bf16[4,256,512]{2,1,0:T(8,128)(2,1)S(1)}, u32[]{:S(2)}, u32[]{:S(2)}) async-start(bf16[4,256,512]{2,1,0:T(8,128)(2,1)} %shard_map.116.refs_2_), calls=%async_computation.1 | async-start | bytes 2097152 | tf_op jit(solution)/shard_map/all_to_all | solution.py:44
  94.6 27.2 %collective-permute-start.13 = (bf16[128,256]{1,0:T(8,128)(2,1)S(1)}, bf16[128,256]{1,0:T(8,128)(2,1)}, u32[]{:S(2)}, u32[]{:S(2)}) collective-permute-start(bf16[128,256]{1,0:T(8,128)(2,1)S(1)} %get-tuple-element.26), channel_id=1, source_target_pairs={{0,256},{256,0},{1,257},{257,1},{2,258},{258,2},{3,259},{259,3},{4... | collective-permute-start | bytes 196616 | tf_op jit(solution)/shard_map/rep_far/ppermute | solution.py:36
  117.2 29.4 %collective-permute-start.12 = (bf16[256,512]{1,0:T(8,128)(2,1)S(1)}, bf16[256,512]{1,0:T(8,128)(2,1)S(1)}, u32[]{:S(2)}, u32[]{:S(2)}) collective-permute-start(bf16[256,512]{1,0:T(8,128)(2,1)S(1)} %get-tuple-element.25), channel_id=1, source_target_pairs={{0,16},{8,24},{16,0},{24,8},{1,17},{9,25},{17,1},{25,9},{2,18},{10... | collective-permute-start | bytes 786440 | tf_op jit(solution)/shard_map/gradient_far/ppermute | solution.py:31
  122.7 24.5 %collective-permute-start.14 = (bf16[128,256]{1,0:T(8,128)(2,1)S(1)}, bf16[128,256]{1,0:T(8,128)(2,1)S(1)}, u32[]{:S(2)}, u32[]{:S(2)}) collective-permute-start(bf16[128,256]{1,0:T(8,128)(2,1)S(1)} %add_convert_fusion), channel_id=1, source_target_pairs={{0,32},{32,0},{1,33},{33,1},{2,34},{34,2},{3,35},{35,3},{4,36},{36... | collective-permute-start | bytes 196616 | tf_op jit(solution)/shard_map/rep_back/ppermute | solution.py:36
  126.1 20.6 %copy-start.3 = (f32[1,256,512]{2,1,0:T(8,128)S(1)}, f32[1,256,512]{2,1,0:T(8,128)}, u32[]{:S(2)}) copy-start(f32[1,256,512]{2,1,0:T(8,128)} %param.12) | copy-start | bytes 1572868
  126.1 20.6 %copy-start.5 = (f32[1,256,512]{2,1,0:T(8,128)S(1)}, f32[1,256,512]{2,1,0:T(8,128)}, u32[]{:S(2)}) copy-start(f32[1,256,512]{2,1,0:T(8,128)} %param.13) | copy-start | bytes 1572868
  126.1 20.6 %copy-start.6 = (bf16[1,256,512]{2,1,0:T(8,128)(2,1)S(1)}, bf16[1,256,512]{2,1,0:T(8,128)(2,1)}, u32[]{:S(2)}) copy-start(bf16[1,256,512]{2,1,0:T(8,128)(2,1)} %param.14) | copy-start | bytes 786436
  126.1 20.6 %copy-start.9 = (f32[256]{0:T(256)S(1)}, f32[256]{0:T(256)}, u32[]{:S(2)}) copy-start(f32[256]{0:T(256)} %get-tuple-element.29) | copy-start | bytes 3076
  126.1 22.4 %collective-permute-start.10 = (bf16[128,512]{1,0:T(8,128)(2,1)S(1)}, bf16[128,512]{1,0:T(8,128)(2,1)S(1)}, u32[]{:S(2)}, u32[]{:S(2)}) collective-permute-start(bf16[128,512]{1,0:T(8,128)(2,1)S(1)} %get-tuple-element.21), channel_id=1, source_target_pairs={{0,4},{4,0},{1,5},{5,1},{2,6},{6,2},{3,7},{7,3},{8,12},{12,8},{9,1... | collective-permute-start | bytes 393224 | tf_op jit(solution)/shard_map/keys_pair/ppermute | solution.py:36
  146.6 1.0 copy-start.7
  146.6 1.0 copy-start.8
  148.5 0.8 copy-start.4

commit v4 on v3

--- a/solution.py
+++ b/solution.py
@@ -15,6 +15,7 @@
 VMEM = pl.BlockSpec(memory_space=pltpu.VMEM)
 SMEM = pl.BlockSpec(memory_space=pltpu.SMEM)
 LAST_COST = 1 << 30
+FIRST_COST = 1 << 34
 KEYS_COST = 1 << 30
 RELAY_COST = 1 << 38
 PARAMS = pltpu.CompilerParams(vmem_limit_bytes=8 * 1024 * 1024)
@@ -93,7 +94,7 @@
 
 
 def gradient_blocks(rows, place_ref, tiles_ref, part_ref, g0, g1, g2, g3, *refs):
-    keep_ref, send_ref, part_out, grad_ref, sems = refs[-5:]
+    keep_a, keep_b, send_a, send_b, part_out, grad_ref, sems = refs[-7:]
     tokens = g0.shape[0] // 2
     copies = []
     for turn, piece in enumerate((g0, g1, g2, g3)):
@@ -107,23 +108,33 @@
     part_out[...] = part_ref[...]
     for copy_in in copies:
         copy_in.wait()
-    for dl in (1, 0):
-        for dh in range(2):
+    half = keep_a.shape[2]
+    for dh in (1, 0):
+        for dl in (1, 0):
             left = tiles_ref[:, block_of(place_ref, dh, dl, rows)]
             value = lax.dot_general(left, grad_ref[...], (((0,), (0,)), ((), ())), preferred_element_type=jnp.float32)
             if dl:
-                send_ref[dh] = value.astype(jnp.bfloat16)
+                send_a[dh] = value[:, :half].astype(jnp.bfloat16)
             else:
-                keep_ref[dh] = value
-
-
-def first_sum(keep_ref, got_ref, mine_ref, send_ref):
-    mine_ref[...] = keep_ref[0] + got_ref[0].astype(jnp.float32)
-    send_ref[...] = (keep_ref[1] + got_ref[1].astype(jnp.float32)).astype(jnp.bfloat16)
-
-
-def second_sum(mine_ref, got_ref, grad_ref):
-    grad_ref[...] = mine_ref[...] + got_ref[...].astype(jnp.float32)
+                keep_a[dh] = value[:, :half]
+            if dh:
+                send_b[dl] = value[:, half:].astype(jnp.bfloat16)
+            else:
+                keep_b[dl] = value[:, half:]
+
+
+def first_sum(keep_a, got_a, keep_b, got_b, mine_ref, rest_a, rest_b):
+    half = keep_a.shape[2]
+    mine_ref[:, :half] = keep_a[0] + got_a[0].astype(jnp.float32)
+    mine_ref[:, half:] = keep_b[0] + got_b[0].astype(jnp.float32)
+    rest_a[...] = (keep_a[1] + got_a[1].astype(jnp.float32)).astype(jnp.bfloat16)
+    rest_b[...] = (keep_b[1] + got_b[1].astype(jnp.float32)).astype(jnp.bfloat16)
+
+
+def second_sum(mine_ref, got_a, got_b, grad_ref):
+    half = got_a.shape[1]
+    grad_ref[:, :half] = mine_ref[:, :half] + got_a[...].astype(jnp.float32)
+    grad_ref[:, half:] = mine_ref[:, half:] + got_b[...].astype(jnp.float32)
 
 
 def key_halves(place_ref, partial_ref, mine_ref, send_ref):
@@ -210,9 +221,11 @@
     last_low = swap(relayed, 1, "weights_last")
 
     flops = 2 * near * tokens * far * rows * key_width
-    keep, send, part = kernel_call(
+    half = key_width // 2
+    block = (2, rows, half)
+    keep_a, keep_b, send_a, send_b, part = kernel_call(
         lambda *refs: gradient_blocks(rows, *refs),
-        [shape((2, rows, key_width), f32), shape((2, rows, key_width), b16), shape(part.shape, b16)],
+        [*(shape(block, f32),) * 2, *(shape(block, b16),) * 2, shape(part.shape, b16)],
         (place, tiles, part),
         flops,
         1,
@@ -220,32 +233,26 @@
         behind=(both, *turned, near_low, last_low),
         read=4,
     )
-    got = swap(send, 1, "gradient_near")
+    got_a, got_b = swap(send_a, 1, "gradient_near"), swap(send_b, 2, "gradient_far")
     (partial_keys,) = kernel_call(
         lambda *refs: key_partials(rows, multiplier, *refs),
         [shape((near // 2, 2 * tokens, key_width), b16)],
         (place, tiles, weight_low, near_low, far_low, last_low),
         KEYS_COST,
         1,
-        behind=(send,),
-    )
-    mine, rest = kernel_call(
+        behind=(send_a,),
+    )
+    mine, rest_a, rest_b = kernel_call(
         first_sum,
-        [shape((rows, key_width), f32), shape((rows, key_width), b16)],
-        (keep, got),
+        [shape((rows, key_width), f32), shape((rows, half), b16), shape((rows, half), b16)],
+        (keep_a, got_a, keep_b, got_b),
+        FIRST_COST,
         behind=(partial_keys,),
     )
-    last = swap(rest, 2, "gradient_far")
+    last_a, last_b = swap(rest_a, 2, "gradient_far"), swap(rest_b, 1, "gradient_near")
     part = add(part, flip(part, "zh", name="rep_far"))
     other = flip(part, "c", name="rep_back")
     summed_cols = jnp.where(core == 0, jnp.concatenate([part, other]), jnp.concatenate([other, part])).astype(f32)
-    (grad_sum,) = kernel_call(second_sum, [shape((rows, key_width), f32)], (mine, last), LAST_COST)
-    gradient = grad_sum * (multiplier * own_gain)
-    moment_next = 0.9 * first_moment[0] + 0.1 * gradient
-    second_next = 0.95 * second_moment[0].astype(f32) + 0.05 * gradient * gradient
-    inner = weight_now - INNER_RATE * (
-        moment_next / (jnp.sqrt(second_next) + ADAM_EPS) + 0.1 * weight_now
-    )
     partial_keys = exchange(partial_keys, "y")
     own_keys, pair_keys = kernel_call(
         key_halves,
@@ -254,6 +261,15 @@
         scalars=1,
     )
     pair_keys = flip(pair_keys, "zp", name="keys_pair")
+    (grad_sum,) = kernel_call(
+        second_sum, [shape((rows, key_width), f32)], (mine, last_a, last_b), LAST_COST, behind=(own_keys,)
+    )
+    gradient = grad_sum * (multiplier * own_gain)
+    moment_next = 0.9 * first_moment[0] + 0.1 * gradient
+    second_next = 0.95 * second_moment[0].astype(f32) + 0.05 * gradient * gradient
+    inner = weight_now - INNER_RATE * (
+        moment_next / (jnp.sqrt(second_next) + ADAM_EPS) + 0.1 * weight_now
+    )
     (keys,) = kernel_call(key_sum, [shape((tokens, key_width), b16)], (own_keys, pair_keys, factor))
 
     replicas = lax.axis_size(REP)

time: 150 us -> 145 us (0.967)
  waiting for transfers between devices: 54 us -> 38.3 us
  starting transfers between devices: 71.5 us -> 80.4 us
  local copies, waits for them, and re-layouts: 4 us -> 6.22 us
    ppermute x5 -> x7, waiting for transfers between devices: 31.7 us -> 15.9 us  [swap(): return lax.ppermute(value, 'zq', [(i, i ^ bit) for i in range(4)])]
    ppermute x5 -> x7, starting transfers between devices: 19.6 us -> 26.8 us  [swap(): return lax.ppermute(value, 'zq', [(i, i ^ bit) for i in range(4)])]
    unnamed x21 -> x25, local copies, waits for them, and re-layouts: 3.02 us -> 5.23 us
    ppermute x7, starting transfers between devices: 33.8 us -> 35.3 us  [flip(): lax.ppermute(value, axis, [(i, i ^ bit) for i in range(lax.axis_size(axis...]
  transfers between devices with their start and end apart: 17 -> 19, of which waited for: 6 -> 7; matrix products, arithmetic and copies ran while one was open for 4% -> 4% of each run, Pallas kernels for 5% -> 5%
where the time goes in v4:
time: 145 us; the launch traced here: 144 us
  starting transfers between devices  80.4 us (55%)
  waiting for transfers between devices  38.3 us (26%)
  Pallas kernels  12.2 us (8%)
  local copies, waits for them, and re-layouts  6.22 us (4%)
  other arithmetic  5.1 us (4%)
  between operations  1.7 us (1%)
    ppermute x7, starting transfers between devices, flip(): lax.ppermute(value, axis, [(i, i ^ bit) for i in range(lax.axis_size(axis...  35.3 us
    ppermute x7, starting transfers between devices, swap(): return lax.ppermute(value, 'zq', [(i, i ^ bit) for i in range(4)])  26.8 us
    ppermute x3, waiting for transfers between devices, on_device(): lax.ppermute(both, 'y', [(i, (i + k) % 4) for i in range(4)])  16 us
    ppermute x7, waiting for transfers between devices, swap(): return lax.ppermute(value, 'zq', [(i, i ^ bit) for i in range(4)])  15.9 us
    pallas_call x8, Pallas kernels, kernel_call(): pl.pallas_call(run, out_shape=outs, in_specs=[SMEM] * scalars + [VMEM] *...  11.5 us
    ppermute x3, starting transfers between devices, on_device(): lax.ppermute(both, 'y', [(i, (i + k) % 4) for i in range(4)])  10.1 us
    all_to_all x2, starting transfers between devices, exchange(): return lax.all_to_all(value, axes, split_axis=0, concat_axis=0, tiled=True)  8.22 us
    unnamed x25, local copies, waits for them, and re-layouts  5.23 us
  transfers between devices with their start and end apart: 19, of which 7 were waited for; matrix products, arithmetic and copies ran while one was open for 4% of the time, Pallas kernels for 5%

profile of v4, /device:TPU:1, one launch (start us, length us, event | category | flops | bytes accessed | tf_op | source)
XLA Modules:
  0.0 143.9 jit_solution(13017025259858424289)
XLA Ops:
  1.3 1.0 dynamic-slice_convert_fusion
  2.3 8.8 %collective-permute-start.4 = (bf16[128,256]{1,0:T(8,128)(2,1)S(1)}, bf16[128,256]{1,0:T(8,128)(2,1)S(1)}, u32[]{:S(2)}, u32[]{:S(2)}) collective-permute-start(bf16[128,256]{1,0:T(8,128)(2,1)S(1)} %dynamic-slice_bitcast_fusion), channel_id=1, source_target_pairs={{0,32},{32,0},{1,33},{33,1},{2,34},{34,2},{3,35},{35,3},{4,36},{36... | collective-permute-start | bytes 196616 | tf_op jit(solution)/shard_map/rep_sum/ppermute | solution.py:37
  11.1 0.0 copy-start
  11.1 1.6 %copy-done = bf16[128,8192]{1,0:T(8,128)(2,1)S(1)} copy-done((bf16[128,8192]{1,0:T(8,128)(2,1)S(1)}, bf16[128,8192]{1,0:T(8,128)(2,1)}, u32[]{:S(2)}) %copy-start) | copy-done | bytes 2097176
  12.7 0.9 copy-done.1
  13.6 1.6 %shard_map.112 = (bf16[8,128,1024]{2,1,0:T(8,128)(2,1)}, bf16[128,512]{1,0:T(8,128)(2,1)S(1)}, f32[128,1]{1,0:T(8,128)S(1)}) custom-call(bf16[128,8192]{1,0:T(8,128)(2,1)S(1)} %copy-done, bf16[128,512]{1,0:T(8,128)(2,1)S(1)} %copy-done.1), custom_call_target="tpu_custom_call" | custom-call | bytes 4456960 | tf_op jit(solution)/shard_map/pallas_call | solution.py:56
  15.2 1.9 %collective-permute-start = (bf16[128,512]{1,0:T(8,128)(2,1)S(1)}, bf16[128,512]{1,0:T(8,128)(2,1)S(1)}, u32[]{:S(2)}, u32[]{:S(2)}) collective-permute-start(bf16[128,512]{1,0:T(8,128)(2,1)S(1)} %get-tuple-element.18.own_ref), channel_id=1, source_target_pairs={{0,4},{4,0},{1,5},{5,1},{2,6},{6,2},{3,7},{7,3},{8,12},{12,8},{9,1... | collective-permute-start | bytes 393224 | tf_op jit(solution)/shard_map/cotangent_pair/ppermute | solution.py:37
  17.1 1.4 broadcast_multiply_fusion
  18.5 0.0 collective-permute-done.4
  18.5 1.9 %collective-permute-start.5 = (bf16[128,256]{1,0:T(8,128)(2,1)S(1)}, bf16[128,256]{1,0:T(8,128)(2,1)S(1)}, u32[]{:S(2)}, u32[]{:S(2)}) collective-permute-start(bf16[128,256]{1,0:T(8,128)(2,1)S(1)} %fusion.8), channel_id=1, source_target_pairs={{0,64},{64,0},{128,192},{192,128},{1,65},{65,1},{129,193},{193,129... | collective-permute-start | bytes 196616 | tf_op jit(solution)/shard_map/rep_sum/ppermute | solution.py:37
  20.4 0.8 fusion.7.refs_2_
  21.2 6.3 %collective-permute-start.2 = (bf16[256,512]{1,0:T(8,128)(2,1)}, bf16[256,512]{1,0:T(8,128)(2,1)S(1)}, u32[]{:S(2)}, u32[]{:S(2)}) collective-permute-start(bf16[256,512]{1,0:T(8,128)(2,1)} %fusion.7.refs_2_), channel_id=1, source_target_pairs={{0,16},{8,24},{16,0},{24,8},{1,17},{9,25},{17,1},{25,9},{2,18},{10... | collective-permute-start | bytes 786440 | tf_op jit(solution)/shard_map/weights_far/ppermute | solution.py:32
  27.5 4.9 %collective-permute-start.1 = (bf16[256,512]{1,0:T(8,128)(2,1)}, bf16[256,512]{1,0:T(8,128)(2,1)}, u32[]{:S(2)}, u32[]{:S(2)}) collective-permute-start(bf16[256,512]{1,0:T(8,128)(2,1)} %fusion.7.refs_2_), channel_id=1, source_target_pairs={{0,8},{8,0},{16,24},{24,16},{1,9},{9,1},{17,25},{25,17},{2,10},{10... | collective-permute-start | bytes 786440 | tf_op jit(solution)/shard_map/weights_near/ppermute | solution.py:32
  32.4 0.0 collective-permute-done.other_ref
  32.4 0.7 shard_map.113
  33.1 4.6 %collective-permute-start.9 = (bf16[256,512]{1,0:T(8,128)(2,1)}, bf16[256,512]{1,0:T(8,128)(2,1)}, u32[]{:S(2)}, u32[]{:S(2)}) collective-permute-start(bf16[256,512]{1,0:T(8,128)(2,1)} %get-tuple-element.21.refs_3_), channel_id=1, source_target_pairs={{0,3},{1,0},{2,1},{3,2},{4,7},{5,4},{6,5},{7,6},{8,11},{9,8},{10,9... | collective-permute-start | bytes 786440 | tf_op jit(solution)/shard_map/cotangent_y/ppermute | solution.py:203
  37.8 2.3 %collective-permute-start.8 = (bf16[256,512]{1,0:T(8,128)(2,1)}, bf16[256,512]{1,0:T(8,128)(2,1)}, u32[]{:S(2)}, u32[]{:S(2)}) collective-permute-start(bf16[256,512]{1,0:T(8,128)(2,1)} %get-tuple-element.21.refs_3_), channel_id=1, source_target_pairs={{0,2},{1,3},{2,0},{3,1},{4,6},{5,7},{6,4},{7,5},{8,10},{9,11},{10,... | collective-permute-start | bytes 786440 | tf_op jit(solution)/shard_map/cotangent_y/ppermute | solution.py:203
  40.1 4.4 %all-to-all-start = ((bf16[8,128,1024]{2,1,0:T(8,128)(2,1)}), bf16[8,128,1024]{2,1,0:T(8,128)(2,1)}, u32[]{:S(2)}, u32[]{:S(2)}) async-start(bf16[8,128,1024]{2,1,0:T(8,128)(2,1)} %get-tuple-element.20), calls=%async_computation | async-start | bytes 4194304 | tf_op jit(solution)/shard_map/all_to_all | solution.py:45
  44.4 0.0 collective-permute-done.5
  44.4 3.2 %collective-permute-start.7 = (bf16[256,512]{1,0:T(8,128)(2,1)}, bf16[256,512]{1,0:T(8,128)(2,1)}, u32[]{:S(2)}, u32[]{:S(2)}) collective-permute-start(bf16[256,512]{1,0:T(8,128)(2,1)} %get-tuple-element.21.refs_3_), channel_id=1, source_target_pairs={{0,1},{1,2},{2,3},{3,0},{4,5},{5,6},{6,7},{7,4},{8,9},{9,10},{10,1... | collective-permute-start | bytes 786440 | tf_op jit(solution)/shard_map/cotangent_y/ppermute | solution.py:203
  47.7 0.6 add_convert_fusion.2
  48.3 3.8 %collective-permute-done.2.refs_0_.refs_4_ = bf16[256,512]{1,0:T(8,128)(2,1)S(1)} collective-permute-done((bf16[256,512]{1,0:T(8,128)(2,1)}, bf16[256,512]{1,0:T(8,128)(2,1)S(1)}, u32[]{:S(2)}, u32[]{:S(2)}) %collective-permute-start.2) | collective-permute-done | bytes 262176 | tf_op jit(solution)/shard_map/weights_far/ppermute | solution.py:32
  52.1 3.4 %collective-permute-start.6 = (bf16[128,256]{1,0:T(8,128)(2,1)}, bf16[128,256]{1,0:T(8,128)(2,1)}, u32[]{:S(2)}, u32[]{:S(2)}) collective-permute-start(bf16[128,256]{1,0:T(8,128)(2,1)} %add_convert_fusion.2), channel_id=1, source_target_pairs={{0,128},{64,192},{128,0},{192,64},{1,129},{65,193},{129,1},{193,65... | collective-permute-start | bytes 196616 | tf_op jit(solution)/shard_map/rep_sum/ppermute | solution.py:37
  55.5 3.4 %collective-permute-done.6 = bf16[128,256]{1,0:T(8,128)(2,1)} collective-permute-done((bf16[128,256]{1,0:T(8,128)(2,1)}, bf16[128,256]{1,0:T(8,128)(2,1)}, u32[]{:S(2)}, u32[]{:S(2)}) %collective-permute-start.6) | collective-permute-done | bytes 65568 | tf_op jit(solution)/shard_map/rep_sum/ppermute | solution.py:37
  58.9 1.9 %collective-permute-start.3 = (bf16[256,512]{1,0:T(8,128)(2,1)S(1)}, bf16[256,512]{1,0:T(8,128)(2,1)S(1)}, u32[]{:S(2)}, u32[]{:S(2)}) collective-permute-start(bf16[256,512]{1,0:T(8,128)(2,1)S(1)} %shard_map.114), channel_id=1, source_target_pairs={{0,8},{8,0},{16,24},{24,16},{1,9},{9,1},{17,25},{25,17},{2,10},{10... | collective-permute-start | bytes 786440 | tf_op jit(solution)/shard_map/weights_last/ppermute | solution.py:32
  60.8 0.1 pad_add_fusion.refs_0_
  60.9 0.9 add_convert_fusion.1.refs_2_
  61.8 0.0 collective-permute-done.1.refs_7_.refs_3_
  61.8 0.0 collective-permute-done.9.refs_6_
  61.8 0.0 collective-permute-done.8.refs_5_
  61.8 16.0 %collective-permute-done.7.refs_4_ = bf16[256,512]{1,0:T(8,128)(2,1)} collective-permute-done((bf16[256,512]{1,0:T(8,128)(2,1)}, bf16[256,512]{1,0:T(8,128)(2,1)}, u32[]{:S(2)}, u32[]{:S(2)}) %collective-permute-start.7) | collective-permute-done | bytes 262176 | tf_op jit(solution)/shard_map/cotangent_y/ppermute | solution.py:203
  77.8 0.0 collective-permute-done.3.refs_8_.refs_5_
  77.8 3.0 %all-to-all-done = bf16[8,128,1024]{2,1,0:T(8,128)(2,1)} async-done(((bf16[8,128,1024]{2,1,0:T(8,128)(2,1)}), bf16[8,128,1024]{2,1,0:T(8,128)(2,1)}, u32[]{:S(2)}, u32[]{:S(2)}) %all-to-all-start) | async-done | bytes 2097184 | tf_op jit(solution)/shard_map/all_to_all | solution.py:45
  80.8 4.3 %shard_map.115 = (f32[2,256,256]{2,1,0:T(8,128)S(1)}, f32[2,256,256]{2,1,0:T(8,128)S(1)}, bf16[2,256,256]{2,1,0:T(8,128)(2,1)S(1)}, bf16[2,256,256]{2,1,0:T(8,128)(2,1)S(1)}, bf16[128,256]{1,0:T(8,128)(2,1)S(1)}) custom-call(s32[4]{0:T(128)S(1)} %pad_add_fusion.refs_0_, bf16[1024,1024]{1,0:T(8,128)(2,1)} %bitcast.4.refs_1_, ...), custom_call_target="tpu_custom_call" | custom-call | flops 1073741824 | bytes 3801104 | tf_op jit(solution)/shard_map/pallas_call | solution.py:56
  85.1 4.9 %collective-permute-start.12 = (bf16[2,256,256]{2,1,0:T(8,128)(2,1)S(1)}, bf16[2,256,256]{2,1,0:T(8,128)(2,1)S(1)}, u32[]{:S(2)}, u32[]{:S(2)}) collective-permute-start(bf16[2,256,256]{2,1,0:T(8,128)(2,1)S(1)} %get-tuple-element.28), channel_id=1, source_target_pairs={{0,16},{8,24},{16,0},{24,8},{1,17},{9,25},{17,1},{25,9},{2,18},{10... | collective-permute-start | bytes 786440 | tf_op jit(solution)/shard_map/gradient_far/ppermute | solution.py:32
  90.0 5.0 %collective-permute-start.11 = (bf16[2,256,256]{2,1,0:T(8,128)(2,1)S(1)}, bf16[2,256,256]{2,1,0:T(8,128)(2,1)S(1)}, u32[]{:S(2)}, u32[]{:S(2)}) collective-permute-start(bf16[2,256,256]{2,1,0:T(8,128)(2,1)S(1)} %get-tuple-element.22.refs_6_), channel_id=1, source_target_pairs={{0,8},{8,0},{16,24},{24,16},{1,9},{9,1},{17,25},{25,17},{2,10},{10... | collective-permute-start | bytes 786440 | tf_op jit(solution)/shard_map/gradient_near/ppermute | solution.py:32
  95.0 3.9 %shard_map.116.refs_4_ = bf16[4,256,512]{2,1,0:T(8,128)(2,1)} custom-call(s32[4]{0:T(128)S(1)} %pad_add_fusion.refs_0_, bf16[1024,1024]{1,0:T(8,128)(2,1)} %bitcast.4.refs_1_, bf16[256,512]{1,0:T(8,128)(2,1)} %fusion.7.refs_2_, bf16[256,512]{1,0:T(8,128)(2,1)} %collective-permute-done.1.refs_7_.refs_3_, ...), custom_call_target="tpu_custom_call" | custom-call | flops 1073741824 | bytes 4194320 | tf_op jit(solution)/shard_map/pallas_call | solution.py:56
  98.9 3.9 %all-to-all-start.1 = ((bf16[4,256,512]{2,1,0:T(8,128)(2,1)}), bf16[4,256,512]{2,1,0:T(8,128)(2,1)S(1)}, u32[]{:S(2)}, u32[]{:S(2)}) async-start(bf16[4,256,512]{2,1,0:T(8,128)(2,1)} %shard_map.116.refs_4_), calls=%async_computation.1 | async-start | bytes 2097152 | tf_op jit(solution)/shard_map/all_to_all | solution.py:45
  102.8 9.3 %collective-permute-start.15 = (bf16[128,256]{1,0:T(8,128)(2,1)S(1)}, bf16[128,256]{1,0:T(8,128)(2,1)S(1)}, u32[]{:S(2)}, u32[]{:S(2)}) collective-permute-start(bf16[128,256]{1,0:T(8,128)(2,1)S(1)} %get-tuple-element.32), channel_id=1, source_target_pairs={{0,256},{256,0},{1,257},{257,1},{2,258},{258,2},{3,259},{259,3},{4... | collective-permute-start | bytes 196616 | tf_op jit(solution)/shard_map/rep_far/ppermute | solution.py:37
  112.1 3.8 %collective-permute-done.12.refs_3_ = bf16[2,256,256]{2,1,0:T(8,128)(2,1)S(1)} collective-permute-done((bf16[2,256,256]{2,1,0:T(8,128)(2,1)S(1)}, bf16[2,256,256]{2,1,0:T(8,128)(2,1)S(1)}, u32[]{:S(2)}, u32[]{:S(2)}) %collective-permute-start.12) | collective-permute-done | bytes 262176 | tf_op jit(solution)/shard_map/gradient_far/ppermute | solution.py:32
  115.8 5.5 %collective-permute-done.11.refs_1_ = bf16[2,256,256]{2,1,0:T(8,128)(2,1)S(1)} collective-permute-done((bf16[2,256,256]{2,1,0:T(8,128)(2,1)S(1)}, bf16[2,256,256]{2,1,0:T(8,128)(2,1)S(1)}, u32[]{:S(2)}, u32[]{:S(2)}) %collective-permute-start.11) | collective-permute-done | bytes 262176 | tf_op jit(solution)/shard_map/gradient_near/ppermute | solution.py:32
  121.4 0.1 shard_map.119
  121.5 0.0 copy-start.2
  121.5 0.8 copy-done.2
  122.3 1.9 %collective-permute-start.13 = (bf16[256,256]{1,0:T(8,128)(2,1)S(1)}, bf16[256,256]{1,0:T(8,128)(2,1)S(1)}, u32[]{:S(2)}, u32[]{:S(2)}) collective-permute-start(bf16[256,256]{1,0:T(8,128)(2,1)S(1)} %get-tuple-element.30), channel_id=1, source_target_pairs={{0,16},{8,24},{16,0},{24,8},{1,17},{9,25},{17,1},{25,9},{2,18},{10... | collective-permute-start | bytes 393224 | tf_op jit(solution)/shard_map/gradient_far/ppermute | solution.py:32
  124.2 1.9 %collective-permute-start.14 = (bf16[256,256]{1,0:T(8,128)(2,1)S(1)}, bf16[256,256]{1,0:T(8,128)(2,1)S(1)}, u32[]{:S(2)}, u32[]{:S(2)}) collective-permute-start(bf16[256,256]{1,0:T(8,128)(2,1)S(1)} %get-tuple-element.31), channel_id=1, source_target_pairs={{0,8},{8,0},{16,24},{24,16},{1,9},{9,1},{17,25},{25,17},{2,10},{10... | collective-permute-start | bytes 393224 | tf_op jit(solution)/shard_map/gradient_near/ppermute | solution.py:32
  126.1 0.0 collective-permute-done.15
  126.2 2.4 %collective-permute-start.16 = (bf16[128,256]{1,0:T(8,128)(2,1)S(1)}, bf16[128,256]{1,0:T(8,128)(2,1)S(1)}, u32[]{:S(2)}, u32[]{:S(2)}) collective-permute-start(bf16[128,256]{1,0:T(8,128)(2,1)S(1)} %add_convert_fusion), channel_id=1, source_target_pairs={{0,32},{32,0},{1,33},{33,1},{2,34},{34,2},{3,35},{35,3},{4,36},{36... | collective-permute-start | bytes 196616 | tf_op jit(solution)/shard_map/rep_back/ppermute | solution.py:37
  128.6 0.0 copy-start.5
  128.6 0.0 copy-start.7
  128.6 0.7 shard_map.117
  129.3 7.6 %collective-permute-start.10 = (bf16[128,512]{1,0:T(8,128)(2,1)S(1)}, bf16[128,512]{1,0:T(8,128)(2,1)S(1)}, u32[]{:S(2)}, u32[]{:S(2)}) collective-permute-start(bf16[128,512]{1,0:T(8,128)(2,1)S(1)} %get-tuple-element.24), channel_id=1, source_target_pairs={{0,4},{4,0},{1,5},{5,1},{2,6},{6,2},{3,7},{7,3},{8,12},{12,8},{9,1... | collective-permute-start | bytes 393224 | tf_op jit(solution)/shard_map/keys_pair/ppermute | solution.py:37
  136.9 2.8 %collective-permute-done.13.refs_1_ = bf16[256,256]{1,0:T(8,128)(2,1)S(1)} collective-permute-done((bf16[256,256]{1,0:T(8,128)(2,1)S(1)}, bf16[256,256]{1,0:T(8,128)(2,1)S(1)}, u32[]{:S(2)}, u32[]{:S(2)}) %collective-permute-start.13) | collective-permute-done | bytes 131104 | tf_op jit(solution)/shard_map/gradient_far/ppermute | solution.py:32
  139.7 0.0 collective-permute-done.14.refs_2_
  139.8 1.0 copy-done.3
  140.8 0.1 shard_map.120
  140.9 0.0 copy-start.9
  140.9 0.0 copy-start.10
  140.9 0.8 copy-done.8
  141.7 0.5 fusion.6
  142.2 0.0 collective-permute-done.16
  142.3 0.8 bitcast_dynamic-update-slice_fusion
  143.1 0.0 collective-permute-done.10.refs_1_
  143.1 0.8 shard_map.118
  (19 shorter events, 0.1 us)
Async XLA Ops:
  2.3 16.2 %collective-permute-start.4 = (bf16[128,256]{1,0:T(8,128)(2,1)S(1)}, bf16[128,256]{1,0:T(8,128)(2,1)S(1)}, u32[]{:S(2)}, u32[]{:S(2)}) collective-permute-start(bf16[128,256]{1,0:T(8,128)(2,1)S(1)} %dynamic-slice_bitcast_fusion), channel_id=1, source_target_pairs={{0,32},{32,0},{1,33},{33,1},{2,34},{34,2},{3,35},{35,3},{4,36},{36... | collective-permute-start | bytes 196616 | tf_op jit(solution)/shard_map/rep_sum/ppermute | solution.py:37
  11.1 1.6 %copy-start = (bf16[128,8192]{1,0:T(8,128)(2,1)S(1)}, bf16[128,8192]{1,0:T(8,128)(2,1)}, u32[]{:S(2)}) copy-start(bf16[128,8192]{1,0:T(8,128)(2,1)} %refs_0_.1) | copy-start | bytes 6291460
  12.7 0.9 copy-start.1
  13.6 6.9 %copy-start.4 = (f32[1,256,512]{2,1,0:T(8,128)S(1)}, f32[1,256,512]{2,1,0:T(8,128)}, u32[]{:S(2)}) copy-start(f32[1,256,512]{2,1,0:T(8,128)} %param.12) | copy-start | bytes 1572868
  15.2 17.2 %collective-permute-start = (bf16[128,512]{1,0:T(8,128)(2,1)S(1)}, bf16[128,512]{1,0:T(8,128)(2,1)S(1)}, u32[]{:S(2)}, u32[]{:S(2)}) collective-permute-start(bf16[128,512]{1,0:T(8,128)(2,1)S(1)} %get-tuple-element.18.own_ref), channel_id=1, source_target_pairs={{0,4},{4,0},{1,5},{5,1},{2,6},{6,2},{3,7},{7,3},{8,12},{12,8},{9,1... | collective-permute-start | bytes 393224 | tf_op jit(solution)/shard_map/cotangent_pair/ppermute | solution.py:37
  18.5 25.9 %collective-permute-start.5 = (bf16[128,256]{1,0:T(8,128)(2,1)S(1)}, bf16[128,256]{1,0:T(8,128)(2,1)S(1)}, u32[]{:S(2)}, u32[]{:S(2)}) collective-permute-start(bf16[128,256]{1,0:T(8,128)(2,1)S(1)} %fusion.8), channel_id=1, source_target_pairs={{0,64},{64,0},{128,192},{192,128},{1,65},{65,1},{129,193},{193,129... | collective-permute-start | bytes 196616 | tf_op jit(solution)/shard_map/rep_sum/ppermute | solution.py:37
  21.2 30.9 %collective-permute-start.2 = (bf16[256,512]{1,0:T(8,128)(2,1)}, bf16[256,512]{1,0:T(8,128)(2,1)S(1)}, u32[]{:S(2)}, u32[]{:S(2)}) collective-permute-start(bf16[256,512]{1,0:T(8,128)(2,1)} %fusion.7.refs_2_), channel_id=1, source_target_pairs={{0,16},{8,24},{16,0},{24,8},{1,17},{9,25},{17,1},{25,9},{2,18},{10... | collective-permute-start | bytes 786440 | tf_op jit(solution)/shard_map/weights_far/ppermute | solution.py:32
  27.5 34.3 %collective-permute-start.1 = (bf16[256,512]{1,0:T(8,128)(2,1)}, bf16[256,512]{1,0:T(8,128)(2,1)}, u32[]{:S(2)}, u32[]{:S(2)}) collective-permute-start(bf16[256,512]{1,0:T(8,128)(2,1)} %fusion.7.refs_2_), channel_id=1, source_target_pairs={{0,8},{8,0},{16,24},{24,16},{1,9},{9,1},{17,25},{25,17},{2,10},{10... | collective-permute-start | bytes 786440 | tf_op jit(solution)/shard_map/weights_near/ppermute | solution.py:32
  33.1 28.7 %collective-permute-start.9 = (bf16[256,512]{1,0:T(8,128)(2,1)}, bf16[256,512]{1,0:T(8,128)(2,1)}, u32[]{:S(2)}, u32[]{:S(2)}) collective-permute-start(bf16[256,512]{1,0:T(8,128)(2,1)} %get-tuple-element.21.refs_3_), channel_id=1, source_target_pairs={{0,3},{1,0},{2,1},{3,2},{4,7},{5,4},{6,5},{7,6},{8,11},{9,8},{10,9... | collective-permute-start | bytes 786440 | tf_op jit(solution)/shard_map/cotangent_y/ppermute | solution.py:203
  37.8 24.1 %collective-permute-start.8 = (bf16[256,512]{1,0:T(8,128)(2,1)}, bf16[256,512]{1,0:T(8,128)(2,1)}, u32[]{:S(2)}, u32[]{:S(2)}) collective-permute-start(bf16[256,512]{1,0:T(8,128)(2,1)} %get-tuple-element.21.refs_3_), channel_id=1, source_target_pairs={{0,2},{1,3},{2,0},{3,1},{4,6},{5,7},{6,4},{7,5},{8,10},{9,11},{10,... | collective-permute-start | bytes 786440 | tf_op jit(solution)/shard_map/cotangent_y/ppermute | solution.py:203
  40.1 40.8 %all-to-all-start = ((bf16[8,128,1024]{2,1,0:T(8,128)(2,1)}), bf16[8,128,1024]{2,1,0:T(8,128)(2,1)}, u32[]{:S(2)}, u32[]{:S(2)}) async-start(bf16[8,128,1024]{2,1,0:T(8,128)(2,1)} %get-tuple-element.20), calls=%async_computation | async-start | bytes 4194304 | tf_op jit(solution)/shard_map/all_to_all | solution.py:45
  44.4 33.4 %collective-permute-start.7 = (bf16[256,512]{1,0:T(8,128)(2,1)}, bf16[256,512]{1,0:T(8,128)(2,1)}, u32[]{:S(2)}, u32[]{:S(2)}) collective-permute-start(bf16[256,512]{1,0:T(8,128)(2,1)} %get-tuple-element.21.refs_3_), channel_id=1, source_target_pairs={{0,1},{1,2},{2,3},{3,0},{4,5},{5,6},{6,7},{7,4},{8,9},{9,10},{10,1... | collective-permute-start | bytes 786440 | tf_op jit(solution)/shard_map/cotangent_y/ppermute | solution.py:203
  52.1 6.8 %collective-permute-start.6 = (bf16[128,256]{1,0:T(8,128)(2,1)}, bf16[128,256]{1,0:T(8,128)(2,1)}, u32[]{:S(2)}, u32[]{:S(2)}) collective-permute-start(bf16[128,256]{1,0:T(8,128)(2,1)} %add_convert_fusion.2), channel_id=1, source_target_pairs={{0,128},{64,192},{128,0},{192,64},{1,129},{65,193},{129,1},{193,65... | collective-permute-start | bytes 196616 | tf_op jit(solution)/shard_map/rep_sum/ppermute | solution.py:37
  58.9 18.9 %collective-permute-start.3 = (bf16[256,512]{1,0:T(8,128)(2,1)S(1)}, bf16[256,512]{1,0:T(8,128)(2,1)S(1)}, u32[]{:S(2)}, u32[]{:S(2)}) collective-permute-start(bf16[256,512]{1,0:T(8,128)(2,1)S(1)} %shard_map.114), channel_id=1, source_target_pairs={{0,8},{8,0},{16,24},{24,16},{1,9},{9,1},{17,25},{25,17},{2,10},{10... | collective-permute-start | bytes 786440 | tf_op jit(solution)/shard_map/weights_last/ppermute | solution.py:32
  85.1 30.8 %collective-permute-start.12 = (bf16[2,256,256]{2,1,0:T(8,128)(2,1)S(1)}, bf16[2,256,256]{2,1,0:T(8,128)(2,1)S(1)}, u32[]{:S(2)}, u32[]{:S(2)}) collective-permute-start(bf16[2,256,256]{2,1,0:T(8,128)(2,1)S(1)} %get-tuple-element.28), channel_id=1, source_target_pairs={{0,16},{8,24},{16,0},{24,8},{1,17},{9,25},{17,1},{25,9},{2,18},{10... | collective-permute-start | bytes 786440 | tf_op jit(solution)/shard_map/gradient_far/ppermute | solution.py:32
  90.0 31.4 %collective-permute-start.11 = (bf16[2,256,256]{2,1,0:T(8,128)(2,1)S(1)}, bf16[2,256,256]{2,1,0:T(8,128)(2,1)S(1)}, u32[]{:S(2)}, u32[]{:S(2)}) collective-permute-start(bf16[2,256,256]{2,1,0:T(8,128)(2,1)S(1)} %get-tuple-element.22.refs_6_), channel_id=1, source_target_pairs={{0,8},{8,0},{16,24},{24,16},{1,9},{9,1},{17,25},{25,17},{2,10},{10... | collective-permute-start | bytes 786440 | tf_op jit(solution)/shard_map/gradient_near/ppermute | solution.py:32
  98.9 29.6 %all-to-all-start.1 = ((bf16[4,256,512]{2,1,0:T(8,128)(2,1)}), bf16[4,256,512]{2,1,0:T(8,128)(2,1)S(1)}, u32[]{:S(2)}, u32[]{:S(2)}) async-start(bf16[4,256,512]{2,1,0:T(8,128)(2,1)} %shard_map.116.refs_4_), calls=%async_computation.1 | async-start | bytes 2097152 | tf_op jit(solution)/shard_map/all_to_all | solution.py:45
  102.8 23.3 %collective-permute-start.15 = (bf16[128,256]{1,0:T(8,128)(2,1)S(1)}, bf16[128,256]{1,0:T(8,128)(2,1)S(1)}, u32[]{:S(2)}, u32[]{:S(2)}) collective-permute-start(bf16[128,256]{1,0:T(8,128)(2,1)S(1)} %get-tuple-element.32), channel_id=1, source_target_pairs={{0,256},{256,0},{1,257},{257,1},{2,258},{258,2},{3,259},{259,3},{4... | collective-permute-start | bytes 196616 | tf_op jit(solution)/shard_map/rep_far/ppermute | solution.py:37
  121.5 0.8 copy-start.2
  122.3 17.5 %collective-permute-start.13 = (bf16[256,256]{1,0:T(8,128)(2,1)S(1)}, bf16[256,256]{1,0:T(8,128)(2,1)S(1)}, u32[]{:S(2)}, u32[]{:S(2)}) collective-permute-start(bf16[256,256]{1,0:T(8,128)(2,1)S(1)} %get-tuple-element.30), channel_id=1, source_target_pairs={{0,16},{8,24},{16,0},{24,8},{1,17},{9,25},{17,1},{25,9},{2,18},{10... | collective-permute-start | bytes 393224 | tf_op jit(solution)/shard_map/gradient_far/ppermute | solution.py:32
  124.2 15.6 %collective-permute-start.14 = (bf16[256,256]{1,0:T(8,128)(2,1)S(1)}, bf16[256,256]{1,0:T(8,128)(2,1)S(1)}, u32[]{:S(2)}, u32[]{:S(2)}) collective-permute-start(bf16[256,256]{1,0:T(8,128)(2,1)S(1)} %get-tuple-element.31), channel_id=1, source_target_pairs={{0,8},{8,0},{16,24},{24,16},{1,9},{9,1},{17,25},{25,17},{2,10},{10... | collective-permute-start | bytes 393224 | tf_op jit(solution)/shard_map/gradient_near/ppermute | solution.py:32
  126.2 16.1 %collective-permute-start.16 = (bf16[128,256]{1,0:T(8,128)(2,1)S(1)}, bf16[128,256]{1,0:T(8,128)(2,1)S(1)}, u32[]{:S(2)}, u32[]{:S(2)}) collective-permute-start(bf16[128,256]{1,0:T(8,128)(2,1)S(1)} %add_convert_fusion), channel_id=1, source_target_pairs={{0,32},{32,0},{1,33},{33,1},{2,34},{34,2},{3,35},{35,3},{4,36},{36... | collective-permute-start | bytes 196616 | tf_op jit(solution)/shard_map/rep_back/ppermute | solution.py:37
  128.6 12.3 %copy-start.5 = (f32[1,256,512]{2,1,0:T(8,128)S(1)}, f32[1,256,512]{2,1,0:T(8,128)}, u32[]{:S(2)}) copy-start(f32[1,256,512]{2,1,0:T(8,128)} %param.12) | copy-start | bytes 1572868
  128.6 12.3 %copy-start.7 = (f32[1,256,512]{2,1,0:T(8,128)S(1)}, f32[1,256,512]{2,1,0:T(8,128)}, u32[]{:S(2)}) copy-start(f32[1,256,512]{2,1,0:T(8,128)} %param.13) | copy-start | bytes 1572868
  129.3 11.6 %copy-start.11 = (f32[256]{0:T(256)S(1)}, f32[256]{0:T(256)}, u32[]{:S(2)}) copy-start(f32[256]{0:T(256)} %get-tuple-element.35) | copy-start | bytes 3076
  129.3 13.8 %collective-permute-start.10 = (bf16[128,512]{1,0:T(8,128)(2,1)S(1)}, bf16[128,512]{1,0:T(8,128)(2,1)S(1)}, u32[]{:S(2)}, u32[]{:S(2)}) collective-permute-start(bf16[128,512]{1,0:T(8,128)(2,1)S(1)} %get-tuple-element.24), channel_id=1, source_target_pairs={{0,4},{4,0},{1,5},{5,1},{2,6},{6,2},{3,7},{7,3},{8,12},{12,8},{9,1... | collective-permute-start | bytes 393224 | tf_op jit(solution)/shard_map/keys_pair/ppermute | solution.py:37
  139.8 1.0 copy-start.3
  140.8 0.9 copy-start.8
  140.9 1.4 copy-start.9
  140.9 1.4 copy-start.10
  143.1 0.8 copy-start.6

commit v5 on v4

--- a/solution.py
+++ b/solution.py
@@ -68,8 +68,13 @@
     to_ref[...] = from_ref[...]
 
 
-def prepare(far, near, rows, hidden_ref, grad_ref, tiles_ref, scaled_ref, factor_ref):
+def prepare(far, near, rows, pick_ref, hidden_ref, grad_ref, now_ref, tiles_ref, scaled_ref, factor_ref, mine_ref, theirs_ref):
     tokens, features = hidden_ref.shape
+    count, width = mine_ref.shape
+    columns = pl.ds(pl.multiple_of(pick_ref[0] * width, width), width)
+    for turn, out_ref in ((0, mine_ref), (1, theirs_ref)):
+        part_rows = pl.ds(pl.multiple_of((pick_ref[1] ^ turn) * count, count), count)
+        out_ref[...] = now_ref[part_rows, columns].astype(jnp.bfloat16)
     total = jnp.zeros((tokens, rows), jnp.float32)
     for a in range(near):
         for q in range(far):
@@ -93,8 +98,8 @@
     return pl.ds(pl.multiple_of(block * rows, rows), rows)
 
 
-def gradient_blocks(rows, place_ref, tiles_ref, part_ref, g0, g1, g2, g3, *refs):
-    keep_a, keep_b, send_a, send_b, part_out, grad_ref, sems = refs[-7:]
+def gradient_blocks(rows, place_ref, part_ref, tiles_in, g0, g1, g2, g3, *refs):
+    keep_a, keep_b, send_a, send_b, part_out, grad_ref, tiles_ref, sems = refs[-8:]
     tokens = g0.shape[0] // 2
     copies = []
     for turn, piece in enumerate((g0, g1, g2, g3)):
@@ -105,13 +110,26 @@
                 pltpu.make_async_copy(piece.at[j * tokens : (j + 1) * tokens], grad_ref.at[where], sems.at[2 * turn + j])
             )
             copies[-1].start()
+    slots = [(1, 1), (1, 0), (0, 1), (0, 0)]
+    loads = []
+    for k, (dh, dl) in enumerate(slots):
+        loads.append(
+            pltpu.make_async_copy(
+                tiles_in.at[:, block_of(place_ref, dh, dl, rows)],
+                tiles_ref.at[:, k * rows : (k + 1) * rows],
+                sems.at[8 + k],
+            )
+        )
+        loads[-1].start()
     part_out[...] = part_ref[...]
     for copy_in in copies:
         copy_in.wait()
     half = keep_a.shape[2]
     for dh in (1, 0):
         for dl in (1, 0):
-            left = tiles_ref[:, block_of(place_ref, dh, dl, rows)]
+            k = slots.index((dh, dl))
+            loads[k].wait()
+            left = tiles_ref[:, k * rows : (k + 1) * rows]
             value = lax.dot_general(left, grad_ref[...], (((0,), (0,)), ((), ())), preferred_element_type=jnp.float32)
             if dl:
                 send_a[dh] = value[:, :half].astype(jnp.bfloat16)
@@ -183,10 +201,13 @@
     f32, b16 = jnp.float32, jnp.bfloat16
 
     wide = far * rows
-    tiles, scaled, factor = kernel_call(
+    core = lax.axis_index("c")
+    cut = shape((rows // 2, anchor.shape[1]), b16)
+    tiles, scaled, factor, mine, theirs = kernel_call(
         lambda *refs: prepare(far, near, rows, *refs),
-        [shape((near, tokens, wide), b16), shape(key_grad.shape, b16), shape((tokens, 1), f32)],
-        (hidden_in, key_grad),
+        [shape((near, tokens, wide), b16), shape(key_grad.shape, b16), shape((tokens, 1), f32), cut, cut],
+        (jnp.stack([fragment[0], core]).astype(jnp.int32), hidden_in, key_grad, weight_now),
+        scalars=1,
     )
     other = flip(scaled, "zp", name="cotangent_pair")
     anywhere = pl.BlockSpec(memory_space=pl.ANY)
@@ -204,10 +225,6 @@
 
     frag_width = anchor.shape[1]
     col_offset = fragment[0] * frag_width
-    start_cols = lax.dynamic_slice_in_dim(weight_now, col_offset, frag_width, 1).astype(b16)
-    core = lax.axis_index("c")
-    mine = lax.dynamic_slice_in_dim(start_cols, core * (rows // 2), rows // 2, 0)
-    theirs = lax.dynamic_slice_in_dim(start_cols, (1 - core) * (rows // 2), rows // 2, 0)
     part = add(mine, flip(theirs, "c"))
 
     part = add(part, flip(part, "x", 1))
@@ -226,12 +243,16 @@
     keep_a, keep_b, send_a, send_b, part = kernel_call(
         lambda *refs: gradient_blocks(rows, *refs),
         [*(shape(block, f32),) * 2, *(shape(block, b16),) * 2, shape(part.shape, b16)],
-        (place, tiles, part),
+        (place, part),
         flops,
         1,
-        [pltpu.VMEM((near * tokens, key_width), b16), pltpu.SemaphoreType.DMA((8,))],
-        behind=(both, *turned, near_low, last_low),
-        read=4,
+        [
+            pltpu.VMEM((near * tokens, key_width), b16),
+            pltpu.VMEM((near * tokens, far * rows), b16),
+            pltpu.SemaphoreType.DMA((12,)),
+        ],
+        behind=(tiles, both, *turned, near_low, last_low),
+        read=5,
     )
     got_a, got_b = swap(send_a, 1, "gradient_near"), swap(send_b, 2, "gradient_far")
     (partial_keys,) = kernel_call(

time: 145 us -> 145 us (level)
    unnamed x25 -> x27, local copies, waits for them, and re-layouts: 5.23 us -> 5.89 us
  transfers between devices with their start and end apart: 19 -> 19, of which waited for: 7 -> 7; matrix products, arithmetic and copies ran while one was open for 4% -> 4% of each run, Pallas kernels for 5% -> 4%
where the time goes in v5:
time: 145 us; the launch traced here: 144 us
  starting transfers between devices  80.6 us (56%)
  waiting for transfers between devices  38.2 us (26%)
  Pallas kernels  12.5 us (9%)
  local copies, waits for them, and re-layouts  5.89 us (4%)
  other arithmetic  5.15 us (4%)
  between operations  1.68 us (1%)
    ppermute x7, starting transfers between devices, flip(): lax.ppermute(value, axis, [(i, i ^ bit) for i in range(lax.axis_size(axis...  35.4 us
    ppermute x7, starting transfers between devices, swap(): return lax.ppermute(value, 'zq', [(i, i ^ bit) for i in range(4)])  26.8 us
    ppermute x3, waiting for transfers between devices, on_device(): lax.ppermute(both, 'y', [(i, (i + k) % 4) for i in range(4)])  16 us
    ppermute x7, waiting for transfers between devices, swap(): return lax.ppermute(value, 'zq', [(i, i ^ bit) for i in range(4)])  15.8 us
    pallas_call x8, Pallas kernels, kernel_call(): pl.pallas_call(run, out_shape=outs, in_specs=[SMEM] * scalars + [VMEM] *...  11.8 us
    ppermute x3, starting transfers between devices, on_device(): lax.ppermute(both, 'y', [(i, (i + k) % 4) for i in range(4)])  10.1 us
    all_to_all x2, starting transfers between devices, exchange(): return lax.all_to_all(value, axes, split_axis=0, concat_axis=0, tiled=True)  8.24 us
    unnamed x27, local copies, waits for them, and re-layouts  5.89 us
  transfers between devices with their start and end apart: 19, of which 7 were waited for; matrix products, arithmetic and copies ran while one was open for 4% of the time, Pallas kernels for 4%

profile of v5, /device:TPU:1, one launch (start us, length us, event | category | flops | bytes accessed | tf_op | source)
XLA Modules:
  0.0 144.0 jit_solution(49512448028008927)
XLA Ops:
  1.3 0.1 pad_add_fusion.1.refs_0_
  1.4 1.0 copy-done
  2.4 1.6 %copy-done.3 = bf16[128,8192]{1,0:T(8,128)(2,1)S(1)} copy-done((bf16[128,8192]{1,0:T(8,128)(2,1)S(1)}, bf16[128,8192]{1,0:T(8,128)(2,1)}, u32[]{:S(2)}) %copy-start.3) | copy-done | bytes 2097176
  4.0 0.9 copy-done.4
  4.9 2.2 %shard_map.112 = (bf16[8,128,1024]{2,1,0:T(8,128)(2,1)}, bf16[128,512]{1,0:T(8,128)(2,1)S(1)}, f32[128,1]{1,0:T(8,128)S(1)}, bf16[128,256]{1,0:T(8,128)(2,1)S(1)}, bf16[128,256]{1,0:T(8,128)(2,1)S(1)}) custom-call(s32[2]{0:T(128)S(1)} %pad_add_fusion.1.refs_0_, bf16[128,8192]{1,0:T(8,128)(2,1)S(1)} %copy-done.3, bf16[128,512]{1,0:T(8,128)(2,1)S(1)} %copy-done.4, ...), custom_call_target="tpu_custom_call" | custom-call | bytes 5112328 | tf_op jit(solution)/shard_map/pallas_call | solution.py:56
  7.1 8.8 %collective-permute-start.4 = (bf16[128,256]{1,0:T(8,128)(2,1)S(1)}, bf16[128,256]{1,0:T(8,128)(2,1)S(1)}, u32[]{:S(2)}, u32[]{:S(2)}) collective-permute-start(bf16[128,256]{1,0:T(8,128)(2,1)S(1)} %get-tuple-element.24), channel_id=1, source_target_pairs={{0,32},{32,0},{1,33},{33,1},{2,34},{34,2},{3,35},{35,3},{4,36},{36... | collective-permute-start | bytes 196616 | tf_op jit(solution)/shard_map/rep_sum/ppermute | solution.py:37
  15.9 1.9 %collective-permute-start = (bf16[128,512]{1,0:T(8,128)(2,1)S(1)}, bf16[128,512]{1,0:T(8,128)(2,1)S(1)}, u32[]{:S(2)}, u32[]{:S(2)}) collective-permute-start(bf16[128,512]{1,0:T(8,128)(2,1)S(1)} %get-tuple-element.20.own_ref), channel_id=1, source_target_pairs={{0,4},{4,0},{1,5},{5,1},{2,6},{6,2},{3,7},{7,3},{8,12},{12,8},{9,1... | collective-permute-start | bytes 393224 | tf_op jit(solution)/shard_map/cotangent_pair/ppermute | solution.py:37
  17.8 1.3 broadcast_multiply_fusion
  19.2 0.0 collective-permute-done.4
  19.2 1.9 %collective-permute-start.5 = (bf16[128,256]{1,0:T(8,128)(2,1)S(1)}, bf16[128,256]{1,0:T(8,128)(2,1)S(1)}, u32[]{:S(2)}, u32[]{:S(2)}) collective-permute-start(bf16[128,256]{1,0:T(8,128)(2,1)S(1)} %add_convert_fusion.3), channel_id=1, source_target_pairs={{0,64},{64,0},{128,192},{192,128},{1,65},{65,1},{129,193},{193,129... | collective-permute-start | bytes 196616 | tf_op jit(solution)/shard_map/rep_sum/ppermute | solution.py:37
  21.1 0.8 multiply_convert_fusion.refs_2_
  21.9 6.3 %collective-permute-start.2 = (bf16[256,512]{1,0:T(8,128)(2,1)}, bf16[256,512]{1,0:T(8,128)(2,1)S(1)}, u32[]{:S(2)}, u32[]{:S(2)}) collective-permute-start(bf16[256,512]{1,0:T(8,128)(2,1)} %multiply_convert_fusion.refs_2_), channel_id=1, source_target_pairs={{0,16},{8,24},{16,0},{24,8},{1,17},{9,25},{17,1},{25,9},{2,18},{10... | collective-permute-start | bytes 786440 | tf_op jit(solution)/shard_map/weights_far/ppermute | solution.py:32
  28.2 4.9 %collective-permute-start.1 = (bf16[256,512]{1,0:T(8,128)(2,1)}, bf16[256,512]{1,0:T(8,128)(2,1)}, u32[]{:S(2)}, u32[]{:S(2)}) collective-permute-start(bf16[256,512]{1,0:T(8,128)(2,1)} %multiply_convert_fusion.refs_2_), channel_id=1, source_target_pairs={{0,8},{8,0},{16,24},{24,16},{1,9},{9,1},{17,25},{25,17},{2,10},{10... | collective-permute-start | bytes 786440 | tf_op jit(solution)/shard_map/weights_near/ppermute | solution.py:32
  33.1 0.0 collective-permute-done.other_ref
  33.1 0.7 shard_map.113
  33.8 4.6 %collective-permute-start.9 = (bf16[256,512]{1,0:T(8,128)(2,1)}, bf16[256,512]{1,0:T(8,128)(2,1)}, u32[]{:S(2)}, u32[]{:S(2)}) collective-permute-start(bf16[256,512]{1,0:T(8,128)(2,1)} %get-tuple-element.25.refs_3_), channel_id=1, source_target_pairs={{0,3},{1,0},{2,1},{3,2},{4,7},{5,4},{6,5},{7,6},{8,11},{9,8},{10,9... | collective-permute-start | bytes 786440 | tf_op jit(solution)/shard_map/cotangent_y/ppermute | solution.py:224
  38.5 2.3 %collective-permute-start.8 = (bf16[256,512]{1,0:T(8,128)(2,1)}, bf16[256,512]{1,0:T(8,128)(2,1)}, u32[]{:S(2)}, u32[]{:S(2)}) collective-permute-start(bf16[256,512]{1,0:T(8,128)(2,1)} %get-tuple-element.25.refs_3_), channel_id=1, source_target_pairs={{0,2},{1,3},{2,0},{3,1},{4,6},{5,7},{6,4},{7,5},{8,10},{9,11},{10,... | collective-permute-start | bytes 786440 | tf_op jit(solution)/shard_map/cotangent_y/ppermute | solution.py:224
  40.7 4.4 %all-to-all-start = ((bf16[8,128,1024]{2,1,0:T(8,128)(2,1)}), bf16[8,128,1024]{2,1,0:T(8,128)(2,1)}, u32[]{:S(2)}, u32[]{:S(2)}) async-start(bf16[8,128,1024]{2,1,0:T(8,128)(2,1)} %get-tuple-element.22), calls=%async_computation | async-start | bytes 4194304 | tf_op jit(solution)/shard_map/all_to_all | solution.py:45
  45.1 0.0 collective-permute-done.5
  45.1 3.2 %collective-permute-start.7 = (bf16[256,512]{1,0:T(8,128)(2,1)}, bf16[256,512]{1,0:T(8,128)(2,1)}, u32[]{:S(2)}, u32[]{:S(2)}) collective-permute-start(bf16[256,512]{1,0:T(8,128)(2,1)} %get-tuple-element.25.refs_3_), channel_id=1, source_target_pairs={{0,1},{1,2},{2,3},{3,0},{4,5},{5,6},{6,7},{7,4},{8,9},{9,10},{10,1... | collective-permute-start | bytes 786440 | tf_op jit(solution)/shard_map/cotangent_y/ppermute | solution.py:224
  48.4 0.6 add_convert_fusion.2
  49.0 3.8 %collective-permute-done.2.refs_0_.refs_4_ = bf16[256,512]{1,0:T(8,128)(2,1)S(1)} collective-permute-done((bf16[256,512]{1,0:T(8,128)(2,1)}, bf16[256,512]{1,0:T(8,128)(2,1)S(1)}, u32[]{:S(2)}, u32[]{:S(2)}) %collective-permute-start.2) | collective-permute-done | bytes 262176 | tf_op jit(solution)/shard_map/weights_far/ppermute | solution.py:32
  52.8 3.4 %collective-permute-start.6 = (bf16[128,256]{1,0:T(8,128)(2,1)}, bf16[128,256]{1,0:T(8,128)(2,1)}, u32[]{:S(2)}, u32[]{:S(2)}) collective-permute-start(bf16[128,256]{1,0:T(8,128)(2,1)} %add_convert_fusion.2), channel_id=1, source_target_pairs={{0,128},{64,192},{128,0},{192,64},{1,129},{65,193},{129,1},{193,65... | collective-permute-start | bytes 196616 | tf_op jit(solution)/shard_map/rep_sum/ppermute | solution.py:37
  56.2 3.4 %collective-permute-done.6 = bf16[128,256]{1,0:T(8,128)(2,1)} collective-permute-done((bf16[128,256]{1,0:T(8,128)(2,1)}, bf16[128,256]{1,0:T(8,128)(2,1)}, u32[]{:S(2)}, u32[]{:S(2)}) %collective-permute-start.6) | collective-permute-done | bytes 65568 | tf_op jit(solution)/shard_map/rep_sum/ppermute | solution.py:37
  59.6 1.9 %collective-permute-start.3 = (bf16[256,512]{1,0:T(8,128)(2,1)S(1)}, bf16[256,512]{1,0:T(8,128)(2,1)S(1)}, u32[]{:S(2)}, u32[]{:S(2)}) collective-permute-start(bf16[256,512]{1,0:T(8,128)(2,1)S(1)} %shard_map.114), channel_id=1, source_target_pairs={{0,8},{8,0},{16,24},{24,16},{1,9},{9,1},{17,25},{25,17},{2,10},{10... | collective-permute-start | bytes 786440 | tf_op jit(solution)/shard_map/weights_last/ppermute | solution.py:32
  61.5 0.1 pad_add_fusion.refs_0_
  61.6 0.9 add_convert_fusion.1.refs_1_
  62.5 0.0 collective-permute-done.9.refs_6_
  62.5 0.0 collective-permute-done.8.refs_5_
  62.5 16.0 %collective-permute-done.7.refs_4_ = bf16[256,512]{1,0:T(8,128)(2,1)} collective-permute-done((bf16[256,512]{1,0:T(8,128)(2,1)}, bf16[256,512]{1,0:T(8,128)(2,1)}, u32[]{:S(2)}, u32[]{:S(2)}) %collective-permute-start.7) | collective-permute-done | bytes 262176 | tf_op jit(solution)/shard_map/cotangent_y/ppermute | solution.py:224
  78.5 0.0 collective-permute-done.3.refs_8_.refs_5_
  78.5 3.0 %all-to-all-done = bf16[8,128,1024]{2,1,0:T(8,128)(2,1)} async-done(((bf16[8,128,1024]{2,1,0:T(8,128)(2,1)}), bf16[8,128,1024]{2,1,0:T(8,128)(2,1)}, u32[]{:S(2)}, u32[]{:S(2)}) %all-to-all-start) | async-done | bytes 2097184 | tf_op jit(solution)/shard_map/all_to_all | solution.py:45
  81.5 4.0 %shard_map.115 = (f32[2,256,256]{2,1,0:T(8,128)S(1)}, f32[2,256,256]{2,1,0:T(8,128)S(1)}, bf16[2,256,256]{2,1,0:T(8,128)(2,1)S(1)}, bf16[2,256,256]{2,1,0:T(8,128)(2,1)S(1)}, bf16[128,256]{1,0:T(8,128)(2,1)S(1)}) custom-call(s32[4]{0:T(128)S(1)} %pad_add_fusion.refs_0_, bf16[128,256]{1,0:T(8,128)(2,1)S(1)} %add_convert_fusion.1.refs_1_, ...), custom_call_target="tpu_custom_call" | custom-call | flops 1073741824 | bytes 1703952 | tf_op jit(solution)/shard_map/pallas_call | solution.py:56
  85.5 4.9 %collective-permute-start.12 = (bf16[2,256,256]{2,1,0:T(8,128)(2,1)S(1)}, bf16[2,256,256]{2,1,0:T(8,128)(2,1)S(1)}, u32[]{:S(2)}, u32[]{:S(2)}) collective-permute-start(bf16[2,256,256]{2,1,0:T(8,128)(2,1)S(1)} %get-tuple-element.32), channel_id=1, source_target_pairs={{0,16},{8,24},{16,0},{24,8},{1,17},{9,25},{17,1},{25,9},{2,18},{10... | collective-permute-start | bytes 786440 | tf_op jit(solution)/shard_map/gradient_far/ppermute | solution.py:32
  90.4 5.0 %collective-permute-start.11 = (bf16[2,256,256]{2,1,0:T(8,128)(2,1)S(1)}, bf16[2,256,256]{2,1,0:T(8,128)(2,1)S(1)}, u32[]{:S(2)}, u32[]{:S(2)}) collective-permute-start(bf16[2,256,256]{2,1,0:T(8,128)(2,1)S(1)} %get-tuple-element.26.refs_6_), channel_id=1, source_target_pairs={{0,8},{8,0},{16,24},{24,16},{1,9},{9,1},{17,25},{25,17},{2,10},{10... | collective-permute-start | bytes 786440 | tf_op jit(solution)/shard_map/gradient_near/ppermute | solution.py:32
  95.5 3.9 %shard_map.116.refs_4_ = bf16[4,256,512]{2,1,0:T(8,128)(2,1)} custom-call(s32[4]{0:T(128)S(1)} %pad_add_fusion.refs_0_, bf16[1024,1024]{1,0:T(8,128)(2,1)} %bitcast.6.refs_2_.refs_1_, bf16[256,512]{1,0:T(8,128)(2,1)} %multiply_convert_fusion.refs_2_, bf16[256,512]{1,0:T(8,128)(2,1)} %collective-permute-done.1.refs_7_.refs_3_, ...), custom_call_target="tpu_custom_call" | custom-call | flops 1073741824 | bytes 4194320 | tf_op jit(solution)/shard_map/pallas_call | solution.py:56
  99.4 3.9 %all-to-all-start.1 = ((bf16[4,256,512]{2,1,0:T(8,128)(2,1)}), bf16[4,256,512]{2,1,0:T(8,128)(2,1)S(1)}, u32[]{:S(2)}, u32[]{:S(2)}) async-start(bf16[4,256,512]{2,1,0:T(8,128)(2,1)} %shard_map.116.refs_4_), calls=%async_computation.1 | async-start | bytes 2097152 | tf_op jit(solution)/shard_map/all_to_all | solution.py:45
  103.3 9.2 %collective-permute-start.15 = (bf16[128,256]{1,0:T(8,128)(2,1)S(1)}, bf16[128,256]{1,0:T(8,128)(2,1)S(1)}, u32[]{:S(2)}, u32[]{:S(2)}) collective-permute-start(bf16[128,256]{1,0:T(8,128)(2,1)S(1)} %get-tuple-element.36), channel_id=1, source_target_pairs={{0,256},{256,0},{1,257},{257,1},{2,258},{258,2},{3,259},{259,3},{4... | collective-permute-start | bytes 196616 | tf_op jit(solution)/shard_map/rep_far/ppermute | solution.py:37
  112.5 3.7 %collective-permute-done.12.refs_3_ = bf16[2,256,256]{2,1,0:T(8,128)(2,1)S(1)} collective-permute-done((bf16[2,256,256]{2,1,0:T(8,128)(2,1)S(1)}, bf16[2,256,256]{2,1,0:T(8,128)(2,1)S(1)}, u32[]{:S(2)}, u32[]{:S(2)}) %collective-permute-start.12) | collective-permute-done | bytes 262176 | tf_op jit(solution)/shard_map/gradient_far/ppermute | solution.py:32
  116.3 5.6 %collective-permute-done.11.refs_1_ = bf16[2,256,256]{2,1,0:T(8,128)(2,1)S(1)} collective-permute-done((bf16[2,256,256]{2,1,0:T(8,128)(2,1)S(1)}, bf16[2,256,256]{2,1,0:T(8,128)(2,1)S(1)}, u32[]{:S(2)}, u32[]{:S(2)}) %collective-permute-start.11) | collective-permute-done | bytes 262176 | tf_op jit(solution)/shard_map/gradient_near/ppermute | solution.py:32
  121.8 0.1 shard_map.119
  121.9 0.0 copy-start.5
  121.9 0.8 copy-done.5
  122.7 1.9 %collective-permute-start.13 = (bf16[256,256]{1,0:T(8,128)(2,1)S(1)}, bf16[256,256]{1,0:T(8,128)(2,1)S(1)}, u32[]{:S(2)}, u32[]{:S(2)}) collective-permute-start(bf16[256,256]{1,0:T(8,128)(2,1)S(1)} %get-tuple-element.34), channel_id=1, source_target_pairs={{0,16},{8,24},{16,0},{24,8},{1,17},{9,25},{17,1},{25,9},{2,18},{10... | collective-permute-start | bytes 393224 | tf_op jit(solution)/shard_map/gradient_far/ppermute | solution.py:32
  124.6 1.9 %collective-permute-start.14 = (bf16[256,256]{1,0:T(8,128)(2,1)S(1)}, bf16[256,256]{1,0:T(8,128)(2,1)S(1)}, u32[]{:S(2)}, u32[]{:S(2)}) collective-permute-start(bf16[256,256]{1,0:T(8,128)(2,1)S(1)} %get-tuple-element.35), channel_id=1, source_target_pairs={{0,8},{8,0},{16,24},{24,16},{1,9},{9,1},{17,25},{25,17},{2,10},{10... | collective-permute-start | bytes 393224 | tf_op jit(solution)/shard_map/gradient_near/ppermute | solution.py:32
  126.6 2.4 %collective-permute-start.16 = (bf16[128,256]{1,0:T(8,128)(2,1)S(1)}, bf16[128,256]{1,0:T(8,128)(2,1)S(1)}, u32[]{:S(2)}, u32[]{:S(2)}) collective-permute-start(bf16[128,256]{1,0:T(8,128)(2,1)S(1)} %add_convert_fusion), channel_id=1, source_target_pairs={{0,32},{32,0},{1,33},{33,1},{2,34},{34,2},{3,35},{35,3},{4,36},{36... | collective-permute-start | bytes 196616 | tf_op jit(solution)/shard_map/rep_back/ppermute | solution.py:37
  129.0 0.0 all-to-all-done.1.refs_1_
  129.0 0.0 copy-start.8
  129.0 0.0 copy-start.9
  129.0 0.7 shard_map.117
  129.7 0.0 copy-start.2
  129.7 7.8 %collective-permute-start.10 = (bf16[128,512]{1,0:T(8,128)(2,1)S(1)}, bf16[128,512]{1,0:T(8,128)(2,1)S(1)}, u32[]{:S(2)}, u32[]{:S(2)}) collective-permute-start(bf16[128,512]{1,0:T(8,128)(2,1)S(1)} %get-tuple-element.28), channel_id=1, source_target_pairs={{0,4},{4,0},{1,5},{5,1},{2,6},{6,2},{3,7},{7,3},{8,12},{12,8},{9,1... | collective-permute-start | bytes 393224 | tf_op jit(solution)/shard_map/keys_pair/ppermute | solution.py:37
  137.5 2.8 %collective-permute-done.13.refs_1_ = bf16[256,256]{1,0:T(8,128)(2,1)S(1)} collective-permute-done((bf16[256,256]{1,0:T(8,128)(2,1)S(1)}, bf16[256,256]{1,0:T(8,128)(2,1)S(1)}, u32[]{:S(2)}, u32[]{:S(2)}) %collective-permute-start.13) | collective-permute-done | bytes 131104 | tf_op jit(solution)/shard_map/gradient_far/ppermute | solution.py:32
  140.3 0.0 collective-permute-done.14.refs_2_
  140.3 1.0 copy-done.6
  141.3 0.1 shard_map.120
  141.4 0.0 copy-start.10
  141.4 0.0 copy-start.11
  141.4 0.5 fusion.6
  141.9 0.4 copy-done.10
  142.3 0.1 copy-done.11
  142.4 0.8 bitcast_dynamic-update-slice_fusion
  143.2 0.0 collective-permute-done.10.refs_1_
  143.2 0.8 shard_map.118
  (20 shorter events, 0.1 us)
Async XLA Ops:
  1.4 1.0 copy-start
  2.4 1.6 %copy-start.3 = (bf16[128,8192]{1,0:T(8,128)(2,1)S(1)}, bf16[128,8192]{1,0:T(8,128)(2,1)}, u32[]{:S(2)}) copy-start(bf16[128,8192]{1,0:T(8,128)(2,1)} %refs_1_.1) | copy-start | bytes 6291460
  4.0 0.9 copy-start.4
  4.9 16.2 %copy-start.1 = (f32[1,256,512]{2,1,0:T(8,128)S(1)}, f32[1,256,512]{2,1,0:T(8,128)}, u32[]{:S(2)}) copy-start(f32[1,256,512]{2,1,0:T(8,128)} %param.12) | copy-start | bytes 1572868
  7.1 12.1 %collective-permute-start.4 = (bf16[128,256]{1,0:T(8,128)(2,1)S(1)}, bf16[128,256]{1,0:T(8,128)(2,1)S(1)}, u32[]{:S(2)}, u32[]{:S(2)}) collective-permute-start(bf16[128,256]{1,0:T(8,128)(2,1)S(1)} %get-tuple-element.24), channel_id=1, source_target_pairs={{0,32},{32,0},{1,33},{33,1},{2,34},{34,2},{3,35},{35,3},{4,36},{36... | collective-permute-start | bytes 196616 | tf_op jit(solution)/shard_map/rep_sum/ppermute | solution.py:37
  15.9 17.2 %collective-permute-start = (bf16[128,512]{1,0:T(8,128)(2,1)S(1)}, bf16[128,512]{1,0:T(8,128)(2,1)S(1)}, u32[]{:S(2)}, u32[]{:S(2)}) collective-permute-start(bf16[128,512]{1,0:T(8,128)(2,1)S(1)} %get-tuple-element.20.own_ref), channel_id=1, source_target_pairs={{0,4},{4,0},{1,5},{5,1},{2,6},{6,2},{3,7},{7,3},{8,12},{12,8},{9,1... | collective-permute-start | bytes 393224 | tf_op jit(solution)/shard_map/cotangent_pair/ppermute | solution.py:37
  19.2 25.9 %collective-permute-start.5 = (bf16[128,256]{1,0:T(8,128)(2,1)S(1)}, bf16[128,256]{1,0:T(8,128)(2,1)S(1)}, u32[]{:S(2)}, u32[]{:S(2)}) collective-permute-start(bf16[128,256]{1,0:T(8,128)(2,1)S(1)} %add_convert_fusion.3), channel_id=1, source_target_pairs={{0,64},{64,0},{128,192},{192,128},{1,65},{65,1},{129,193},{193,129... | collective-permute-start | bytes 196616 | tf_op jit(solution)/shard_map/rep_sum/ppermute | solution.py:37
  21.9 30.9 %collective-permute-start.2 = (bf16[256,512]{1,0:T(8,128)(2,1)}, bf16[256,512]{1,0:T(8,128)(2,1)S(1)}, u32[]{:S(2)}, u32[]{:S(2)}) collective-permute-start(bf16[256,512]{1,0:T(8,128)(2,1)} %multiply_convert_fusion.refs_2_), channel_id=1, source_target_pairs={{0,16},{8,24},{16,0},{24,8},{1,17},{9,25},{17,1},{25,9},{2,18},{10... | collective-permute-start | bytes 786440 | tf_op jit(solution)/shard_map/weights_far/ppermute | solution.py:32
  28.2 34.3 %collective-permute-start.1 = (bf16[256,512]{1,0:T(8,128)(2,1)}, bf16[256,512]{1,0:T(8,128)(2,1)}, u32[]{:S(2)}, u32[]{:S(2)}) collective-permute-start(bf16[256,512]{1,0:T(8,128)(2,1)} %multiply_convert_fusion.refs_2_), channel_id=1, source_target_pairs={{0,8},{8,0},{16,24},{24,16},{1,9},{9,1},{17,25},{25,17},{2,10},{10... | collective-permute-start | bytes 786440 | tf_op jit(solution)/shard_map/weights_near/ppermute | solution.py:32
  33.8 28.7 %collective-permute-start.9 = (bf16[256,512]{1,0:T(8,128)(2,1)}, bf16[256,512]{1,0:T(8,128)(2,1)}, u32[]{:S(2)}, u32[]{:S(2)}) collective-permute-start(bf16[256,512]{1,0:T(8,128)(2,1)} %get-tuple-element.25.refs_3_), channel_id=1, source_target_pairs={{0,3},{1,0},{2,1},{3,2},{4,7},{5,4},{6,5},{7,6},{8,11},{9,8},{10,9... | collective-permute-start | bytes 786440 | tf_op jit(solution)/shard_map/cotangent_y/ppermute | solution.py:224
  38.5 24.1 %collective-permute-start.8 = (bf16[256,512]{1,0:T(8,128)(2,1)}, bf16[256,512]{1,0:T(8,128)(2,1)}, u32[]{:S(2)}, u32[]{:S(2)}) collective-permute-start(bf16[256,512]{1,0:T(8,128)(2,1)} %get-tuple-element.25.refs_3_), channel_id=1, source_target_pairs={{0,2},{1,3},{2,0},{3,1},{4,6},{5,7},{6,4},{7,5},{8,10},{9,11},{10,... | collective-permute-start | bytes 786440 | tf_op jit(solution)/shard_map/cotangent_y/ppermute | solution.py:224
  40.7 40.8 %all-to-all-start = ((bf16[8,128,1024]{2,1,0:T(8,128)(2,1)}), bf16[8,128,1024]{2,1,0:T(8,128)(2,1)}, u32[]{:S(2)}, u32[]{:S(2)}) async-start(bf16[8,128,1024]{2,1,0:T(8,128)(2,1)} %get-tuple-element.22), calls=%async_computation | async-start | bytes 4194304 | tf_op jit(solution)/shard_map/all_to_all | solution.py:45
  45.1 33.4 %collective-permute-start.7 = (bf16[256,512]{1,0:T(8,128)(2,1)}, bf16[256,512]{1,0:T(8,128)(2,1)}, u32[]{:S(2)}, u32[]{:S(2)}) collective-permute-start(bf16[256,512]{1,0:T(8,128)(2,1)} %get-tuple-element.25.refs_3_), channel_id=1, source_target_pairs={{0,1},{1,2},{2,3},{3,0},{4,5},{5,6},{6,7},{7,4},{8,9},{9,10},{10,1... | collective-permute-start | bytes 786440 | tf_op jit(solution)/shard_map/cotangent_y/ppermute | solution.py:224
  52.8 6.8 %collective-permute-start.6 = (bf16[128,256]{1,0:T(8,128)(2,1)}, bf16[128,256]{1,0:T(8,128)(2,1)}, u32[]{:S(2)}, u32[]{:S(2)}) collective-permute-start(bf16[128,256]{1,0:T(8,128)(2,1)} %add_convert_fusion.2), channel_id=1, source_target_pairs={{0,128},{64,192},{128,0},{192,64},{1,129},{65,193},{129,1},{193,65... | collective-permute-start | bytes 196616 | tf_op jit(solution)/shard_map/rep_sum/ppermute | solution.py:37
  59.6 18.9 %collective-permute-start.3 = (bf16[256,512]{1,0:T(8,128)(2,1)S(1)}, bf16[256,512]{1,0:T(8,128)(2,1)S(1)}, u32[]{:S(2)}, u32[]{:S(2)}) collective-permute-start(bf16[256,512]{1,0:T(8,128)(2,1)S(1)} %shard_map.114), channel_id=1, source_target_pairs={{0,8},{8,0},{16,24},{24,16},{1,9},{9,1},{17,25},{25,17},{2,10},{10... | collective-permute-start | bytes 786440 | tf_op jit(solution)/shard_map/weights_last/ppermute | solution.py:32
  85.5 30.7 %collective-permute-start.12 = (bf16[2,256,256]{2,1,0:T(8,128)(2,1)S(1)}, bf16[2,256,256]{2,1,0:T(8,128)(2,1)S(1)}, u32[]{:S(2)}, u32[]{:S(2)}) collective-permute-start(bf16[2,256,256]{2,1,0:T(8,128)(2,1)S(1)} %get-tuple-element.32), channel_id=1, source_target_pairs={{0,16},{8,24},{16,0},{24,8},{1,17},{9,25},{17,1},{25,9},{2,18},{10... | collective-permute-start | bytes 786440 | tf_op jit(solution)/shard_map/gradient_far/ppermute | solution.py:32
  90.4 31.4 %collective-permute-start.11 = (bf16[2,256,256]{2,1,0:T(8,128)(2,1)S(1)}, bf16[2,256,256]{2,1,0:T(8,128)(2,1)S(1)}, u32[]{:S(2)}, u32[]{:S(2)}) collective-permute-start(bf16[2,256,256]{2,1,0:T(8,128)(2,1)S(1)} %get-tuple-element.26.refs_6_), channel_id=1, source_target_pairs={{0,8},{8,0},{16,24},{24,16},{1,9},{9,1},{17,25},{25,17},{2,10},{10... | collective-permute-start | bytes 786440 | tf_op jit(solution)/shard_map/gradient_near/ppermute | solution.py:32
  99.4 29.6 %all-to-all-start.1 = ((bf16[4,256,512]{2,1,0:T(8,128)(2,1)}), bf16[4,256,512]{2,1,0:T(8,128)(2,1)S(1)}, u32[]{:S(2)}, u32[]{:S(2)}) async-start(bf16[4,256,512]{2,1,0:T(8,128)(2,1)} %shard_map.116.refs_4_), calls=%async_computation.1 | async-start | bytes 2097152 | tf_op jit(solution)/shard_map/all_to_all | solution.py:45
  103.3 23.3 %collective-permute-start.15 = (bf16[128,256]{1,0:T(8,128)(2,1)S(1)}, bf16[128,256]{1,0:T(8,128)(2,1)S(1)}, u32[]{:S(2)}, u32[]{:S(2)}) collective-permute-start(bf16[128,256]{1,0:T(8,128)(2,1)S(1)} %get-tuple-element.36), channel_id=1, source_target_pairs={{0,256},{256,0},{1,257},{257,1},{2,258},{258,2},{3,259},{259,3},{4... | collective-permute-start | bytes 196616 | tf_op jit(solution)/shard_map/rep_far/ppermute | solution.py:37
  121.9 0.8 copy-start.5
  122.7 17.6 %collective-permute-start.13 = (bf16[256,256]{1,0:T(8,128)(2,1)S(1)}, bf16[256,256]{1,0:T(8,128)(2,1)S(1)}, u32[]{:S(2)}, u32[]{:S(2)}) collective-permute-start(bf16[256,256]{1,0:T(8,128)(2,1)S(1)} %get-tuple-element.34), channel_id=1, source_target_pairs={{0,16},{8,24},{16,0},{24,8},{1,17},{9,25},{17,1},{25,9},{2,18},{10... | collective-permute-start | bytes 393224 | tf_op jit(solution)/shard_map/gradient_far/ppermute | solution.py:32
  124.6 15.7 %collective-permute-start.14 = (bf16[256,256]{1,0:T(8,128)(2,1)S(1)}, bf16[256,256]{1,0:T(8,128)(2,1)S(1)}, u32[]{:S(2)}, u32[]{:S(2)}) collective-permute-start(bf16[256,256]{1,0:T(8,128)(2,1)S(1)} %get-tuple-element.35), channel_id=1, source_target_pairs={{0,8},{8,0},{16,24},{24,16},{1,9},{9,1},{17,25},{25,17},{2,10},{10... | collective-permute-start | bytes 393224 | tf_op jit(solution)/shard_map/gradient_near/ppermute | solution.py:32
  126.6 15.4 %collective-permute-start.16 = (bf16[128,256]{1,0:T(8,128)(2,1)S(1)}, bf16[128,256]{1,0:T(8,128)(2,1)S(1)}, u32[]{:S(2)}, u32[]{:S(2)}) collective-permute-start(bf16[128,256]{1,0:T(8,128)(2,1)S(1)} %add_convert_fusion), channel_id=1, source_target_pairs={{0,32},{32,0},{1,33},{33,1},{2,34},{34,2},{3,35},{35,3},{4,36},{36... | collective-permute-start | bytes 196616 | tf_op jit(solution)/shard_map/rep_back/ppermute | solution.py:37
  129.0 12.4 %copy-start.8 = (f32[1,256,512]{2,1,0:T(8,128)S(1)}, f32[1,256,512]{2,1,0:T(8,128)}, u32[]{:S(2)}) copy-start(f32[1,256,512]{2,1,0:T(8,128)} %param.13) | copy-start | bytes 1572868
  129.0 12.4 %copy-start.9 = (bf16[1,256,512]{2,1,0:T(8,128)(2,1)S(1)}, bf16[1,256,512]{2,1,0:T(8,128)(2,1)}, u32[]{:S(2)}) copy-start(bf16[1,256,512]{2,1,0:T(8,128)(2,1)} %param.14) | copy-start | bytes 786436
  129.0 12.4 %copy-start.12 = (f32[256]{0:T(256)S(1)}, f32[256]{0:T(256)}, u32[]{:S(2)}) copy-start(f32[256]{0:T(256)} %get-tuple-element.39) | copy-start | bytes 3076
  129.7 11.7 %copy-start.2 = (f32[1,256,512]{2,1,0:T(8,128)S(1)}, f32[1,256,512]{2,1,0:T(8,128)}, u32[]{:S(2)}) copy-start(f32[1,256,512]{2,1,0:T(8,128)} %param.12) | copy-start | bytes 1572868
  129.7 13.5 %collective-permute-start.10 = (bf16[128,512]{1,0:T(8,128)(2,1)S(1)}, bf16[128,512]{1,0:T(8,128)(2,1)S(1)}, u32[]{:S(2)}, u32[]{:S(2)}) collective-permute-start(bf16[128,512]{1,0:T(8,128)(2,1)S(1)} %get-tuple-element.28), channel_id=1, source_target_pairs={{0,4},{4,0},{1,5},{5,1},{2,6},{6,2},{3,7},{7,3},{8,12},{12,8},{9,1... | collective-permute-start | bytes 393224 | tf_op jit(solution)/shard_map/keys_pair/ppermute | solution.py:37
  140.3 1.0 copy-start.6
  141.4 1.0 copy-start.10
  141.4 1.0 copy-start.11
  143.2 0.8 copy-start.7
